TPU v7x, 512 devices: a whole 4x4x16 slice. The times are simulated.
512 devices in a mesh: ctx: 32 (over y, x, core), tp: 16 (over z).
Axes of the slice: x: 4, y: 4, z: 16, core: 2. Of those that a mesh axis runs over, the one named last changes fastest.
Arguments:
- queries: bfloat16 [8192, 2048], P('ctx', 'tp'), may hold values from -6 to 6
- key_vectors: bfloat16 [8192, 2048], P('ctx', 'tp'), may hold values from -4 to 4
- value_vectors: bfloat16 [8192, 4096], P('ctx', 'tp'), may hold values from -6 to 6
- output_gate: bfloat16 [8192, 4096], P('ctx', 'tp'), may hold values from -6 to 6
- write_rate: float32 [8192, 32], P('ctx', 'tp'), may hold values from 0 to 1, as said below
- log_decay: float32 [8192, 32], P('ctx', 'tp'), may hold values from -1 to 0, as said below
- norm_gain: float32 [128], replicated, may hold values from 0.5 to 2
- out_weight: bfloat16 [4096, 2048], P('tp'), may hold values from -0.09375 to 0.09375
Outputs:
- mixed: bfloat16 [8192, 2048], P(('ctx', 'tp'))
Inputs may be any that keep to these rules, and one draw needn't show every extreme that they name: `write_rate`: write strengths are positive. `log_decay`: log decays are negative.
All inputs are finite; a program needn't handle non-finite values.
Results may differ from a plain program's by a relative error of at most 0.025.
Values may be sent and summed in bfloat16 or wider, within the bound.
No kernel may reach another device: no remote copies, remote signals or barrier semaphores. Data moves between devices by JAX's collectives and lax.ppermute only.
A program may use at most 64 MiB of HBM per device.

v0:
```python
import jax
import jax.numpy as jnp
from jax import lax
from jax.sharding import PartitionSpec as P

DK = 128
DV = 128


highest_precision = lax.Precision.HIGHEST


def prefix(value, axis, combine, identity):
    length, index = (lax.axis_size(axis), lax.axis_index(axis))
    everything = jax.tree.map(
        lambda part, kind: lax.all_gather(part.astype(kind), axis),
        value,
        (jnp.bfloat16, jnp.bfloat16),
    )
    start = jax.tree.map(
        lambda part, zero: jnp.broadcast_to(jnp.asarray(zero, part.dtype), part.shape),
        value,
        identity,
    )

    def lap(k, before):
        reached = k < index
        new = combine(
            before, jax.tree.map(lambda part, own: part[k].astype(own.dtype), everything, value)
        )
        return jax.tree.map(lambda a, b: jnp.where(reached, a, b), new, before)

    return lax.fori_loop(0, length, lap, start)


def matmul(left, right):
    return jnp.matmul(left, right, precision=highest_precision)


def flipped(matrix):
    return jnp.swapaxes(matrix, -1, -2)


def unit_rows(source, count_heads, size_head):
    values_f = source.astype(jnp.float32).reshape(source.shape[0], count_heads, size_head)
    return values_f * lax.rsqrt(jnp.sum(values_f * values_f, axis=-1, keepdims=True) + 1e-06)


def to_blocks(source, count, length):
    return jnp.transpose(
        source.reshape(count, length, source.shape[1], source.shape[2]), (0, 2, 1, 3)
    )


def local(
    queries, key_vectors, value_vectors, output_gate, write_rate, log_decay, norm_gain, out_weight
):
    tokens_here = queries.shape[0]
    key_heads = queries.shape[1] // DK
    value_heads = value_vectors.shape[1] // DV
    sharing = value_heads // key_heads
    length = min(64, tokens_here)
    count = tokens_here // length
    query_blocks = to_blocks(
        jnp.repeat(unit_rows(queries, key_heads, DK), sharing, axis=1), count, length
    )
    key_blocks = to_blocks(
        jnp.repeat(unit_rows(key_vectors, key_heads, DK), sharing, axis=1), count, length
    )
    value_blocks = to_blocks(
        value_vectors.astype(jnp.float32).reshape(tokens_here, value_heads, DV), count, length
    )
    rate_blocks = jnp.transpose(write_rate.reshape(count, length, value_heads), (0, 2, 1))[
        ..., None
    ]
    decay_sums = jnp.cumsum(
        jnp.transpose(log_decay.reshape(count, length, value_heads), (0, 2, 1)), axis=-1
    )
    closing = decay_sums[..., -1:]
    positions = jnp.arange(length)
    inclusive = positions[:, None] >= positions[None, :]
    strict = positions[:, None] > positions[None, :]
    spread = decay_sums[..., :, None] - decay_sums[..., None, :]
    ratios = jnp.where(inclusive, jnp.exp(jnp.where(inclusive, spread, 0.0)), 0.0)
    key_gram = matmul(key_blocks, flipped(key_blocks))
    lower = jnp.where(strict, rate_blocks * key_gram * ratios, 0.0)
    identity = jnp.eye(length, dtype=jnp.float32)
    inverse = identity - lower
    power = lower
    reach = 1
    while reach < length - 1:
        power = matmul(power, power)
        inverse = matmul(inverse, identity + power)
        reach = 2 * reach + 1
    fresh = matmul(inverse, rate_blocks * value_blocks)
    erase = matmul(inverse, rate_blocks * jnp.exp(decay_sums)[..., None] * key_blocks)
    scores = ratios * matmul(query_blocks, flipped(key_blocks))
    read_query = jnp.exp(decay_sums)[..., None] * query_blocks
    write_key = jnp.exp(closing - decay_sums)[..., None] * key_blocks
    fade = jnp.exp(closing)[..., None]
    eye_key = jnp.broadcast_to(jnp.eye(DK, dtype=jnp.float32), (value_heads, DK, DK))
    empty_state = jnp.zeros((value_heads, DK, DV), jnp.float32)
    per_block = (fresh, erase, scores, read_query, write_key, fade)

    def summarize(carry, block):
        transit, held = carry
        fresh_b, erase_b, score_b, read_b, write_b, fade_b = block
        moved = fade_b * transit - matmul(flipped(write_b), matmul(erase_b, transit))
        delta = fresh_b - matmul(erase_b, held)
        return ((moved, fade_b * held + matmul(flipped(write_b), delta)), None)

    (transit, held), _ = lax.scan(summarize, (eye_key, empty_state), per_block)

    def compose(earlier, later):
        return (matmul(later[0], earlier[0]), matmul(later[0], earlier[1]) + later[1])

    _, start_state = prefix((transit, held), "ctx", compose, (eye_key, empty_state))

    def advance(current, block):
        fresh_b, erase_b, score_b, read_b, write_b, fade_b = block
        delta = fresh_b - matmul(erase_b, current)
        produced = matmul(read_b, current) + matmul(score_b, delta)
        return (fade_b * current + matmul(flipped(write_b), delta), produced)

    _, core_blocks = lax.scan(advance, start_state, per_block)
    attention_core = jnp.transpose(core_blocks, (0, 2, 1, 3)).reshape(tokens_here, value_heads, DV)
    square_mean = jnp.mean(attention_core * attention_core, axis=-1, keepdims=True)
    gate_full = output_gate.astype(jnp.float32).reshape(tokens_here, value_heads, DV)
    normed = attention_core * lax.rsqrt(square_mean + 1e-06) * norm_gain * jax.nn.silu(gate_full)
    normed = normed.astype(jnp.bfloat16).reshape(tokens_here, value_heads * DV)
    return lax.psum_scatter(
        jnp.dot(normed, out_weight, preferred_element_type=jnp.float32).astype(jnp.bfloat16),
        "tp",
        scatter_dimension=0,
        tiled=True,
    )


def solution(mesh):
    placed = (
        P("ctx", "tp"),
        P("ctx", "tp"),
        P("ctx", "tp"),
        P("ctx", "tp"),
        P("ctx", "tp"),
        P("ctx", "tp"),
        P(),
        P("tp", None),
    )
    return jax.shard_map(
        local, mesh=mesh, in_specs=placed, out_specs=P(("ctx", "tp"), None), check_vma=False
    )
```

profile of v0, /device:TPU:24, one launch (start us, length us, event | category | flops | bytes accessed | tf_op | source)
XLA Modules:
  0.0 270.4 jit_solution(5774078055299888976)
XLA Ops:
  6.6 1.0 fusion.66
  7.6 1.0 fusion.65
  8.6 0.8 reshape.93
  9.4 0.8 reshape.92
  10.2 0.9 reduce_window_sum.11
  11.6 0.9 convert_multiply_fusion.3
  12.5 0.9 convert_multiply_fusion.1
  13.4 0.6 fusion.43
  18.1 0.4 fusion.53
  18.5 0.4 fusion.51
  19.2 5.4 %while.40 = (s32[]{:T(128)}, f32[2,128,128]{2,1,0:T(8,128)S(1)}, f32[2,128,128]{2,1,0:T(8,128)S(1)}, f32[4,2,1,1]{1,3,2,0:T(1,128)S(1)}, f32[4,2,64,128]{3,2,1,0...) while((s32[]{:T(128)}, f32[2,128,128]{2,1,0:T(8,128)S(1)}, ...), condition=%wide.region_3.4_spmd.clone, body=%wide.region_2.0_spmd.clone.sunk | while | flops 100876288 | bytes 1378959 | solution.py:112
  19.5 0.4 convolution_add_fusion.8
  20.2 0.4 convolution_subtract_fusion.7
  20.9 0.4 convolution_add_fusion.8
  21.5 0.4 convolution_subtract_fusion.7
  22.2 0.4 convolution_add_fusion.8
  22.9 0.4 convolution_subtract_fusion.7
  23.6 0.4 convolution_add_fusion.8
  24.3 0.4 convolution_subtract_fusion.7
  24.7 0.6 convert_element_type.60
  25.4 0.6 convert_element_type.59
  26.2 0.5 convolution_multiply_fusion
  26.7 61.6 %all-gather.7.cloned.1.call-done = bf16[64,128,128]{2,1,0:T(8,128)(2,1)} async-done(((bf16[2,128,128]{2,1,0:T(8,128)(2,1)}), bf16[64,128,128]{2,1,0:T(8,128)(2,1)}) %all-gather.7.cloned.1.call-update) | async-done | bytes 2097168 | tf_op jit(solution)/shard_map/all_gather | solution.py:16
  88.3 61.6 %all-gather.5.cloned.1.call-done = bf16[64,128,128]{2,1,0:T(8,128)(2,1)} async-done(((bf16[2,128,128]{2,1,0:T(8,128)(2,1)}), bf16[64,128,128]{2,1,0:T(8,128)(2,1)}) %all-gather.5.cloned.1.call-update) | async-done | bytes 2097168 | tf_op jit(solution)/shard_map/all_gather | solution.py:16
  150.0 36.5 %while.41 = (s32[]{:T(128)}, f32[2,128,128]{2,1,0:T(8,128)S(1)}, s32[]{:T(128)}, bf16[32,2,128,128]{3,2,1,0:T(8,128)(2,1)}, bf16[32,2,128,128]{3,2,1,0:T(8,128)(2,1)}, /*index=5*/s32[]{:T(128)}, s32[]{:T(128)}) while((s32[]{:T(128)}, f32[2,128,128]{2,1,0:T(8,128)S(1)}, s32[]{:T(128)}, bf16[32,2,128,128]{3,2,1,0:T(8,128)(2,1)}, ...), condition=%wide.region_5.6_spmd.clone, body=%wide.region_4.5_spmd.clone.sunk | while | flops 50495492 | bytes 789095 | solution.py:33
  150.0 1.1 fusion.165
  151.1 1.1 fusion.165
  152.3 1.1 fusion.165
  153.4 1.1 fusion.165
  154.6 1.1 fusion.165
  155.7 1.1 fusion.165
  156.9 1.1 fusion.165
  158.0 1.1 fusion.165
  159.1 1.1 fusion.165
  160.3 1.1 fusion.165
  161.4 1.1 fusion.165
  162.6 1.1 fusion.165
  163.7 1.1 fusion.165
  164.8 1.1 fusion.165
  166.0 1.1 fusion.165
  167.1 1.1 fusion.165
  168.3 1.1 fusion.165
  169.4 1.1 fusion.165
  170.5 1.1 fusion.165
  171.7 1.1 fusion.165
  172.8 1.1 fusion.165
  174.0 1.1 fusion.165
  175.1 1.1 fusion.165
  176.3 1.1 fusion.165
  177.4 1.1 fusion.165
  178.5 1.1 fusion.165
  179.7 1.1 fusion.165
  180.8 1.1 fusion.165
  182.0 1.1 fusion.165
  183.1 1.1 fusion.165
  184.2 1.1 fusion.165
  185.4 1.1 fusion.165
  186.5 4.6 %while.39 = (s32[]{:T(128)}, f32[2,128,128]{2,1,0:T(8,128)S(1)}, f32[4,2,64,128]{3,2,1,0:T(8,128)S(1)}, f32[4,2,1,1]{1,3,2,0:T(1,128)S(1)}, f32[4,2,64,128]{3,2,...) while((s32[]{:T(128)}, f32[2,128,128]{2,1,0:T(8,128)S(1)}, ...), condition=%wide.region_8.9_spmd, body=%wide.region_7.8_spmd.sunk | while | flops 88178688 | bytes 1247881 | solution.py:125
  187.0 0.4 convolution_add_fusion.7
  188.2 0.4 convolution_add_fusion.7
  189.3 0.4 convolution_add_fusion.7
  190.5 0.4 convolution_add_fusion.7
  192.0 1.5 convolution_convert_fusion
  193.4 70.4 %reduce-scatter.2.cloned.1.call-done = bf16[16,2048]{1,0:T(8,128)(2,1)} async-done(((bf16[256,2048]{1,0:T(8,128)(2,1)}), bf16[16,2048]{1,0:T(8,128)(2,1)}) %reduce-scatter.2.cloned.1.call-update) | async-done | bytes 65552 | tf_op jit(solution)/shard_map/reduce_scatter | solution.py:131
  (109 shorter events, 10.7 us)
Async XLA Ops:
  6.5 185.4 %copy-start = (bf16[256,2048]{1,0:T(8,128)(2,1)S(1)}, bf16[256,2048]{1,0:T(8,128)(2,1)}, u32[]{:S(2)}) copy-start(bf16[256,2048]{1,0:T(8,128)(2,1)} %param.21) | copy-start | bytes 3145732
  6.5 81.8 %all-gather.7.cloned.1.call-start = ((), (), s32[]{:S(2)}) async-start(), calls=%async_computation.3 | async-start | bytes 2162688 | tf_op jit(solution)/shard_map/all_gather | solution.py:16
  15.6 2.0 copy-start.1
  19.2 7.0 %copy-start.3 = (f32[128]{0:T(128)S(1)}, f32[128]{0:T(128)}, u32[]{:S(2)}) copy-start(f32[128]{0:T(128)} %param.20) | copy-start | bytes 1540
  25.3 124.6 %all-gather.5.cloned.1.call-start = ((), (), s32[]{:S(2)}) async-start(), calls=%async_computation.2 | async-start | bytes 2162688 | tf_op jit(solution)/shard_map/all_gather | solution.py:16
  26.1 237.8 %reduce-scatter.2.cloned.1.call-start = ((), (), s32[]{:S(2)}) async-start(), calls=%async_computation.1 | async-start | bytes 1114112 | tf_op jit(solution)/shard_map/reduce_scatter | solution.py:131
  186.5 5.5 %copy-start.2 = (bf16[256,256]{1,0:T(8,128)(2,1)S(1)}, bf16[256,256]{1,0:T(8,128)(2,1)}, u32[]{:S(2)}) copy-start(bf16[256,256]{1,0:T(8,128)(2,1)} %param.17) | copy-start | bytes 393220
Sparse Core Ops, SparseCore 0:
  25.5 62.8 all-gather.6
  91.5 58.4 all-gather.4
  193.6 70.2 reduce-scatter.1
where the time goes:
time: 272 us; the launch traced here: 270 us
  waiting for transfers between devices  194 us (71%)
  matrix products  51.8 us (19%)
  between operations  13.4 us (5%)
  other arithmetic  6.56 us (2%)
  local copies, waits for them, and re-layouts  3.12 us (1%)
    all_gather x2, waiting for transfers between devices, prefix(): lax.all_gather(part.astype(kind), axis)  123 us
    reduce_scatter x1, waiting for transfers between devices, local(): lax.psum_scatter(jnp.dot(normed, out_weight, preferred_element_type=jnp.f...  70.4 us
    dot_general x78, matrix products, matmul(): return jnp.matmul(left, right, precision=highest_precision)  50.4 us
  transfers between devices with their start and end apart: 3, of which 3 were waited for; matrix products, arithmetic and copies ran while one was open for 0% of the time, Pallas kernels for 0%

commit v1 on v0

v1 whole, which is shorter than its diff:
```python
import jax
import jax.numpy as jnp
from jax import lax
from jax.experimental import pallas as pl
from jax.experimental.pallas import tpu as pltpu
from jax.sharding import PartitionSpec as P

F32 = jnp.float32
BF = jnp.bfloat16
TOK = 256
DK = 128
DV = 128
HALF = 128


def dot(a, b, dims=((1,), (0,))):
    return lax.dot_general(a, b, (dims, ((), ())), preferred_element_type=F32)


def split(a):
    hi = a.astype(BF)
    return hi, (a - hi.astype(F32)).astype(BF)


def dot_fine(a, b, dims=((1,), (0,))):
    ah, al = split(a)
    bh, bl = split(b)
    return dot(ah, bh, dims) + (dot(ah, bl, dims) + dot(al, bh, dims))


def dot_left(a, b, dims=((1,), (0,))):
    ah, al = split(a)
    return dot(ah, b, dims) + dot(al, b, dims)


def dot_right(a, b, dims=((1,), (0,))):
    bh, bl = split(b)
    return dot(a, bh, dims) + dot(a, bl, dims)


def grid_iota(rows, cols):
    return (
        lax.broadcasted_iota(jnp.int32, (rows, cols), 0),
        lax.broadcasted_iota(jnp.int32, (rows, cols), 1),
    )


def to_row(eye, column):
    return jnp.sum(jnp.where(eye, column, 0.0), axis=0, keepdims=True)


def decay_columns(decay):
    row, col = grid_iota(TOK, TOK)
    ones = jnp.where(row >= col, 1.0, 0.0).astype(BF)
    hi = decay.astype(BF).astype(F32)
    rest = decay - hi
    mid = rest.astype(BF).astype(F32)
    low = rest - mid
    lane = lax.broadcasted_iota(jnp.int32, (TOK, 128), 1)
    parts = jnp.zeros((TOK, 128), F32)
    for place, piece in enumerate((hi, mid, low)):
        for head in range(2):
            parts = jnp.where(lane == 2 * place + head, piece[:, head : head + 1], parts)
    sums = dot(ones, parts.astype(BF))
    return [
        sums[:, head : head + 1] + (sums[:, 2 + head : 3 + head] + sums[:, 4 + head : 5 + head])
        for head in range(2)
    ]


def unit_scale(source):
    full = source.astype(F32)
    return lax.rsqrt(jnp.sum(full * full, axis=1, keepdims=True) + 1e-06)


def map_kernel(k_ref, v_ref, rate_ref, decay_ref, maps_ref, solved_ref):
    keys = k_ref[...]
    keys_f = keys.astype(F32)
    values = v_ref[...].astype(F32)
    rate = rate_ref[...]
    row, col = grid_iota(TOK, TOK)
    eye = row == col
    strict = row > col
    gram = dot(keys, keys, ((1,), (1,)))
    scale = unit_scale(keys)
    gram = gram * scale * to_row(eye, scale)
    sums = decay_columns(decay_ref[...])
    r_s, c_s = grid_iota(HALF, HALF)
    eye_s = jnp.where(r_s == c_s, 1.0, 0.0).astype(F32)

    lowers, corners = [], []
    for head in range(2):
        fall = jnp.exp(jnp.minimum(sums[head] - to_row(eye, sums[head]), 0.0))
        low = jnp.where(strict, rate[:, head : head + 1] * gram * fall, 0.0)
        lowers += [low[:HALF, :HALF], low[HALF:, HALF:]]
        corners.append(low[HALF:, :HALF])

    small = (r_s // 8) == (c_s // 8)
    first = [jnp.where(small, low, 0.0) for low in lowers]
    first_b = [a.astype(BF) for a in first]
    square = [dot(a, a).astype(BF) for a in first_b]
    fourth = [dot(a, a).astype(BF) for a in square]
    inv = [eye_s - a for a in first]
    inv = [x + dot(x.astype(BF), a) for x, a in zip(inv, square)]
    inv = [x + dot(x.astype(BF), a) for x, a in zip(inv, fourth)]
    size = 8
    while size < HALF:
        off = ((r_s // (2 * size)) == (c_s // (2 * size))) & ((r_s // size) > (c_s // size))
        inv_b = [x.astype(BF) for x in inv]
        part = [jnp.where(off, low, 0.0).astype(BF) for low in lowers]
        part = [dot(a, x).astype(BF) for a, x in zip(part, inv_b)]
        inv = [x - dot(xb, a) for x, xb, a in zip(inv, inv_b, part)]
        size *= 2
    inv_b = [x.astype(BF) for x in inv]
    gap = [
        eye_s - xb.astype(F32) - dot_left(low, xb) for low, xb in zip(lowers, inv_b)
    ]
    inv = [xb.astype(F32) + dot(xb, g.astype(BF)) for xb, g in zip(inv_b, gap)]

    eye_k = jnp.where(r_s == c_s, 1.0, 0.0).astype(F32)
    solved = []
    for head in range(2):
        b = rate[:, head : head + 1]
        grow = b * jnp.exp(sums[head]) * scale
        right = jnp.concatenate(
            [grow * keys_f, b * values[:, head * DV : (head + 1) * DV]], axis=1
        )
        top = dot_fine(inv[2 * head], right[:HALF])
        solved.append((top, right[HALF:]))
    for head in range(2):
        top, below = solved[head]
        below = below - dot_fine(corners[head], top)
        below = dot_fine(inv[2 * head + 1], below)
        solved[head] = jnp.concatenate([top, below], axis=0)
    maps = []
    for head in range(2):
        closing = sums[head][TOK - 1 :, :]
        weight = scale * jnp.exp(closing - sums[head])
        moved = dot_right(keys, weight * solved[head], ((0,), (0,)))
        transit = eye_k * jnp.exp(closing) - moved[:, :DK]
        maps.append(jnp.concatenate([transit, moved[:, DK:]], axis=1).astype(BF))
    for place in range(maps_ref.shape[0]):
        maps_ref[place] = maps[place % 2]
    for head in range(2):
        solved_ref[head] = solved[head]


def read_kernel(
    q_ref, k_ref, decay_ref, gate_ref, gain_ref, solved_ref, inner_ref, outer_ref, gated_ref
):
    queries = q_ref[...]
    keys = k_ref[...]
    row, col = grid_iota(TOK, TOK)
    eye = row == col
    inclusive = row >= col
    unit_q = unit_scale(queries)
    scores = dot(queries, keys, ((1,), (1,))) * unit_q * to_row(eye, unit_scale(keys))
    sums = decay_columns(decay_ref[...])
    for head in range(2):
        fall = jnp.exp(jnp.minimum(sums[head] - to_row(eye, sums[head]), 0.0))
        weights = jnp.where(inclusive, scores * fall, 0.0)
        both = dot_fine(weights, solved_ref[head])
        outer_ref[head] = jnp.exp(sums[head]) * unit_q * queries.astype(F32) - both[:, :DK]
        inner_ref[head] = both[:, DK:]
        gate = gate_ref[:, head * DV : (head + 1) * DV].astype(F32)
        gated_ref[head] = gain_ref[...] * (gate / (1.0 + jnp.exp(-gate)))


def after(later_t, later_h, earlier, fine):
    moved = dot_fine(later_t, earlier) if fine else dot_right(later_t, earlier)
    return jnp.concatenate([moved[:, :DK], moved[:, DK:] + later_h], axis=1)


def row_kernel(place_ref, parts_ref, total_ref, ahead_ref, first_ref):
    x = place_ref[1]

    def pair(i):
        later = parts_ref[2 * i + 1]
        moved = dot(later[:, :DK], parts_ref[2 * i])
        return jnp.concatenate(
            [moved[:, :DK], moved[:, DK:] + later[:, DK:].astype(F32)], axis=1
        )

    pairs = [pair(i) for i in range(4)]
    upto2 = pairs[0]
    upto4 = after(pairs[1][:, :DK], pairs[1][:, DK:], upto2, True)
    last2 = after(pairs[3][:, :DK], pairs[3][:, DK:], pairs[2], True)
    upto6 = after(pairs[2][:, :DK], pairs[2][:, DK:], upto4, True)
    total = after(last2[:, :DK], last2[:, DK:], upto4, True).astype(BF)
    for place in range(4):
        total_ref[place] = total
    row, col = grid_iota(DK, DK + DV)
    none = jnp.where(row == col, 1.0, 0.0).astype(F32)
    ahead_ref[...] = jnp.where(
        x == 0, none, jnp.where(x == 1, upto2, jnp.where(x == 2, upto4, upto6))
    )
    first_ref[...] = parts_ref[2 * x]


def state_kernel(place_ref, rows_ref, ahead_ref, first_ref, send_ref, mine_ref):
    y = place_ref[0]
    core = place_ref[2]

    def onward(later, state):
        return dot_right(later[:, :DK], state) + later[:, DK:].astype(F32)

    one = rows_ref[0][:, DK:].astype(F32)
    two = onward(rows_ref[1], one)
    three = onward(rows_ref[2], two)
    start = jnp.where(
        y == 0, jnp.zeros_like(one), jnp.where(y == 1, one, jnp.where(y == 2, two, three))
    )
    ahead = ahead_ref[...]
    chip = dot_fine(ahead[:, :DK], start) + ahead[:, DK:]
    second = onward(first_ref[...], chip)
    send_ref[...] = jnp.where(core == 0, second, chip).astype(BF)
    mine_ref[...] = jnp.where(core == 0, chip, second).astype(BF)


def out_kernel(place_ref, mine_ref, came_ref, inner_ref, outer_ref, gated_ref, out_ref):
    core = place_ref[2]
    mine = mine_ref[...].astype(F32)
    came = came_ref[...].astype(F32)
    for head in range(2):
        state = jnp.where(core == head, mine, came).astype(BF)
        reached = inner_ref[head] + dot_left(outer_ref[head], state)
        mean = jnp.sum(reached * reached, axis=1, keepdims=True) * (1.0 / DV)
        normed = (reached * lax.rsqrt(mean + 1e-06) * gated_ref[head]).astype(BF)
        for group in range(4):
            for near in range(4):
                piece = normed[(4 * group + near) * 16 : (4 * group + near + 1) * 16]
                for c in range(2):
                    out_ref[
                        4 * c + near,
                        group * 16 : (group + 1) * 16,
                        head * DV : (head + 1) * DV,
                    ] = piece


def project_kernel(normed_ref, weight_ref, out_ref):
    for core in range(2):
        total = None
        for near in range(4):
            term = dot(normed_ref[4 * core + near], weight_ref[near * 256 : (near + 1) * 256])
            total = term if total is None else total + term
        total = total.astype(BF)
        for group in range(4):
            out_ref[4 * core + group] = total[group * 16 : (group + 1) * 16]


def sum_kernel(parts_ref, out_ref):
    width = parts_ref.shape[2]
    for core in range(2):
        total = parts_ref[4 * core].astype(F32)
        for group in range(1, 4):
            total = total + parts_ref[4 * core + group].astype(F32)
        out_ref[:, core * width : (core + 1) * width] = total.astype(BF)


def in_vmem():
    return pl.BlockSpec(memory_space=pltpu.VMEM)


def call(kernel, outs, *args, scalars=0, flops=10**8, name=None):
    return pl.pallas_call(
        kernel,
        out_shape=outs,
        in_specs=[pl.BlockSpec(memory_space=pltpu.SMEM)] * scalars
        + [in_vmem()] * (len(args) - scalars),
        out_specs=jax.tree.map(lambda _: in_vmem(), outs),
        compiler_params=pltpu.CompilerParams(vmem_limit_bytes=32 * 1024 * 1024),
        cost_estimate=pl.CostEstimate(flops=flops, bytes_accessed=10**6, transcendentals=0),
        name=name,
    )(*args)


def shape(dims, kind):
    return jax.ShapeDtypeStruct(dims, kind)


def local(
    queries, key_vectors, value_vectors, output_gate, write_rate, log_decay, norm_gain, out_weight
):
    at = lax.axis_index("ctx")
    core = at % 2
    place = jnp.stack([at // 8, (at // 2) % 4, core]).astype(jnp.int32)
    width = out_weight.shape[1] // 2

    own_half = lax.dynamic_slice_in_dim(out_weight, core * width, width, axis=1)
    near = [[4 * g + j for j in range(4)] for g in range(4)]
    weight = lax.all_gather(own_half, "tp", axis_index_groups=near, tiled=True)

    maps, solved = call(
        map_kernel,
        (shape((8, DK, DK + DV), BF), shape((2, TOK, DK + DV), F32)),
        key_vectors,
        value_vectors,
        write_rate,
        log_decay,
        flops=10**9,
        name="shard_maps",
    )
    lines = [[8 * y + i for i in range(8)] for y in range(4)]
    parts = lax.all_to_all(maps, "ctx", 0, 0, axis_index_groups=lines)
    inner, outer, gated = call(
        read_kernel,
        (shape((2, TOK, DV), F32), shape((2, TOK, DK), F32), shape((2, TOK, DV), F32)),
        queries,
        key_vectors,
        log_decay,
        output_gate,
        norm_gain.reshape(1, DV),
        solved,
        flops=10**9,
        name="read_parts",
    )
    total, ahead, first = call(
        row_kernel,
        (shape((4, DK, DK + DV), BF), shape((DK, DK + DV), F32), shape((DK, DK + DV), BF)),
        place,
        parts,
        scalars=1,
        name="row_maps",
    )
    columns = [[8 * y + i for y in range(4)] for i in range(8)]
    rows = lax.all_to_all(total, "ctx", 0, 0, axis_index_groups=columns)
    send, mine = call(
        state_kernel,
        (shape((DK, DV), BF), shape((DK, DV), BF)),
        place,
        rows,
        ahead,
        first,
        scalars=1,
        name="states",
    )
    came = lax.ppermute(send, "ctx", [(i, i ^ 1) for i in range(32)])
    normed = call(
        out_kernel,
        shape((8, 64, 2 * DV), BF),
        place,
        mine,
        came,
        inner,
        outer,
        gated,
        scalars=1,
        name="gated_norm",
    )
    close, far = [], []
    for chip in range(16):
        for i in range(4):
            close.append([(2 * chip + c) * 16 + 4 * i + j for c in range(2) for j in range(4)])
            far.append([(2 * chip + c) * 16 + 4 * j + i for c in range(2) for j in range(4)])
    both = ("ctx", "tp")
    gathered = lax.all_to_all(normed, both, 0, 0, axis_index_groups=close)
    partial = call(
        project_kernel,
        shape((8, 16, width), BF),
        gathered,
        weight,
        name="project",
    )
    shares = lax.all_to_all(partial, both, 0, 0, axis_index_groups=far)
    return call(sum_kernel, shape((16, 2 * width), BF), shares, name="sum_shares")


def solution(mesh):
    placed = (
        P("ctx", "tp"),
        P("ctx", "tp"),
        P("ctx", "tp"),
        P("ctx", "tp"),
        P("ctx", "tp"),
        P("ctx", "tp"),
        P(),
        P("tp", None),
    )
    return jax.shard_map(
        local, mesh=mesh, in_specs=placed, out_specs=P(("ctx", "tp"), None), check_vma=False
    )
```

time: 272 us -> 115 us (0.42)
  the two profiles are of different devices: /device:TPU:24 before, /device:TPU:33 now
where the time goes in v1:
time: 115 us; the launch traced here: 114 us
  blocking collectives  58.2 us (51%)
  waiting for transfers between devices  16 us (14%)
  between operations  13.5 us (12%)
  Pallas kernels  10.2 us (9%)
  starting transfers between devices  9.32 us (8%)
  local copies, waits for them, and re-layouts  7.05 us (6%)
    all_to_all x1, blocking collectives, local(): shares = lax.all_to_all(partial, both, 0, 0, axis_index_groups=far)  30.7 us
    all_to_all x1, blocking collectives, local(): gathered = lax.all_to_all(normed, both, 0, 0, axis_index_groups=close)  18 us
    pallas_call x7, Pallas kernels, call(): pl.pallas_call(kernel, out_shape=outs, in_specs=[pl.BlockSpec(memory_spac...  10.2 us
    all_to_all x1, blocking collectives, local(): rows = lax.all_to_all(total, 'ctx', 0, 0, axis_index_groups=columns)  9.53 us
    all_to_all x1, waiting for transfers between devices, local(): parts = lax.all_to_all(maps, 'ctx', 0, 0, axis_index_groups=lines)  9.41 us
    all_gather x1, waiting for transfers between devices, local(): weight = lax.all_gather(own_half, 'tp', axis_index_groups=near, tiled=True)  6.62 us
    unnamed x18, local copies, waits for them, and re-layouts  6.19 us
    all_to_all x1, starting transfers between devices, local(): parts = lax.all_to_all(maps, 'ctx', 0, 0, axis_index_groups=lines)  5.11 us
  transfers between devices with their start and end apart: 3, of which 2 were waited for; matrix products, arithmetic and copies ran while one was open for 1% of the time, Pallas kernels for 8%

profile of v1, /device:TPU:33, one launch (start us, length us, event | category | flops | bytes accessed | tf_op | source)
XLA Modules:
  0.0 114.4 jit_solution(5986438542603691571)
XLA Ops:
  6.5 0.0 copy-start
  6.5 0.0 all-gather.2.cloned.1.call-start
  6.5 1.2 %copy-done = bf16[256,2048]{1,0:T(8,128)(2,1)S(1)} copy-done((bf16[256,2048]{1,0:T(8,128)(2,1)S(1)}, bf16[256,2048]{1,0:T(8,128)(2,1)}, u32[]{:S(2)}) %copy-start) | copy-done | bytes 1048600
  7.8 0.9 constant_dynamic-slice_fusion
  8.6 0.0 all-gather.2.cloned.1.call-update
  8.6 0.8 copy.10.decay_ref
  9.5 0.8 copy.9.rate_ref
  10.3 0.0 copy-start.2
  10.3 0.9 copy-done.2
  11.2 0.0 copy-start.4
  11.2 0.8 copy-done.4
  12.0 4.3 %shard_maps.1 = (bf16[8,128,256]{2,1,0:T(8,128)(2,1)}, f32[2,256,256]{2,1,0:T(8,128)S(1)}) custom-call(bf16[256,128]{1,0:T(8,128)(2,1)S(1)} %copy-done.4, bf16[256,256]{1,0:T(8,128)(2,1)S(1)} %copy-done.2, f32[256,2]{1,0:T(8,128)S(1)} %copy.9.rate_ref, f32[256,2]{1,0:T(8,128)S(1)} %copy.10.decay_ref), custom_call_target="tpu_custom_call" | custom-call | flops 1000000000 | bytes 1000000 | tf_op jit(solution)/shard_map/shard_maps/pallas_call | solution.py:265
  16.3 0.0 copy-start.3
  16.3 0.0 copy-start.5
  16.3 0.0 copy-start.6
  16.3 0.0 copy-start.7
  16.4 5.1 %all-to-all-start = ((bf16[8,128,256]{2,1,0:T(8,128)(2,1)}), bf16[8,128,256]{2,1,0:T(8,128)(2,1)S(1)}, u32[]{:S(2)}, u32[]{:S(2)}) async-start(bf16[8,128,256]{2,1,0:T(8,128)(2,1)} %get-tuple-element.15), calls=%async_computation | async-start | bytes 1048576 | tf_op jit(solution)/shard_map/all_to_all | solution.py:304
  21.5 0.1 pad_add_fusion.place_ref
  21.5 9.4 %all-to-all-done.parts_ref = bf16[8,128,256]{2,1,0:T(8,128)(2,1)S(1)} async-done(((bf16[8,128,256]{2,1,0:T(8,128)(2,1)}), bf16[8,128,256]{2,1,0:T(8,128)(2,1)S(1)}, u32[]{:S(2)}, u32[]{:S(2)}) %all-to-all-start) | async-done | bytes 524320 | tf_op jit(solution)/shard_map/all_to_all | solution.py:304
  30.9 1.2 %row_maps.1 = (bf16[4,128,256]{2,1,0:T(8,128)(2,1)S(1)}, f32[128,256]{1,0:T(8,128)S(1)}, bf16[128,256]{1,0:T(8,128)(2,1)S(1)}) custom-call(s32[3]{0:T(128)S(1)} %pad_add_fusion.place_ref, bf16[8,128,256]{2,1,0:T(8,128)(2,1)S(1)} %all-to-all-done.parts_ref), custom_call_target="tpu_custom_call" | custom-call | flops 100000000 | bytes 1000000 | tf_op jit(solution)/shard_map/row_maps/pallas_call | solution.py:265
  32.1 9.5 %all_to_all.20.rows_ref = bf16[4,128,256]{2,1,0:T(8,128)(2,1)S(1)} all-to-all(bf16[4,128,256]{2,1,0:T(8,128)(2,1)S(1)} %get-tuple-element.16), channel_id=1, replica_groups={{0,128,256,384},{16,144,272,400},{32,160,288,416},{48,176,304,432},{64,..., dimensions={0} | all-to-all | bytes 524288 | tf_op jit(solution)/shard_map/all_to_all | solution.py:326
  41.7 1.2 %states.1 = (bf16[128,128]{1,0:T(8,128)(2,1)S(1)}, bf16[128,128]{1,0:T(8,128)(2,1)S(1)}) custom-call(s32[3]{0:T(128)S(1)} %pad_add_fusion.place_ref, bf16[4,128,256]{2,1,0:T(8,128)(2,1)S(1)} %all_to_all.20.rows_ref, f32[128,256]{1,0:T(8,128)S(1)} %get-tuple-element.17.ahead_ref, bf16[128,256]{1,0:T(8,128)(2,1)S(1)} %get-tuple-element.18.first_ref), custom_call_target="tpu_custom_call" | custom-call | flops 100000000 | bytes 1000000 | tf_op jit(solution)/shard_map/states/pallas_call | solution.py:265
  42.9 4.2 %collective-permute-start = (bf16[128,128]{1,0:T(8,128)(2,1)S(1)}, bf16[128,128]{1,0:T(8,128)(2,1)S(1)}, u32[]{:S(2)}, u32[]{:S(2)}) collective-permute-start(bf16[128,128]{1,0:T(8,128)(2,1)S(1)} %get-tuple-element.20), channel_id=1, source_target_pairs={{0,16},{16,0},{32,48},{48,32},{64,80},{80,64},{96,112},{112,96},{1... | collective-permute-start | bytes 98312 | tf_op jit(solution)/shard_map/ppermute | solution.py:337
  47.1 0.0 copy-done.3
  47.1 0.0 copy-done.5
  47.1 0.0 copy-done.6
  47.1 0.0 copy-done.7
  47.1 1.1 read_parts.1
  48.3 0.0 collective-permute-done.came_ref
  48.3 0.9 gated_norm.1
  49.2 18.0 %all_to_all.21.normed_ref = bf16[8,64,256]{2,1,0:T(8,128)(2,1)S(1)} all-to-all(bf16[8,64,256]{2,1,0:T(8,128)(2,1)S(1)} %gated_norm.1), channel_id=1, replica_groups={{0,1,2,3,16,17,18,19},{4,5,6,7,20,21,22,23},{8,9,10,11,24,25,26,27},{12..., dimensions={0} | all-to-all | bytes 524288 | tf_op jit(solution)/shard_map/all_to_all | solution.py:356
  67.1 6.6 %all-gather.2.cloned.1.call-done.weight_ref = bf16[1024,1024]{1,0:T(8,128)(2,1)} async-done(((bf16[256,1024]{1,0:T(8,128)(2,1)}), bf16[1024,1024]{1,0:T(8,128)(2,1)}) %all-gather.2.cloned.1.call-update) | async-done | bytes 2097168 | tf_op jit(solution)/shard_map/all_gather | solution.py:291
  73.7 0.0 copy-start.1
  73.7 1.6 %copy-done.1 = bf16[1024,1024]{1,0:T(8,128)(2,1)S(1)} copy-done((bf16[1024,1024]{1,0:T(8,128)(2,1)S(1)}, bf16[1024,1024]{1,0:T(8,128)(2,1)}, u32[]{:S(2)}) %copy-start.1) | copy-done | bytes 2097176
  75.3 0.8 project.1
  76.2 30.7 %all_to_all.22.parts_ref = bf16[8,16,1024]{2,1,0:T(8,128)(2,1)S(1)} all-to-all(bf16[8,16,1024]{2,1,0:T(8,128)(2,1)S(1)} %project.1), channel_id=1, replica_groups={{0,4,8,12,16,20,24,28},{1,5,9,13,17,21,25,29},{2,6,10,14,18,22,26,30},{..., dimensions={0} | all-to-all | bytes 524288 | tf_op jit(solution)/shard_map/all_to_all | solution.py:364
  106.9 0.7 sum_shares.1
Async XLA Ops:
  6.5 1.2 %copy-start = (bf16[256,2048]{1,0:T(8,128)(2,1)S(1)}, bf16[256,2048]{1,0:T(8,128)(2,1)}, u32[]{:S(2)}) copy-start(bf16[256,2048]{1,0:T(8,128)(2,1)} %param.15) | copy-start | bytes 3145732
  6.5 67.2 %all-gather.2.cloned.1.call-start = ((), (), s32[]{:S(2)}) async-start(), calls=%async_computation.4 | async-start | bytes 2621440 | tf_op jit(solution)/shard_map/all_gather | solution.py:291
  10.3 0.9 copy-start.2
  11.2 0.8 copy-start.4
  16.3 30.7 %copy-start.3 = (bf16[256,256]{1,0:T(8,128)(2,1)S(1)}, bf16[256,256]{1,0:T(8,128)(2,1)}, u32[]{:S(2)}) copy-start(bf16[256,256]{1,0:T(8,128)(2,1)} %gate_ref.1) | copy-start | bytes 393220
  16.3 30.7 %copy-start.5 = (bf16[256,128]{1,0:T(8,128)(2,1)S(1)}, bf16[256,128]{1,0:T(8,128)(2,1)}, u32[]{:S(2)}) copy-start(bf16[256,128]{1,0:T(8,128)(2,1)} %k_ref.3) | copy-start | bytes 196612
  16.3 30.7 %copy-start.6 = (bf16[256,128]{1,0:T(8,128)(2,1)S(1)}, bf16[256,128]{1,0:T(8,128)(2,1)}, u32[]{:S(2)}) copy-start(bf16[256,128]{1,0:T(8,128)(2,1)} %q_ref.1) | copy-start | bytes 196612
  16.3 30.8 %copy-start.7 = (f32[128]{0:T(128)S(1)}, f32[128]{0:T(128)}, u32[]{:S(2)}) copy-start(f32[128]{0:T(128)} %param.14) | copy-start | bytes 1540
  16.4 14.6 %all-to-all-start = ((bf16[8,128,256]{2,1,0:T(8,128)(2,1)}), bf16[8,128,256]{2,1,0:T(8,128)(2,1)S(1)}, u32[]{:S(2)}, u32[]{:S(2)}) async-start(bf16[8,128,256]{2,1,0:T(8,128)(2,1)} %get-tuple-element.15), calls=%async_computation | async-start | bytes 1048576 | tf_op jit(solution)/shard_map/all_to_all | solution.py:304
  42.9 5.4 %collective-permute-start = (bf16[128,128]{1,0:T(8,128)(2,1)S(1)}, bf16[128,128]{1,0:T(8,128)(2,1)S(1)}, u32[]{:S(2)}, u32[]{:S(2)}) collective-permute-start(bf16[128,128]{1,0:T(8,128)(2,1)S(1)} %get-tuple-element.20), channel_id=1, source_target_pairs={{0,16},{16,0},{32,48},{48,32},{64,80},{80,64},{96,112},{112,96},{1... | collective-permute-start | bytes 98312 | tf_op jit(solution)/shard_map/ppermute | solution.py:337
  73.7 1.6 %copy-start.1 = (bf16[1024,1024]{1,0:T(8,128)(2,1)S(1)}, bf16[1024,1024]{1,0:T(8,128)(2,1)}, u32[]{:S(2)}) copy-start(bf16[1024,1024]{1,0:T(8,128)(2,1)} %all-gather.2.cloned.1.call-done.weight_ref) | copy-start | bytes 6291460
Sparse Core Ops, SparseCore 0:
  9.5 64.2 all-gather.1

commit v2 on v1

v2 whole, which is shorter than its diff:
```python
import jax
import jax.numpy as jnp
from jax import lax
from jax.experimental import pallas as pl
from jax.experimental.pallas import tpu as pltpu
from jax.sharding import PartitionSpec as P

F32 = jnp.float32
BF = jnp.bfloat16
TOK = 256
DK = 128
DV = 128
HALF = 128


def dot(a, b, dims=((1,), (0,))):
    return lax.dot_general(a, b, (dims, ((), ())), preferred_element_type=F32)


def split(a):
    hi = a.astype(BF)
    return hi, (a - hi.astype(F32)).astype(BF)


def dot_fine(a, b, dims=((1,), (0,))):
    ah, al = split(a)
    bh, bl = split(b)
    return dot(ah, bh, dims) + (dot(ah, bl, dims) + dot(al, bh, dims))


def dot_left(a, b, dims=((1,), (0,))):
    ah, al = split(a)
    return dot(ah, b, dims) + dot(al, b, dims)


def dot_right(a, b, dims=((1,), (0,))):
    bh, bl = split(b)
    return dot(a, bh, dims) + dot(a, bl, dims)


def grid_iota(rows, cols):
    return (
        lax.broadcasted_iota(jnp.int32, (rows, cols), 0),
        lax.broadcasted_iota(jnp.int32, (rows, cols), 1),
    )


def to_row(eye, column):
    return jnp.sum(jnp.where(eye, column, 0.0), axis=0, keepdims=True)


def to_column(eye, row):
    return jnp.sum(jnp.where(eye, row, 0.0), axis=1, keepdims=True)


def decay_sums(decay):
    row, col = grid_iota(TOK, TOK)
    ones = jnp.where(row <= col, 1.0, 0.0).astype(BF)
    eye = row == col
    hi = decay.astype(BF).astype(F32)
    rest = decay - hi
    mid = rest.astype(BF).astype(F32)
    low = rest - mid
    parts = jnp.concatenate([hi, mid, low, jnp.zeros((2, TOK), F32)], axis=0)
    sums = dot(parts.astype(BF), ones)
    rows = sums[0:2] + (sums[2:4] + sums[4:6])
    return [(rows[h : h + 1], to_column(eye, rows[h : h + 1])) for h in range(2)]


def unit_scale(source):
    full = source.astype(F32)
    return lax.rsqrt(jnp.sum(full * full, axis=1, keepdims=True) + 1e-06)


def map_kernel(
    place_ref,
    k_far,
    v_far,
    rate_far,
    decay_far,
    weight_far,
    maps_ref,
    solved_ref,
    half_ref,
    k_ref,
    v_ref,
    rate_ref,
    decay_ref,
    sems,
):
    rows = half_ref.shape[0]
    begin = pl.multiple_of(place_ref[2] * rows, rows)
    copies = [
        pltpu.make_async_copy(k_far, k_ref, sems.at[0]),
        pltpu.make_async_copy(decay_far, decay_ref, sems.at[1]),
        pltpu.make_async_copy(rate_far, rate_ref, sems.at[2]),
        pltpu.make_async_copy(v_far, v_ref, sems.at[3]),
        pltpu.make_async_copy(weight_far.at[pl.ds(begin, rows)], half_ref, sems.at[4]),
    ]
    for copy in copies:
        copy.start()
    for copy in copies[:4]:
        copy.wait()
    keys = k_ref[...]
    keys_f = keys.astype(F32)
    values = v_ref[...].astype(F32)
    row, col = grid_iota(TOK, TOK)
    eye = row == col
    strict = row > col
    rate = [to_column(eye, rate_ref[h : h + 1, :]) for h in range(2)]
    gram = dot(keys, keys, ((1,), (1,)))
    scale = unit_scale(keys)
    gram = gram * scale * to_row(eye, scale)
    sum_rows, sums = zip(*decay_sums(decay_ref[...]))
    r_s, c_s = grid_iota(HALF, HALF)
    eye_s = jnp.where(r_s == c_s, 1.0, 0.0).astype(F32)

    lowers, corners = [], []
    for head in range(2):
        fall = jnp.exp(jnp.minimum(sums[head] - sum_rows[head], 0.0))
        low = jnp.where(strict, rate[head] * gram * fall, 0.0)
        lowers += [low[:HALF, :HALF], low[HALF:, HALF:]]
        corners.append(low[HALF:, :HALF])

    small = (r_s // 8) == (c_s // 8)
    first = [jnp.where(small, low, 0.0) for low in lowers]
    first_b = [a.astype(BF) for a in first]
    square = [dot(a, a).astype(BF) for a in first_b]
    fourth = [dot(a, a).astype(BF) for a in square]
    inv = [eye_s - a for a in first]
    inv = [x + dot(x.astype(BF), a) for x, a in zip(inv, square)]
    inv = [x + dot(x.astype(BF), a) for x, a in zip(inv, fourth)]
    size = 8
    while size < HALF:
        off = ((r_s // (2 * size)) == (c_s // (2 * size))) & ((r_s // size) > (c_s // size))
        inv_b = [x.astype(BF) for x in inv]
        part = [jnp.where(off, low, 0.0).astype(BF) for low in lowers]
        part = [dot(a, x).astype(BF) for a, x in zip(part, inv_b)]
        inv = [x - dot(xb, a) for x, xb, a in zip(inv, inv_b, part)]
        size *= 2
    inv_b = [x.astype(BF) for x in inv]
    gap = [
        eye_s - xb.astype(F32) - dot_left(low, xb) for low, xb in zip(lowers, inv_b)
    ]
    inv = [xb.astype(F32) + dot(xb, g.astype(BF)) for xb, g in zip(inv_b, gap)]

    eye_k = jnp.where(r_s == c_s, 1.0, 0.0).astype(F32)
    solved = []
    for head in range(2):
        b = rate[head]
        grow = b * jnp.exp(sums[head]) * scale
        right = jnp.concatenate(
            [grow * keys_f, b * values[:, head * DV : (head + 1) * DV]], axis=1
        )
        top = dot_fine(inv[2 * head], right[:HALF])
        solved.append((top, right[HALF:]))
    for head in range(2):
        top, below = solved[head]
        below = below - dot_fine(corners[head], top)
        below = dot_fine(inv[2 * head + 1], below)
        solved[head] = jnp.concatenate([top, below], axis=0)
    maps = []
    for head in range(2):
        closing = sums[head][TOK - 1 :, :]
        weight = scale * jnp.exp(closing - sums[head])
        moved = dot_right(keys, weight * solved[head], ((0,), (0,)))
        transit = eye_k * jnp.exp(closing) - moved[:, :DK]
        maps.append(jnp.concatenate([transit, moved[:, DK:]], axis=1).astype(BF))
    for place in range(maps_ref.shape[0]):
        maps_ref[place] = maps[place % 2]
    for head in range(2):
        solved_ref[head] = solved[head]
    copies[4].wait()


def read_kernel(
    place_ref, q_ref, k_ref, decay_ref, gate_ref, gain_ref, solved_ref, keep_ref, send_ref
):
    core = place_ref[2]
    queries = q_ref[...]
    keys = k_ref[...]
    row, col = grid_iota(TOK, TOK)
    eye = row == col
    inclusive = row >= col
    unit_q = unit_scale(queries)
    scores = dot(queries, keys, ((1,), (1,))) * unit_q * to_row(eye, unit_scale(keys))
    sums = decay_sums(decay_ref[...])
    read = []
    for head in range(2):
        sum_row, sum_column = sums[head]
        fall = jnp.exp(jnp.minimum(sum_column - sum_row, 0.0))
        weights = jnp.where(inclusive, scores * fall, 0.0)
        both = dot_fine(weights, solved_ref[head])
        outer = jnp.exp(sum_column) * unit_q * queries.astype(F32) - both[:, :DK]
        gate = gate_ref[:, head * DV : (head + 1) * DV].astype(F32)
        gated = gain_ref[...] * (gate / (1.0 + jnp.exp(-gate)))
        read.append((both[:, DK:], outer, gated))
    for i in range(3):
        keep_ref[i] = jnp.where(core == 0, read[0][i], read[1][i])
        send_ref[i] = jnp.where(core == 0, read[1][i], read[0][i]).astype(BF)


def after(later_t, later_h, earlier, fine):
    moved = dot_fine(later_t, earlier) if fine else dot_right(later_t, earlier)
    return jnp.concatenate([moved[:, :DK], moved[:, DK:] + later_h], axis=1)


def row_kernel(place_ref, parts_ref, total_ref, ahead_ref, first_ref):
    x = place_ref[1]

    def pair(i):
        later = parts_ref[2 * i + 1]
        moved = dot(later[:, :DK], parts_ref[2 * i])
        return jnp.concatenate(
            [moved[:, :DK], moved[:, DK:] + later[:, DK:].astype(F32)], axis=1
        )

    pairs = [pair(i) for i in range(4)]
    upto2 = pairs[0]
    upto4 = after(pairs[1][:, :DK], pairs[1][:, DK:], upto2, True)
    last2 = after(pairs[3][:, :DK], pairs[3][:, DK:], pairs[2], True)
    upto6 = after(pairs[2][:, :DK], pairs[2][:, DK:], upto4, True)
    total = after(last2[:, :DK], last2[:, DK:], upto4, True).astype(BF)
    for place in range(4):
        total_ref[place] = total
    row, col = grid_iota(DK, DK + DV)
    none = jnp.where(row == col, 1.0, 0.0).astype(F32)
    ahead_ref[...] = jnp.where(
        x == 0, none, jnp.where(x == 1, upto2, jnp.where(x == 2, upto4, upto6))
    )
    first_ref[...] = parts_ref[2 * x]


def token_of(group, label):
    return 4 * group + (label if group < 2 else 3 - label)


def out_kernel(place_ref, rows_ref, ahead_ref, first_ref, keep_ref, came_ref, out_ref):
    y = place_ref[0]
    core = place_ref[2]

    def onward(later, state):
        return dot_right(later[:, :DK], state) + later[:, DK:].astype(F32)

    one = rows_ref[0][:, DK:].astype(F32)
    two = onward(rows_ref[1], one)
    three = onward(rows_ref[2], two)
    start = jnp.where(
        y == 0, jnp.zeros_like(one), jnp.where(y == 1, one, jnp.where(y == 2, two, three))
    )
    ahead = ahead_ref[...]
    chip = dot_fine(ahead[:, :DK], start) + ahead[:, DK:]
    second = onward(first_ref[...], chip)

    def finish(state, inner, outer, gated):
        reached = inner + dot_left(outer, state.astype(BF))
        mean = jnp.sum(reached * reached, axis=1, keepdims=True) * (1.0 / DV)
        return (reached * lax.rsqrt(mean + 1e-06) * gated).astype(BF)

    own = finish(jnp.where(core == 0, chip, second), keep_ref[0], keep_ref[1], keep_ref[2])
    came = [came_ref[i].astype(F32) for i in range(3)]
    other = finish(jnp.where(core == 0, second, chip), *came)
    shards = (jnp.where(core == 0, own, other), jnp.where(core == 0, other, own))
    for label in range(4):
        for shard in range(2):
            for group in range(4):
                source = 16 * token_of(group, label)
                target = 64 * shard + 16 * group
                out_ref[label, target : target + 16] = shards[shard][source : source + 16]


def project_kernel(place_ref, normed_ref, w0_ref, w1_ref, w2_ref, w3_ref, keep_ref, send_ref):
    core = place_ref[2]
    total = None
    for i, weight_ref in enumerate((w0_ref, w1_ref, w2_ref, w3_ref)):
        term = dot(normed_ref[place_ref[4 + i]], weight_ref[...])
        total = term if total is None else total + term
    keep_ref[...] = jnp.where(core == 0, total[:64], total[64:])
    send_ref[...] = jnp.where(core == 0, total[64:], total[:64]).astype(BF)


def join_kernel(keep_ref, came_ref, out_ref):
    total = (keep_ref[...] + came_ref[...].astype(F32)).astype(BF)
    for group in range(4):
        out_ref[group] = total[16 * group : 16 * (group + 1)]


def sum_kernel(parts_ref, out_ref):
    total = parts_ref[0].astype(F32)
    for group in range(1, 4):
        total = total + parts_ref[group].astype(F32)
    out_ref[...] = total.astype(BF)


def in_vmem():
    return pl.BlockSpec(memory_space=pltpu.VMEM)


def in_hbm():
    return pl.BlockSpec(memory_space=pltpu.HBM)


def call(kernel, outs, *args, scalars=0, flops=10**8, name=None, ins=None, out_specs=None, scratch=(), room=32):
    if ins is None:
        ins = [in_vmem()] * (len(args) - scalars)
    return pl.pallas_call(
        kernel,
        out_shape=outs,
        in_specs=[pl.BlockSpec(memory_space=pltpu.SMEM)] * scalars + ins,
        out_specs=jax.tree.map(lambda _: in_vmem(), outs) if out_specs is None else out_specs,
        scratch_shapes=scratch,
        compiler_params=pltpu.CompilerParams(vmem_limit_bytes=room * 1024 * 1024),
        cost_estimate=pl.CostEstimate(flops=flops, bytes_accessed=10**6, transcendentals=0),
        name=name,
    )(*args)


def shape(dims, kind):
    return jax.ShapeDtypeStruct(dims, kind)


def local(
    queries, key_vectors, value_vectors, output_gate, write_rate, log_decay, norm_gain, out_weight
):
    at = lax.axis_index("ctx")
    along = lax.axis_index("tp")
    near = along % 4
    label = [jnp.where(along < 8, near ^ i, 3 - (near ^ i)) for i in range(4)]
    place = jnp.stack([at // 8, (at // 2) % 4, at % 2, along] + label).astype(jnp.int32)
    width = out_weight.shape[1]
    rate, decay = write_rate.T, log_decay.T

    maps, solved, w0 = call(
        map_kernel,
        (
            shape((8, DK, DK + DV), BF),
            shape((2, TOK, DK + DV), F32),
            shape((DV, width), BF),
        ),
        place,
        key_vectors,
        value_vectors,
        rate,
        decay,
        out_weight,
        scalars=1,
        ins=[in_hbm()] * 5,
        out_specs=(in_vmem(), in_vmem(), in_hbm()),
        scratch=[
            pltpu.VMEM((TOK, DK), BF),
            pltpu.VMEM((TOK, 2 * DV), BF),
            pltpu.VMEM((2, TOK), F32),
            pltpu.VMEM((2, TOK), F32),
            pltpu.SemaphoreType.DMA((5,)),
        ],
        flops=10**9,
        room=60,
        name="shard_maps",
    )
    lines = [[8 * y + i for i in range(8)] for y in range(4)]
    parts = lax.all_to_all(maps, "ctx", 0, 0, axis_index_groups=lines)
    keep, send = call(
        read_kernel,
        (shape((3, TOK, DV), F32), shape((3, TOK, DV), BF)),
        place,
        queries,
        key_vectors,
        decay,
        output_gate,
        norm_gain.reshape(1, DV),
        solved,
        scalars=1,
        flops=10**9,
        name="read_parts",
    )
    across = [(i, i ^ 1) for i in range(32)]
    came = lax.ppermute(send, "ctx", across)

    w1 = lax.ppermute(w0, "tp", [(j, j ^ 1) for j in range(16)])
    w2 = lax.ppermute(w0, "tp", [(j, j ^ 2) for j in range(16)])
    w3 = lax.ppermute(w2, "tp", [(j, j ^ 1) for j in range(16)])

    total, ahead, first = call(
        row_kernel,
        (shape((4, DK, DK + DV), BF), shape((DK, DK + DV), F32), shape((DK, DK + DV), BF)),
        place,
        parts,
        scalars=1,
        name="row_maps",
    )
    columns = [[8 * y + i for y in range(4)] for i in range(8)]
    rows = lax.all_to_all(total, "ctx", 0, 0, axis_index_groups=columns)
    normed = call(
        out_kernel,
        shape((4, 128, DV), BF),
        place,
        rows,
        ahead,
        first,
        keep,
        came,
        scalars=1,
        name="gated_norm",
    )
    close = [[token_of(g, m) for m in range(4)] for g in range(4)]
    gathered = lax.all_to_all(normed, "tp", 0, 0, axis_index_groups=close)
    half, other_half = call(
        project_kernel,
        (shape((64, width), F32), shape((64, width), BF)),
        place,
        gathered,
        w0,
        w1,
        w2,
        w3,
        scalars=1,
        name="project",
    )
    other_half = lax.ppermute(other_half, "ctx", across)
    partial = call(join_kernel, shape((4, 16, width), BF), half, other_half, name="join")
    far = [[token_of(g, m) for g in range(4)] for m in range(4)]
    shares = lax.all_to_all(partial, "tp", 0, 0, axis_index_groups=far)
    return call(sum_kernel, shape((16, width), BF), shares, name="sum_shares")


def solution(mesh):
    placed = (
        P("ctx", "tp"),
        P("ctx", "tp"),
        P("ctx", "tp"),
        P("ctx", "tp"),
        P("ctx", "tp"),
        P("ctx", "tp"),
        P(),
        P("tp", None),
    )
    return jax.shard_map(
        local, mesh=mesh, in_specs=placed, out_specs=P(("ctx", "tp"), None), check_vma=False
    )
```

time: 115 us -> 115 us (level)
  the two profiles are of different devices: /device:TPU:33 before, /device:TPU:24 now
where the time goes in v2:
time: 115 us
  blocking collectives  31.6 us (27%)
  starting transfers between devices  30.2 us (26%)
  Pallas kernels  26.7 us (23%)
  waiting for transfers between devices  23.5 us (20%)
  local copies, waits for them, and re-layouts  2.36 us (2%)
    all_to_all x1, blocking collectives, local(): shares = lax.all_to_all(partial, 'tp', 0, 0, axis_index_groups=far)  31.6 us
    pallas_call x7, Pallas kernels, call(): pl.pallas_call(kernel, out_shape=outs, in_specs=[pl.BlockSpec(memory_spac...  26.7 us
    all_to_all x1, waiting for transfers between devices, local(): gathered = lax.all_to_all(normed, 'tp', 0, 0, axis_index_groups=close)  13.2 us
    all_to_all x1, starting transfers between devices, local(): rows = lax.all_to_all(total, 'ctx', 0, 0, axis_index_groups=columns)  7.28 us
    ppermute x1, waiting for transfers between devices, local(): w2 = lax.ppermute(w0, 'tp', [(j, j ^ 2) for j in range(16)])  7 us
    ppermute x1, starting transfers between devices, local(): w2 = lax.ppermute(w0, 'tp', [(j, j ^ 2) for j in range(16)])  5.18 us
    all_to_all x1, starting transfers between devices, local(): gathered = lax.all_to_all(normed, 'tp', 0, 0, axis_index_groups=close)  4.69 us
    all_to_all x1, starting transfers between devices, local(): parts = lax.all_to_all(maps, 'ctx', 0, 0, axis_index_groups=lines)  4.44 us
  transfers between devices with their start and end apart: 8, of which 4 were waited for; matrix products, arithmetic and copies ran while one was open for 0% of the time, Pallas kernels for 5%

profile of v2, /device:TPU:24, one launch (start us, length us, event | category | flops | bytes accessed | tf_op | source)
XLA Modules:
  0.0 114.5 jit_solution(16175094869011547696)
XLA Ops:
  0.0 0.7 stack.35.place_ref
  0.7 18.7 %shard_maps.1 = (bf16[8,128,256]{2,1,0:T(8,128)(2,1)}, f32[2,256,256]{2,1,0:T(8,128)}, bf16[128,2048]{1,0:T(8,128)(2,1)}) custom-call(s32[8]{0:T(128)} %stack.35.place_ref, bf16[256,128]{1,0:T(8,128)(2,1)} %k_ref.1, bf16[256,256]{1,0:T(8,128)(2,1)} %v_far.1, f32[2,256]{1,0:T(2,128)} %bitcast.14, f32[2,256]{1,0:T(2,128)} %bitcast.11, bf16[256,2048]{1,0:T(8,128)(2,1)} %weight_far.1), custom_call_target="tpu_custom_call" | custom-call | flops 1000000000 | bytes 1000000 | tf_op jit(solution)/shard_map/shard_maps/pallas_call | solution.py:306
  19.4 0.0 copy-start
  19.4 0.0 copy-start.2
  19.4 0.0 copy-start.3
  19.4 0.0 copy-start.4
  19.4 4.4 %all-to-all-start = ((bf16[8,128,256]{2,1,0:T(8,128)(2,1)}), bf16[8,128,256]{2,1,0:T(8,128)(2,1)S(1)}, u32[]{:S(2)}, u32[]{:S(2)}) async-start(bf16[8,128,256]{2,1,0:T(8,128)(2,1)} %get-tuple-element.15), calls=%async_computation | async-start | bytes 1048576 | tf_op jit(solution)/shard_map/all_to_all | solution.py:361
  23.9 0.0 copy-done
  23.9 0.0 copy-start.5
  23.9 5.2 %collective-permute-start.2 = (bf16[128,2048]{1,0:T(8,128)(2,1)S(1)}, bf16[128,2048]{1,0:T(8,128)(2,1)S(1)}, u32[]{:S(2)}, u32[]{:S(2)}) collective-permute-start(bf16[128,2048]{1,0:T(8,128)(2,1)S(1)} %copy-done), channel_id=1, source_target_pairs={{0,2},{1,3},{2,0},{3,1},{4,6},{5,7},{6,4},{7,5},{8,10},{9,11},{10,... | collective-permute-start | bytes 1572872 | tf_op jit(solution)/shard_map/ppermute | solution.py:380
  29.1 0.0 copy-start.1
  29.1 0.0 copy-start.6
  29.1 0.0 copy-done.2
  29.1 0.0 copy-done.3
  29.1 0.0 copy-done.4
  29.1 0.0 copy-done.5
  29.1 0.6 copy-done.1
  29.7 0.0 copy-done.6
  29.7 0.0 copy-start.7
  29.7 1.0 copy-done.7
  30.8 2.0 %read_parts.1 = (f32[3,256,128]{2,1,0:T(8,128)S(1)}, bf16[3,256,128]{2,1,0:T(8,128)(2,1)}) custom-call(s32[8]{0:T(128)S(1)} %copy-done.1, bf16[256,128]{1,0:T(8,128)(2,1)S(1)} %copy-done.4, bf16[256,128]{1,0:T(8,128)(2,1)S(1)} %copy-done.3, f32[2,256]{1,0:T(2,128)S(1)} %bitcast.12, bf16[256,256]{1,0:T(8,128)(2,1)S(1)} %copy-done.2, f32[1,128]{1,0:T(1,128)S(1)} %bitcast.13, ...), custom_call_target="tpu_custom_call" | custom-call | flops 1000000000 | bytes 1000000 | tf_op jit(solution)/shard_map/read_parts/pallas_call | solution.py:306
  32.8 2.2 %collective-permute-start = (bf16[3,256,128]{2,1,0:T(8,128)(2,1)}, bf16[3,256,128]{2,1,0:T(8,128)(2,1)S(1)}, u32[]{:S(2)}, u32[]{:S(2)}) collective-permute-start(bf16[3,256,128]{2,1,0:T(8,128)(2,1)} %get-tuple-element.21), channel_id=1, source_target_pairs={{0,16},{16,0},{32,48},{48,32},{64,80},{80,64},{96,112},{112,96},{1... | collective-permute-start | bytes 589832 | tf_op jit(solution)/shard_map/ppermute | solution.py:377
  35.0 0.0 all-to-all-done.parts_ref
  35.0 1.9 %row_maps.1 = (bf16[4,128,256]{2,1,0:T(8,128)(2,1)}, f32[128,256]{1,0:T(8,128)S(1)}, bf16[128,256]{1,0:T(8,128)(2,1)S(1)}) custom-call(s32[8]{0:T(128)S(1)} %copy-done.1, bf16[8,128,256]{2,1,0:T(8,128)(2,1)S(1)} %all-to-all-done.parts_ref), custom_call_target="tpu_custom_call" | custom-call | flops 100000000 | bytes 1000000 | tf_op jit(solution)/shard_map/row_maps/pallas_call | solution.py:306
  36.9 7.3 %all-to-all-start.1 = ((bf16[4,128,256]{2,1,0:T(8,128)(2,1)}), bf16[4,128,256]{2,1,0:T(8,128)(2,1)S(1)}, u32[]{:S(2)}, u32[]{:S(2)}) async-start(bf16[4,128,256]{2,1,0:T(8,128)(2,1)} %get-tuple-element.16), calls=%async_computation.1 | async-start | bytes 524288 | tf_op jit(solution)/shard_map/all_to_all | solution.py:392
  44.2 1.9 %collective-permute-start.1 = (bf16[128,2048]{1,0:T(8,128)(2,1)S(1)}, bf16[128,2048]{1,0:T(8,128)(2,1)S(1)}, u32[]{:S(2)}, u32[]{:S(2)}) collective-permute-start(bf16[128,2048]{1,0:T(8,128)(2,1)S(1)} %copy-done), channel_id=1, source_target_pairs={{0,1},{1,0},{2,3},{3,2},{4,5},{5,4},{6,7},{7,6},{8,9},{9,8},{10,11... | collective-permute-start | bytes 1572872 | tf_op jit(solution)/shard_map/ppermute | solution.py:379
  46.1 7.0 %collective-permute-done.2.w2_ref = bf16[128,2048]{1,0:T(8,128)(2,1)S(1)} collective-permute-done((bf16[128,2048]{1,0:T(8,128)(2,1)S(1)}, bf16[128,2048]{1,0:T(8,128)(2,1)S(1)}, u32[]{:S(2)}, u32[]{:S(2)}) %collective-permute-start.2) | collective-permute-done | bytes 524320 | tf_op jit(solution)/shard_map/ppermute | solution.py:380
  53.1 2.6 %collective-permute-start.3 = (bf16[128,2048]{1,0:T(8,128)(2,1)S(1)}, bf16[128,2048]{1,0:T(8,128)(2,1)S(1)}, u32[]{:S(2)}, u32[]{:S(2)}) collective-permute-start(bf16[128,2048]{1,0:T(8,128)(2,1)S(1)} %collective-permute-done.2.w2_ref), channel_id=1, source_target_pairs={{0,1},{1,0},{2,3},{3,2},{4,5},{5,4},{6,7},{7,6},{8,9},{9,8},{10,11... | collective-permute-start | bytes 1572872 | tf_op jit(solution)/shard_map/ppermute | solution.py:381
  55.7 0.0 collective-permute-done.came_ref
  55.7 0.0 all-to-all-done.1.rows_ref
  55.7 2.2 %gated_norm.1 = bf16[4,128,128]{2,1,0:T(8,128)(2,1)} custom-call(s32[8]{0:T(128)S(1)} %copy-done.1, bf16[4,128,256]{2,1,0:T(8,128)(2,1)S(1)} %all-to-all-done.1.rows_ref, f32[128,256]{1,0:T(8,128)S(1)} %get-tuple-element.17.ahead_ref, bf16[128,256]{1,0:T(8,128)(2,1)S(1)} %get-tuple-element.18.first_ref, f32[3,256,128]{2,1,0:T(8,128)S(1)} %get-tuple-element.20.keep_ref, ...), custom_call_target="tpu_custom_call" | custom-call | flops 100000000 | bytes 1000000 | tf_op jit(solution)/shard_map/gated_norm/pallas_call | solution.py:306
  57.9 4.7 %all-to-all-start.2 = ((bf16[4,128,128]{2,1,0:T(8,128)(2,1)}), bf16[4,128,128]{2,1,0:T(8,128)(2,1)S(1)}, u32[]{:S(2)}, u32[]{:S(2)}) async-start(bf16[4,128,128]{2,1,0:T(8,128)(2,1)} %gated_norm.1), calls=%async_computation.2 | async-start | bytes 262144 | tf_op jit(solution)/shard_map/all_to_all | solution.py:406
  62.6 1.8 %collective-permute-done.1.w1_ref = bf16[128,2048]{1,0:T(8,128)(2,1)S(1)} collective-permute-done((bf16[128,2048]{1,0:T(8,128)(2,1)S(1)}, bf16[128,2048]{1,0:T(8,128)(2,1)S(1)}, u32[]{:S(2)}, u32[]{:S(2)}) %collective-permute-start.1) | collective-permute-done | bytes 524320 | tf_op jit(solution)/shard_map/ppermute | solution.py:379
  64.3 13.2 %all-to-all-done.2.normed_ref = bf16[4,128,128]{2,1,0:T(8,128)(2,1)S(1)} async-done(((bf16[4,128,128]{2,1,0:T(8,128)(2,1)}), bf16[4,128,128]{2,1,0:T(8,128)(2,1)S(1)}, u32[]{:S(2)}, u32[]{:S(2)}) %all-to-all-start.2) | async-done | bytes 131104 | tf_op jit(solution)/shard_map/all_to_all | solution.py:406
  77.6 0.0 collective-permute-done.3.w3_ref
  77.6 1.2 %project.1 = (f32[64,2048]{1,0:T(8,128)S(1)}, bf16[64,2048]{1,0:T(8,128)(2,1)S(1)}) custom-call(s32[8]{0:T(128)S(1)} %copy-done.1, bf16[4,128,128]{2,1,0:T(8,128)(2,1)S(1)} %all-to-all-done.2.normed_ref, bf16[128,2048]{1,0:T(8,128)(2,1)S(1)} %copy-done, bf16[128,2048]{1,0:T(8,128)(2,1)S(1)} %collective-permute-done.1.w1_ref, ...), custom_call_target="tpu_custom_call" | custom-call | flops 100000000 | bytes 1000000 | tf_op jit(solution)/shard_map/project/pallas_call | solution.py:306
  78.8 1.9 %collective-permute-start.4 = (bf16[64,2048]{1,0:T(8,128)(2,1)S(1)}, bf16[64,2048]{1,0:T(8,128)(2,1)S(1)}, u32[]{:S(2)}, u32[]{:S(2)}) collective-permute-start(bf16[64,2048]{1,0:T(8,128)(2,1)S(1)} %get-tuple-element.24), channel_id=1, source_target_pairs={{0,16},{16,0},{32,48},{48,32},{64,80},{80,64},{96,112},{112,96},{1... | collective-permute-start | bytes 786440 | tf_op jit(solution)/shard_map/ppermute | solution.py:419
  80.8 1.5 %collective-permute-done.4.came_ref = bf16[64,2048]{1,0:T(8,128)(2,1)S(1)} collective-permute-done((bf16[64,2048]{1,0:T(8,128)(2,1)S(1)}, bf16[64,2048]{1,0:T(8,128)(2,1)S(1)}, u32[]{:S(2)}, u32[]{:S(2)}) %collective-permute-start.4) | collective-permute-done | bytes 262176 | tf_op jit(solution)/shard_map/ppermute | solution.py:419
  82.3 31.6 %all_to_all.20.parts_ref = bf16[4,16,2048]{2,1,0:T(8,128)(2,1)S(1)} all-to-all(bf16[4,16,2048]{2,1,0:T(8,128)(2,1)S(1)} %join.1), channel_id=1, replica_groups={{0,4,11,15},{1,5,10,14},{2,6,9,13},{3,7,8,12},{16,20,27,31},{17,21,26,3..., dimensions={0} | all-to-all | bytes 524288 | tf_op jit(solution)/shard_map/all_to_all | solution.py:422
  113.9 0.7 sum_shares.1
  (1 shorter events, 0.0 us)
Async XLA Ops:
  19.4 4.5 %copy-start = (bf16[128,2048]{1,0:T(8,128)(2,1)S(1)}, bf16[128,2048]{1,0:T(8,128)(2,1)}, u32[]{:S(2)}) copy-start(bf16[128,2048]{1,0:T(8,128)(2,1)} %get-tuple-element.22.w0_ref) | copy-start | bytes 1572868
  19.4 9.7 %copy-start.2 = (bf16[256,256]{1,0:T(8,128)(2,1)S(1)}, bf16[256,256]{1,0:T(8,128)(2,1)}, u32[]{:S(2)}) copy-start(bf16[256,256]{1,0:T(8,128)(2,1)} %gate_ref.1) | copy-start | bytes 393220
  19.4 9.7 %copy-start.3 = (bf16[256,128]{1,0:T(8,128)(2,1)S(1)}, bf16[256,128]{1,0:T(8,128)(2,1)}, u32[]{:S(2)}) copy-start(bf16[256,128]{1,0:T(8,128)(2,1)} %k_ref.1) | copy-start | bytes 196612
  19.4 9.7 %copy-start.4 = (bf16[256,128]{1,0:T(8,128)(2,1)S(1)}, bf16[256,128]{1,0:T(8,128)(2,1)}, u32[]{:S(2)}) copy-start(bf16[256,128]{1,0:T(8,128)(2,1)} %q_ref.1) | copy-start | bytes 196612
  19.4 15.6 %all-to-all-start = ((bf16[8,128,256]{2,1,0:T(8,128)(2,1)}), bf16[8,128,256]{2,1,0:T(8,128)(2,1)S(1)}, u32[]{:S(2)}, u32[]{:S(2)}) async-start(bf16[8,128,256]{2,1,0:T(8,128)(2,1)} %get-tuple-element.15), calls=%async_computation | async-start | bytes 1048576 | tf_op jit(solution)/shard_map/all_to_all | solution.py:361
  23.9 5.3 %copy-start.5 = (f32[256,2]{0,1:T(2,128)S(1)}, f32[256,2]{0,1:T(2,128)}, u32[]{:S(2)}) copy-start(f32[256,2]{0,1:T(2,128)} %param.13) | copy-start | bytes 6148
  23.9 29.2 %collective-permute-start.2 = (bf16[128,2048]{1,0:T(8,128)(2,1)S(1)}, bf16[128,2048]{1,0:T(8,128)(2,1)S(1)}, u32[]{:S(2)}, u32[]{:S(2)}) collective-permute-start(bf16[128,2048]{1,0:T(8,128)(2,1)S(1)} %copy-done), channel_id=1, source_target_pairs={{0,2},{1,3},{2,0},{3,1},{4,6},{5,7},{6,4},{7,5},{8,10},{9,11},{10,... | collective-permute-start | bytes 1572872 | tf_op jit(solution)/shard_map/ppermute | solution.py:380
  29.1 0.7 copy-start.1
  29.1 0.7 copy-start.6
  29.7 1.0 copy-start.7
  32.8 22.9 %collective-permute-start = (bf16[3,256,128]{2,1,0:T(8,128)(2,1)}, bf16[3,256,128]{2,1,0:T(8,128)(2,1)S(1)}, u32[]{:S(2)}, u32[]{:S(2)}) collective-permute-start(bf16[3,256,128]{2,1,0:T(8,128)(2,1)} %get-tuple-element.21), channel_id=1, source_target_pairs={{0,16},{16,0},{32,48},{48,32},{64,80},{80,64},{96,112},{112,96},{1... | collective-permute-start | bytes 589832 | tf_op jit(solution)/shard_map/ppermute | solution.py:377
  36.9 18.8 %all-to-all-start.1 = ((bf16[4,128,256]{2,1,0:T(8,128)(2,1)}), bf16[4,128,256]{2,1,0:T(8,128)(2,1)S(1)}, u32[]{:S(2)}, u32[]{:S(2)}) async-start(bf16[4,128,256]{2,1,0:T(8,128)(2,1)} %get-tuple-element.16), calls=%async_computation.1 | async-start | bytes 524288 | tf_op jit(solution)/shard_map/all_to_all | solution.py:392
  44.2 20.1 %collective-permute-start.1 = (bf16[128,2048]{1,0:T(8,128)(2,1)S(1)}, bf16[128,2048]{1,0:T(8,128)(2,1)S(1)}, u32[]{:S(2)}, u32[]{:S(2)}) collective-permute-start(bf16[128,2048]{1,0:T(8,128)(2,1)S(1)} %copy-done), channel_id=1, source_target_pairs={{0,1},{1,0},{2,3},{3,2},{4,5},{5,4},{6,7},{7,6},{8,9},{9,8},{10,11... | collective-permute-start | bytes 1572872 | tf_op jit(solution)/shard_map/ppermute | solution.py:379
  53.1 24.5 %collective-permute-start.3 = (bf16[128,2048]{1,0:T(8,128)(2,1)S(1)}, bf16[128,2048]{1,0:T(8,128)(2,1)S(1)}, u32[]{:S(2)}, u32[]{:S(2)}) collective-permute-start(bf16[128,2048]{1,0:T(8,128)(2,1)S(1)} %collective-permute-done.2.w2_ref), channel_id=1, source_target_pairs={{0,1},{1,0},{2,3},{3,2},{4,5},{5,4},{6,7},{7,6},{8,9},{9,8},{10,11... | collective-permute-start | bytes 1572872 | tf_op jit(solution)/shard_map/ppermute | solution.py:381
  57.9 19.7 %all-to-all-start.2 = ((bf16[4,128,128]{2,1,0:T(8,128)(2,1)}), bf16[4,128,128]{2,1,0:T(8,128)(2,1)S(1)}, u32[]{:S(2)}, u32[]{:S(2)}) async-start(bf16[4,128,128]{2,1,0:T(8,128)(2,1)} %gated_norm.1), calls=%async_computation.2 | async-start | bytes 262144 | tf_op jit(solution)/shard_map/all_to_all | solution.py:406
  78.8 3.4 %collective-permute-start.4 = (bf16[64,2048]{1,0:T(8,128)(2,1)S(1)}, bf16[64,2048]{1,0:T(8,128)(2,1)S(1)}, u32[]{:S(2)}, u32[]{:S(2)}) collective-permute-start(bf16[64,2048]{1,0:T(8,128)(2,1)S(1)} %get-tuple-element.24), channel_id=1, source_target_pairs={{0,16},{16,0},{32,48},{48,32},{64,80},{80,64},{96,112},{112,96},{1... | collective-permute-start | bytes 786440 | tf_op jit(solution)/shard_map/ppermute | solution.py:419

commit v3 on v2

--- a/solution.py
+++ b/solution.py
@@ -73,7 +73,6 @@
 
 
 def map_kernel(
-    place_ref,
     k_far,
     v_far,
     rate_far,
@@ -89,7 +88,7 @@
     sems,
 ):
     rows = half_ref.shape[0]
-    begin = pl.multiple_of(place_ref[2] * rows, rows)
+    begin = pl.multiple_of(places()[2] * rows, rows)
     copies = [
         pltpu.make_async_copy(k_far, k_ref, sems.at[0]),
         pltpu.make_async_copy(decay_far, decay_ref, sems.at[1]),
@@ -174,9 +173,9 @@
 
 
 def read_kernel(
-    place_ref, q_ref, k_ref, decay_ref, gate_ref, gain_ref, solved_ref, keep_ref, send_ref
+    q_ref, k_ref, decay_ref, gate_ref, gain_ref, solved_ref, keep_ref, send_ref
 ):
-    core = place_ref[2]
+    core = places()[2]
     queries = q_ref[...]
     keys = k_ref[...]
     row, col = grid_iota(TOK, TOK)
@@ -205,8 +204,8 @@
     return jnp.concatenate([moved[:, :DK], moved[:, DK:] + later_h], axis=1)
 
 
-def row_kernel(place_ref, parts_ref, total_ref, ahead_ref, first_ref):
-    x = place_ref[1]
+def row_kernel(parts_ref, total_ref, ahead_ref, first_ref):
+    x = places()[1]
 
     def pair(i):
         later = parts_ref[2 * i + 1]
@@ -235,9 +234,8 @@
     return 4 * group + (label if group < 2 else 3 - label)
 
 
-def out_kernel(place_ref, rows_ref, ahead_ref, first_ref, keep_ref, came_ref, out_ref):
-    y = place_ref[0]
-    core = place_ref[2]
+def out_kernel(rows_ref, ahead_ref, first_ref, keep_ref, came_ref, out_ref):
+    y, _, core = places()
 
     def onward(later, state):
         return dot_right(later[:, :DK], state) + later[:, DK:].astype(F32)
@@ -269,11 +267,13 @@
                 out_ref[label, target : target + 16] = shards[shard][source : source + 16]
 
 
-def project_kernel(place_ref, normed_ref, w0_ref, w1_ref, w2_ref, w3_ref, keep_ref, send_ref):
-    core = place_ref[2]
+def project_kernel(normed_ref, w0_ref, w1_ref, w2_ref, w3_ref, keep_ref, send_ref):
+    core = places()[2]
+    along = lax.axis_index("tp")
     total = None
     for i, weight_ref in enumerate((w0_ref, w1_ref, w2_ref, w3_ref)):
-        term = dot(normed_ref[place_ref[4 + i]], weight_ref[...])
+        near = (along % 4) ^ i
+        term = dot(normed_ref[jnp.where(along < 8, near, 3 - near)], weight_ref[...])
         total = term if total is None else total + term
     keep_ref[...] = jnp.where(core == 0, total[:64], total[64:])
     send_ref[...] = jnp.where(core == 0, total[64:], total[:64]).astype(BF)
@@ -292,6 +292,11 @@
     out_ref[...] = total.astype(BF)
 
 
+def places():
+    at = lax.axis_index("ctx")
+    return at // 8, (at // 2) % 4, at % 2
+
+
 def in_vmem():
     return pl.BlockSpec(memory_space=pltpu.VMEM)
 
@@ -300,13 +305,13 @@
     return pl.BlockSpec(memory_space=pltpu.HBM)
 
 
-def call(kernel, outs, *args, scalars=0, flops=10**8, name=None, ins=None, out_specs=None, scratch=(), room=32):
+def call(kernel, outs, *args, flops=10**8, name=None, ins=None, out_specs=None, scratch=(), room=32):
     if ins is None:
-        ins = [in_vmem()] * (len(args) - scalars)
+        ins = [in_vmem()] * len(args)
     return pl.pallas_call(
         kernel,
         out_shape=outs,
-        in_specs=[pl.BlockSpec(memory_space=pltpu.SMEM)] * scalars + ins,
+        in_specs=ins,
         out_specs=jax.tree.map(lambda _: in_vmem(), outs) if out_specs is None else out_specs,
         scratch_shapes=scratch,
         compiler_params=pltpu.CompilerParams(vmem_limit_bytes=room * 1024 * 1024),
@@ -322,11 +327,6 @@
 def local(
     queries, key_vectors, value_vectors, output_gate, write_rate, log_decay, norm_gain, out_weight
 ):
-    at = lax.axis_index("ctx")
-    along = lax.axis_index("tp")
-    near = along % 4
-    label = [jnp.where(along < 8, near ^ i, 3 - (near ^ i)) for i in range(4)]
-    place = jnp.stack([at // 8, (at // 2) % 4, at % 2, along] + label).astype(jnp.int32)
     width = out_weight.shape[1]
     rate, decay = write_rate.T, log_decay.T
 
@@ -337,15 +337,13 @@
             shape((2, TOK, DK + DV), F32),
             shape((DV, width), BF),
         ),
-        place,
         key_vectors,
         value_vectors,
         rate,
         decay,
         out_weight,
-        scalars=1,
         ins=[in_hbm()] * 5,
-        out_specs=(in_vmem(), in_vmem(), in_hbm()),
+        out_specs=(in_vmem(), in_vmem(), in_vmem()),
         scratch=[
             pltpu.VMEM((TOK, DK), BF),
             pltpu.VMEM((TOK, 2 * DV), BF),
@@ -362,14 +360,12 @@
     keep, send = call(
         read_kernel,
         (shape((3, TOK, DV), F32), shape((3, TOK, DV), BF)),
-        place,
         queries,
         key_vectors,
         decay,
         output_gate,
         norm_gain.reshape(1, DV),
         solved,
-        scalars=1,
         flops=10**9,
         name="read_parts",
     )
@@ -378,14 +374,13 @@
 
     w1 = lax.ppermute(w0, "tp", [(j, j ^ 1) for j in range(16)])
     w2 = lax.ppermute(w0, "tp", [(j, j ^ 2) for j in range(16)])
+    w1, w2 = lax.optimization_barrier((w1, w2))
     w3 = lax.ppermute(w2, "tp", [(j, j ^ 1) for j in range(16)])
 
     total, ahead, first = call(
         row_kernel,
         (shape((4, DK, DK + DV), BF), shape((DK, DK + DV), F32), shape((DK, DK + DV), BF)),
-        place,
         parts,
-        scalars=1,
         name="row_maps",
     )
     columns = [[8 * y + i for y in range(4)] for i in range(8)]
@@ -393,13 +388,11 @@
     normed = call(
         out_kernel,
         shape((4, 128, DV), BF),
-        place,
         rows,
         ahead,
         first,
         keep,
         came,
-        scalars=1,
         name="gated_norm",
     )
     close = [[token_of(g, m) for m in range(4)] for g in range(4)]
@@ -407,13 +400,11 @@
     half, other_half = call(
         project_kernel,
         (shape((64, width), F32), shape((64, width), BF)),
-        place,
         gathered,
         w0,
         w1,
         w2,
         w3,
-        scalars=1,
         name="project",
     )
     other_half = lax.ppermute(other_half, "ctx", across)

time: 115 us -> 96.1 us (0.84)
  Pallas kernels: 26.7 us -> 10.4 us
  blocking collectives: 31.6 us -> 45.3 us
  waiting for transfers between devices: 23.5 us -> 14.1 us
  starting transfers between devices: 30.2 us -> 23.9 us
    pallas_call x7, Pallas kernels: 26.7 us -> 10.4 us  [call(): pl.pallas_call(kernel, out_shape=outs, in_specs=ins, out_specs=jax.tree.m...]
    all_to_all x0 -> x1, blocking collectives: none -> 14.8 us  [local(): gathered = lax.all_to_all(normed, 'tp', 0, 0, axis_index_groups=close)]
    all_to_all x1 -> x0, waiting for transfers between devices: 13.2 us -> none  [local(): gathered = lax.all_to_all(normed, 'tp', 0, 0, axis_index_groups=close)]
    all_to_all x1 -> x0, starting transfers between devices: 4.69 us -> none  [local(): gathered = lax.all_to_all(normed, 'tp', 0, 0, axis_index_groups=close)]
    ppermute x1, waiting for transfers between devices: 1.76 us -> 5.46 us  [local(): w1 = lax.ppermute(w0, 'tp', [(j, j ^ 1) for j in range(16)])]
    all_to_all x1, starting transfers between devices: 7.28 us -> 4.68 us  [local(): rows = lax.all_to_all(total, 'ctx', 0, 0, axis_index_groups=columns)]
    ppermute x1, starting transfers between devices: 1.91 us -> 3.82 us  [local(): w1 = lax.ppermute(w0, 'tp', [(j, j ^ 1) for j in range(16)])]
  transfers between devices with their start and end apart: 8 -> 7, of which waited for: 4 -> 3; matrix products, arithmetic and copies ran while one was open for 0% -> 0% of each run, Pallas kernels for 5% -> 4%
where the time goes in v3:
time: 96.1 us; the launch traced here: 95.5 us
  blocking collectives  45.3 us (47%)
  starting transfers between devices  23.9 us (25%)
  waiting for transfers between devices  14.1 us (15%)
  Pallas kernels  10.4 us (11%)
  local copies, waits for them, and re-layouts  1.68 us (2%)
    all_to_all x1, blocking collectives, local(): shares = lax.all_to_all(partial, 'tp', 0, 0, axis_index_groups=far)  30.5 us
    all_to_all x1, blocking collectives, local(): gathered = lax.all_to_all(normed, 'tp', 0, 0, axis_index_groups=close)  14.8 us
    pallas_call x7, Pallas kernels, call(): pl.pallas_call(kernel, out_shape=outs, in_specs=ins, out_specs=jax.tree.m...  10.4 us
    ppermute x1, waiting for transfers between devices, local(): w2 = lax.ppermute(w0, 'tp', [(j, j ^ 2) for j in range(16)])  7.1 us
    ppermute x1, waiting for transfers between devices, local(): w1 = lax.ppermute(w0, 'tp', [(j, j ^ 1) for j in range(16)])  5.46 us
    ppermute x1, starting transfers between devices, local(): w2 = lax.ppermute(w0, 'tp', [(j, j ^ 2) for j in range(16)])  5.18 us
    all_to_all x1, starting transfers between devices, local(): rows = lax.all_to_all(total, 'ctx', 0, 0, axis_index_groups=columns)  4.68 us
    all_to_all x1, starting transfers between devices, local(): parts = lax.all_to_all(maps, 'ctx', 0, 0, axis_index_groups=lines)  4.45 us
  transfers between devices with their start and end apart: 7, of which 3 were waited for; matrix products, arithmetic and copies ran while one was open for 0% of the time, Pallas kernels for 4%

profile of v3, /device:TPU:24, one launch (start us, length us, event | category | flops | bytes accessed | tf_op | source)
XLA Modules:
  0.0 95.5 jit_solution(13106951229999752278)
XLA Ops:
  0.0 5.2 %shard_maps.1 = (bf16[8,128,256]{2,1,0:T(8,128)(2,1)}, f32[2,256,256]{2,1,0:T(8,128)}, bf16[128,2048]{1,0:T(8,128)(2,1)}) custom-call(bf16[256,128]{1,0:T(8,128)(2,1)} %k_ref.1, bf16[256,256]{1,0:T(8,128)(2,1)} %v_far.1, f32[2,256]{1,0:T(2,128)} %bitcast.6, f32[2,256]{1,0:T(2,128)} %bitcast.3, bf16[256,2048]{1,0:T(8,128)(2,1)} %weight_far.1), custom_call_target="tpu_custom_call" | custom-call | flops 1000000000 | bytes 1000000 | tf_op jit(solution)/shard_map/shard_maps/pallas_call | solution.py:311
  5.3 0.0 copy-start
  5.3 0.0 copy-start.1
  5.3 0.0 copy-start.2
  5.3 0.0 copy-start.3
  5.3 4.5 %all-to-all-start = ((bf16[8,128,256]{2,1,0:T(8,128)(2,1)}), bf16[8,128,256]{2,1,0:T(8,128)(2,1)S(1)}, u32[]{:S(2)}, u32[]{:S(2)}) async-start(bf16[8,128,256]{2,1,0:T(8,128)(2,1)} %get-tuple-element.17), calls=%async_computation | async-start | bytes 1048576 | tf_op jit(solution)/shard_map/all_to_all | solution.py:359
  9.8 0.0 copy-done
  9.8 0.0 copy-start.4
  9.8 3.8 %collective-permute-start.1 = (bf16[128,2048]{1,0:T(8,128)(2,1)S(1)}, bf16[128,2048]{1,0:T(8,128)(2,1)S(1)}, u32[]{:S(2)}, u32[]{:S(2)}) collective-permute-start(bf16[128,2048]{1,0:T(8,128)(2,1)S(1)} %copy-done), channel_id=1, source_target_pairs={{0,1},{1,0},{2,3},{3,2},{4,5},{5,4},{6,7},{7,6},{8,9},{9,8},{10,11... | collective-permute-start | bytes 1572872 | tf_op jit(solution)/shard_map/ppermute | solution.py:375
  13.6 5.2 %collective-permute-start.2 = (bf16[128,2048]{1,0:T(8,128)(2,1)S(1)}, bf16[128,2048]{1,0:T(8,128)(2,1)S(1)}, u32[]{:S(2)}, u32[]{:S(2)}) collective-permute-start(bf16[128,2048]{1,0:T(8,128)(2,1)S(1)} %copy-done), channel_id=1, source_target_pairs={{0,2},{1,3},{2,0},{3,1},{4,6},{5,7},{6,4},{7,5},{8,10},{9,11},{10,... | collective-permute-start | bytes 1572872 | tf_op jit(solution)/shard_map/ppermute | solution.py:376
  18.8 0.0 copy-start.5
  18.8 0.0 copy-done.1
  18.8 0.0 copy-done.2
  18.8 0.0 copy-done.3
  18.8 0.0 copy-done.4
  18.8 0.6 copy-done.5
  19.4 0.0 copy-start.6
  19.4 1.0 %copy-done.6 = f32[2,256,256]{2,1,0:T(8,128)S(1)} copy-done((f32[2,256,256]{2,1,0:T(8,128)S(1)}, f32[2,256,256]{2,1,0:T(8,128)}, u32[]{:S(2)}) %copy-start.6) | copy-done | bytes 524312
  20.5 1.4 %read_parts.1 = (f32[3,256,128]{2,1,0:T(8,128)S(1)}, bf16[3,256,128]{2,1,0:T(8,128)(2,1)}) custom-call(bf16[256,128]{1,0:T(8,128)(2,1)S(1)} %copy-done.3, bf16[256,128]{1,0:T(8,128)(2,1)S(1)} %copy-done.2, f32[2,256]{1,0:T(2,128)S(1)} %bitcast.4, bf16[256,256]{1,0:T(8,128)(2,1)S(1)} %copy-done.1, f32[1,128]{1,0:T(1,128)S(1)} %bitcast.5, ...), custom_call_target="tpu_custom_call" | custom-call | flops 1000000000 | bytes 1000000 | tf_op jit(solution)/shard_map/read_parts/pallas_call | solution.py:311
  21.9 2.0 %collective-permute-start = (bf16[3,256,128]{2,1,0:T(8,128)(2,1)}, bf16[3,256,128]{2,1,0:T(8,128)(2,1)S(1)}, u32[]{:S(2)}, u32[]{:S(2)}) collective-permute-start(bf16[3,256,128]{2,1,0:T(8,128)(2,1)} %get-tuple-element.23), channel_id=1, source_target_pairs={{0,16},{16,0},{32,48},{48,32},{64,80},{80,64},{96,112},{112,96},{1... | collective-permute-start | bytes 589832 | tf_op jit(solution)/shard_map/ppermute | solution.py:373
  23.9 0.0 all-to-all-done.parts_ref
  23.9 1.3 %row_maps.1 = (bf16[4,128,256]{2,1,0:T(8,128)(2,1)}, f32[128,256]{1,0:T(8,128)S(1)}, bf16[128,256]{1,0:T(8,128)(2,1)S(1)}) custom-call(bf16[8,128,256]{2,1,0:T(8,128)(2,1)S(1)} %all-to-all-done.parts_ref), custom_call_target="tpu_custom_call" | custom-call | flops 100000000 | bytes 1000000 | tf_op jit(solution)/shard_map/row_maps/pallas_call | solution.py:311
  25.2 4.7 %all-to-all-start.1 = ((bf16[4,128,256]{2,1,0:T(8,128)(2,1)}), bf16[4,128,256]{2,1,0:T(8,128)(2,1)S(1)}, u32[]{:S(2)}, u32[]{:S(2)}) async-start(bf16[4,128,256]{2,1,0:T(8,128)(2,1)} %get-tuple-element.18), calls=%async_computation.1 | async-start | bytes 524288 | tf_op jit(solution)/shard_map/all_to_all | solution.py:387
  29.9 5.5 %collective-permute-done.1.w1_ref = bf16[128,2048]{1,0:T(8,128)(2,1)S(1)} collective-permute-done((bf16[128,2048]{1,0:T(8,128)(2,1)S(1)}, bf16[128,2048]{1,0:T(8,128)(2,1)S(1)}, u32[]{:S(2)}, u32[]{:S(2)}) %collective-permute-start.1) | collective-permute-done | bytes 524320 | tf_op jit(solution)/shard_map/ppermute | solution.py:375
  35.4 7.1 %collective-permute-done.2.w2_ref = bf16[128,2048]{1,0:T(8,128)(2,1)S(1)} collective-permute-done((bf16[128,2048]{1,0:T(8,128)(2,1)S(1)}, bf16[128,2048]{1,0:T(8,128)(2,1)S(1)}, u32[]{:S(2)}, u32[]{:S(2)}) %collective-permute-start.2) | collective-permute-done | bytes 524320 | tf_op jit(solution)/shard_map/ppermute | solution.py:376
  42.5 1.9 %collective-permute-start.3 = (bf16[128,2048]{1,0:T(8,128)(2,1)S(1)}, bf16[128,2048]{1,0:T(8,128)(2,1)S(1)}, u32[]{:S(2)}, u32[]{:S(2)}) collective-permute-start(bf16[128,2048]{1,0:T(8,128)(2,1)S(1)} %collective-permute-done.2.w2_ref), channel_id=1, source_target_pairs={{0,1},{1,0},{2,3},{3,2},{4,5},{5,4},{6,7},{7,6},{8,9},{9,8},{10,11... | collective-permute-start | bytes 1572872 | tf_op jit(solution)/shard_map/ppermute | solution.py:378
  44.4 0.0 collective-permute-done.came_ref
  44.4 0.0 all-to-all-done.1.rows_ref
  44.4 1.0 %gated_norm.1 = bf16[4,128,128]{2,1,0:T(8,128)(2,1)S(1)} custom-call(bf16[4,128,256]{2,1,0:T(8,128)(2,1)S(1)} %all-to-all-done.1.rows_ref, f32[128,256]{1,0:T(8,128)S(1)} %get-tuple-element.19.ahead_ref, bf16[128,256]{1,0:T(8,128)(2,1)S(1)} %get-tuple-element.20.first_ref, f32[3,256,128]{2,1,0:T(8,128)S(1)} %get-tuple-element.22.keep_ref, ...), custom_call_target="tpu_custom_call" | custom-call | flops 100000000 | bytes 1000000 | tf_op jit(solution)/shard_map/gated_norm/pallas_call | solution.py:311
  45.4 14.8 %all_to_all.20.normed_ref = bf16[4,128,128]{2,1,0:T(8,128)(2,1)S(1)} all-to-all(bf16[4,128,128]{2,1,0:T(8,128)(2,1)S(1)} %gated_norm.1), channel_id=1, replica_groups={{0,1,2,3},{4,5,6,7},{11,10,9,8},{15,14,13,12},{16,17,18,19},{20,21,22,2..., dimensions={0} | all-to-all | bytes 262144 | tf_op jit(solution)/shard_map/all_to_all | solution.py:399
  60.2 0.0 collective-permute-done.3.w3_ref
  60.2 0.7 project.1
  60.9 1.9 %collective-permute-start.4 = (bf16[64,2048]{1,0:T(8,128)(2,1)S(1)}, bf16[64,2048]{1,0:T(8,128)(2,1)S(1)}, u32[]{:S(2)}, u32[]{:S(2)}) collective-permute-start(bf16[64,2048]{1,0:T(8,128)(2,1)S(1)} %get-tuple-element.28), channel_id=1, source_target_pairs={{0,16},{16,0},{32,48},{48,32},{64,80},{80,64},{96,112},{112,96},{1... | collective-permute-start | bytes 786440 | tf_op jit(solution)/shard_map/ppermute | solution.py:410
  62.8 1.5 %collective-permute-done.4.came_ref = bf16[64,2048]{1,0:T(8,128)(2,1)S(1)} collective-permute-done((bf16[64,2048]{1,0:T(8,128)(2,1)S(1)}, bf16[64,2048]{1,0:T(8,128)(2,1)S(1)}, u32[]{:S(2)}, u32[]{:S(2)}) %collective-permute-start.4) | collective-permute-done | bytes 262176 | tf_op jit(solution)/shard_map/ppermute | solution.py:410
  64.3 30.5 %all_to_all.21.parts_ref = bf16[4,16,2048]{2,1,0:T(8,128)(2,1)S(1)} all-to-all(bf16[4,16,2048]{2,1,0:T(8,128)(2,1)S(1)} %join.1), channel_id=1, replica_groups={{0,4,11,15},{1,5,10,14},{2,6,9,13},{3,7,8,12},{16,20,27,31},{17,21,26,3..., dimensions={0} | all-to-all | bytes 524288 | tf_op jit(solution)/shard_map/all_to_all | solution.py:413
  94.8 0.7 sum_shares.1
  (1 shorter events, 0.0 us)
Async XLA Ops:
  5.3 4.5 %copy-start = (bf16[128,2048]{1,0:T(8,128)(2,1)S(1)}, bf16[128,2048]{1,0:T(8,128)(2,1)}, u32[]{:S(2)}) copy-start(bf16[128,2048]{1,0:T(8,128)(2,1)} %get-tuple-element.24.w0_ref) | copy-start | bytes 1572868
  5.3 13.5 %copy-start.1 = (bf16[256,256]{1,0:T(8,128)(2,1)S(1)}, bf16[256,256]{1,0:T(8,128)(2,1)}, u32[]{:S(2)}) copy-start(bf16[256,256]{1,0:T(8,128)(2,1)} %gate_ref.1) | copy-start | bytes 393220
  5.3 13.5 %copy-start.2 = (bf16[256,128]{1,0:T(8,128)(2,1)S(1)}, bf16[256,128]{1,0:T(8,128)(2,1)}, u32[]{:S(2)}) copy-start(bf16[256,128]{1,0:T(8,128)(2,1)} %k_ref.1) | copy-start | bytes 196612
  5.3 13.5 %copy-start.3 = (bf16[256,128]{1,0:T(8,128)(2,1)S(1)}, bf16[256,128]{1,0:T(8,128)(2,1)}, u32[]{:S(2)}) copy-start(bf16[256,128]{1,0:T(8,128)(2,1)} %q_ref.1) | copy-start | bytes 196612
  5.3 18.6 %all-to-all-start = ((bf16[8,128,256]{2,1,0:T(8,128)(2,1)}), bf16[8,128,256]{2,1,0:T(8,128)(2,1)S(1)}, u32[]{:S(2)}, u32[]{:S(2)}) async-start(bf16[8,128,256]{2,1,0:T(8,128)(2,1)} %get-tuple-element.17), calls=%async_computation | async-start | bytes 1048576 | tf_op jit(solution)/shard_map/all_to_all | solution.py:359
  9.8 9.1 %copy-start.4 = (f32[256,2]{0,1:T(2,128)S(1)}, f32[256,2]{0,1:T(2,128)}, u32[]{:S(2)}) copy-start(f32[256,2]{0,1:T(2,128)} %param.13) | copy-start | bytes 6148
  9.8 25.6 %collective-permute-start.1 = (bf16[128,2048]{1,0:T(8,128)(2,1)S(1)}, bf16[128,2048]{1,0:T(8,128)(2,1)S(1)}, u32[]{:S(2)}, u32[]{:S(2)}) collective-permute-start(bf16[128,2048]{1,0:T(8,128)(2,1)S(1)} %copy-done), channel_id=1, source_target_pairs={{0,1},{1,0},{2,3},{3,2},{4,5},{5,4},{6,7},{7,6},{8,9},{9,8},{10,11... | collective-permute-start | bytes 1572872 | tf_op jit(solution)/shard_map/ppermute | solution.py:375
  13.6 28.9 %collective-permute-start.2 = (bf16[128,2048]{1,0:T(8,128)(2,1)S(1)}, bf16[128,2048]{1,0:T(8,128)(2,1)S(1)}, u32[]{:S(2)}, u32[]{:S(2)}) collective-permute-start(bf16[128,2048]{1,0:T(8,128)(2,1)S(1)} %copy-done), channel_id=1, source_target_pairs={{0,2},{1,3},{2,0},{3,1},{4,6},{5,7},{6,4},{7,5},{8,10},{9,11},{10,... | collective-permute-start | bytes 1572872 | tf_op jit(solution)/shard_map/ppermute | solution.py:376
  18.8 0.7 copy-start.5
  19.4 1.0 %copy-start.6 = (f32[2,256,256]{2,1,0:T(8,128)S(1)}, f32[2,256,256]{2,1,0:T(8,128)}, u32[]{:S(2)}) copy-start(f32[2,256,256]{2,1,0:T(8,128)} %get-tuple-element.21.solved_ref) | copy-start | bytes 1572868
  21.9 22.5 %collective-permute-start = (bf16[3,256,128]{2,1,0:T(8,128)(2,1)}, bf16[3,256,128]{2,1,0:T(8,128)(2,1)S(1)}, u32[]{:S(2)}, u32[]{:S(2)}) collective-permute-start(bf16[3,256,128]{2,1,0:T(8,128)(2,1)} %get-tuple-element.23), channel_id=1, source_target_pairs={{0,16},{16,0},{32,48},{48,32},{64,80},{80,64},{96,112},{112,96},{1... | collective-permute-start | bytes 589832 | tf_op jit(solution)/shard_map/ppermute | solution.py:373
  25.2 19.2 %all-to-all-start.1 = ((bf16[4,128,256]{2,1,0:T(8,128)(2,1)}), bf16[4,128,256]{2,1,0:T(8,128)(2,1)S(1)}, u32[]{:S(2)}, u32[]{:S(2)}) async-start(bf16[4,128,256]{2,1,0:T(8,128)(2,1)} %get-tuple-element.18), calls=%async_computation.1 | async-start | bytes 524288 | tf_op jit(solution)/shard_map/all_to_all | solution.py:387
  42.5 17.7 %collective-permute-start.3 = (bf16[128,2048]{1,0:T(8,128)(2,1)S(1)}, bf16[128,2048]{1,0:T(8,128)(2,1)S(1)}, u32[]{:S(2)}, u32[]{:S(2)}) collective-permute-start(bf16[128,2048]{1,0:T(8,128)(2,1)S(1)} %collective-permute-done.2.w2_ref), channel_id=1, source_target_pairs={{0,1},{1,0},{2,3},{3,2},{4,5},{5,4},{6,7},{7,6},{8,9},{9,8},{10,11... | collective-permute-start | bytes 1572872 | tf_op jit(solution)/shard_map/ppermute | solution.py:378
  60.9 3.4 %collective-permute-start.4 = (bf16[64,2048]{1,0:T(8,128)(2,1)S(1)}, bf16[64,2048]{1,0:T(8,128)(2,1)S(1)}, u32[]{:S(2)}, u32[]{:S(2)}) collective-permute-start(bf16[64,2048]{1,0:T(8,128)(2,1)S(1)} %get-tuple-element.28), channel_id=1, source_target_pairs={{0,16},{16,0},{32,48},{48,32},{64,80},{80,64},{96,112},{112,96},{1... | collective-permute-start | bytes 786440 | tf_op jit(solution)/shard_map/ppermute | solution.py:410

commit v4 on v3

--- a/solution.py
+++ b/solution.py
@@ -374,8 +374,6 @@
 
     w1 = lax.ppermute(w0, "tp", [(j, j ^ 1) for j in range(16)])
     w2 = lax.ppermute(w0, "tp", [(j, j ^ 2) for j in range(16)])
-    w1, w2 = lax.optimization_barrier((w1, w2))
-    w3 = lax.ppermute(w2, "tp", [(j, j ^ 1) for j in range(16)])
 
     total, ahead, first = call(
         row_kernel,
@@ -395,6 +393,8 @@
         came,
         name="gated_norm",
     )
+    w2, normed = lax.optimization_barrier((w2, normed))
+    w3 = lax.ppermute(w2, "tp", [(j, j ^ 1) for j in range(16)])
     close = [[token_of(g, m) for m in range(4)] for g in range(4)]
     gathered = lax.all_to_all(normed, "tp", 0, 0, axis_index_groups=close)
     half, other_half = call(

time: 96.1 us -> 101 us (1.051)
  blocking collectives: 45.3 us -> 31.5 us
  waiting for transfers between devices: 14.1 us -> 25.1 us
  starting transfers between devices: 23.9 us -> 31.1 us
    all_to_all x1 -> x0, blocking collectives: 14.8 us -> none  [local(): gathered = lax.all_to_all(normed, 'tp', 0, 0, axis_index_groups=close)]
    all_to_all x0 -> x1, waiting for transfers between devices: none -> 12.9 us  [local(): gathered = lax.all_to_all(normed, 'tp', 0, 0, axis_index_groups=close)]
    all_to_all x0 -> x1, starting transfers between devices: none -> 4.7 us  [local(): gathered = lax.all_to_all(normed, 'tp', 0, 0, axis_index_groups=close)]
    ppermute x1, waiting for transfers between devices: 7.1 us -> 3.15 us  [local(): w2 = lax.ppermute(w0, 'tp', [(j, j ^ 2) for j in range(16)])]
    all_to_all x1, starting transfers between devices: 4.68 us -> 8.08 us  [local(): rows = lax.all_to_all(total, 'ctx', 0, 0, axis_index_groups=columns)]
    all_to_all x1, waiting for transfers between devices: 0.01 us -> 2.75 us  [local(): rows = lax.all_to_all(total, 'ctx', 0, 0, axis_index_groups=columns)]
    ppermute x1, starting transfers between devices: 3.82 us -> 1.91 us  [local(): w1 = lax.ppermute(w0, 'tp', [(j, j ^ 1) for j in range(16)])]
    ppermute x1, waiting for transfers between devices: 5.46 us -> 4.29 us  [local(): w1 = lax.ppermute(w0, 'tp', [(j, j ^ 1) for j in range(16)])]
  transfers between devices with their start and end apart: 7 -> 8, of which waited for: 3 -> 6; matrix products, arithmetic and copies ran while one was open for 0% -> 0% of each run, Pallas kernels for 4% -> 4%
where the time goes in v4:
time: 101 us; the launch traced here: 99.9 us
  blocking collectives  31.5 us (31%)
  starting transfers between devices  31.1 us (31%)
  waiting for transfers between devices  25.1 us (25%)
  Pallas kernels  10.3 us (10%)
  local copies, waits for them, and re-layouts  1.68 us (2%)
    all_to_all x1, blocking collectives, local(): shares = lax.all_to_all(partial, 'tp', 0, 0, axis_index_groups=far)  31.5 us
    all_to_all x1, waiting for transfers between devices, local(): gathered = lax.all_to_all(normed, 'tp', 0, 0, axis_index_groups=close)  12.9 us
    pallas_call x7, Pallas kernels, call(): pl.pallas_call(kernel, out_shape=outs, in_specs=ins, out_specs=jax.tree.m...  10.3 us
    all_to_all x1, starting transfers between devices, local(): rows = lax.all_to_all(total, 'ctx', 0, 0, axis_index_groups=columns)  8.08 us
    ppermute x1, starting transfers between devices, local(): w2 = lax.ppermute(w0, 'tp', [(j, j ^ 2) for j in range(16)])  5.17 us
    all_to_all x1, starting transfers between devices, local(): gathered = lax.all_to_all(normed, 'tp', 0, 0, axis_index_groups=close)  4.7 us
    all_to_all x1, starting transfers between devices, local(): parts = lax.all_to_all(maps, 'ctx', 0, 0, axis_index_groups=lines)  4.45 us
    ppermute x1, waiting for transfers between devices, local(): w1 = lax.ppermute(w0, 'tp', [(j, j ^ 1) for j in range(16)])  4.29 us
  transfers between devices with their start and end apart: 8, of which 6 were waited for; matrix products, arithmetic and copies ran while one was open for 0% of the time, Pallas kernels for 4%

profile of v4, /device:TPU:24, one launch (start us, length us, event | category | flops | bytes accessed | tf_op | source)
XLA Modules:
  0.0 99.9 jit_solution(18041987735636306387)
XLA Ops:
  0.0 5.3 %shard_maps.1 = (bf16[8,128,256]{2,1,0:T(8,128)(2,1)}, f32[2,256,256]{2,1,0:T(8,128)}, bf16[128,2048]{1,0:T(8,128)(2,1)}) custom-call(bf16[256,128]{1,0:T(8,128)(2,1)} %k_ref.1, bf16[256,256]{1,0:T(8,128)(2,1)} %v_far.1, f32[2,256]{1,0:T(2,128)} %bitcast.6, f32[2,256]{1,0:T(2,128)} %bitcast.3, bf16[256,2048]{1,0:T(8,128)(2,1)} %weight_far.1), custom_call_target="tpu_custom_call" | custom-call | flops 1000000000 | bytes 1000000 | tf_op jit(solution)/shard_map/shard_maps/pallas_call | solution.py:311
  5.3 0.0 copy-start
  5.3 0.0 copy-start.1
  5.3 0.0 copy-start.2
  5.3 0.0 copy-start.3
  5.3 4.5 %all-to-all-start = ((bf16[8,128,256]{2,1,0:T(8,128)(2,1)}), bf16[8,128,256]{2,1,0:T(8,128)(2,1)S(1)}, u32[]{:S(2)}, u32[]{:S(2)}) async-start(bf16[8,128,256]{2,1,0:T(8,128)(2,1)} %get-tuple-element.18), calls=%async_computation | async-start | bytes 1048576 | tf_op jit(solution)/shard_map/all_to_all | solution.py:359
  9.8 0.0 copy-done
  9.8 0.0 copy-start.4
  9.8 5.2 %collective-permute-start = (bf16[128,2048]{1,0:T(8,128)(2,1)S(1)}, bf16[128,2048]{1,0:T(8,128)(2,1)S(1)}, u32[]{:S(2)}, u32[]{:S(2)}) collective-permute-start(bf16[128,2048]{1,0:T(8,128)(2,1)S(1)} %copy-done), channel_id=1, source_target_pairs={{0,2},{1,3},{2,0},{3,1},{4,6},{5,7},{6,4},{7,5},{8,10},{9,11},{10,... | collective-permute-start | bytes 1572872 | tf_op jit(solution)/shard_map/ppermute | solution.py:376
  15.0 0.0 copy-start.5
  15.0 0.0 copy-done.1
  15.0 0.0 copy-done.2
  15.0 0.0 copy-done.3
  15.0 0.0 copy-done.4
  15.0 0.6 copy-done.5
  15.6 0.0 copy-start.6
  15.6 1.0 %copy-done.6 = f32[2,256,256]{2,1,0:T(8,128)S(1)} copy-done((f32[2,256,256]{2,1,0:T(8,128)S(1)}, f32[2,256,256]{2,1,0:T(8,128)}, u32[]{:S(2)}) %copy-start.6) | copy-done | bytes 524312
  16.7 0.7 read_parts.1
  17.4 2.2 %collective-permute-start.1 = (bf16[3,256,128]{2,1,0:T(8,128)(2,1)S(1)}, bf16[3,256,128]{2,1,0:T(8,128)(2,1)S(1)}, u32[]{:S(2)}, u32[]{:S(2)}) collective-permute-start(bf16[3,256,128]{2,1,0:T(8,128)(2,1)S(1)} %get-tuple-element.24), channel_id=1, source_target_pairs={{0,16},{16,0},{32,48},{48,32},{64,80},{80,64},{96,112},{112,96},{1... | collective-permute-start | bytes 589832 | tf_op jit(solution)/shard_map/ppermute | solution.py:373
  19.6 0.5 all-to-all-done.parts_ref
  20.1 1.3 %row_maps.1 = (bf16[4,128,256]{2,1,0:T(8,128)(2,1)}, f32[128,256]{1,0:T(8,128)S(1)}, bf16[128,256]{1,0:T(8,128)(2,1)S(1)}) custom-call(bf16[8,128,256]{2,1,0:T(8,128)(2,1)S(1)} %all-to-all-done.parts_ref), custom_call_target="tpu_custom_call" | custom-call | flops 100000000 | bytes 1000000 | tf_op jit(solution)/shard_map/row_maps/pallas_call | solution.py:311
  21.5 8.1 %all-to-all-start.1 = ((bf16[4,128,256]{2,1,0:T(8,128)(2,1)}), bf16[4,128,256]{2,1,0:T(8,128)(2,1)S(1)}, u32[]{:S(2)}, u32[]{:S(2)}) async-start(bf16[4,128,256]{2,1,0:T(8,128)(2,1)} %get-tuple-element.19), calls=%async_computation.1 | async-start | bytes 524288 | tf_op jit(solution)/shard_map/all_to_all | solution.py:385
  29.5 1.9 %collective-permute-start.2 = (bf16[128,2048]{1,0:T(8,128)(2,1)S(1)}, bf16[128,2048]{1,0:T(8,128)(2,1)S(1)}, u32[]{:S(2)}, u32[]{:S(2)}) collective-permute-start(bf16[128,2048]{1,0:T(8,128)(2,1)S(1)} %copy-done), channel_id=1, source_target_pairs={{0,1},{1,0},{2,3},{3,2},{4,5},{5,4},{6,7},{7,6},{8,9},{9,8},{10,11... | collective-permute-start | bytes 1572872 | tf_op jit(solution)/shard_map/ppermute | solution.py:375
  31.5 0.0 collective-permute-done.1.came_ref
  31.5 2.8 %all-to-all-done.1.rows_ref = bf16[4,128,256]{2,1,0:T(8,128)(2,1)S(1)} async-done(((bf16[4,128,256]{2,1,0:T(8,128)(2,1)}), bf16[4,128,256]{2,1,0:T(8,128)(2,1)S(1)}, u32[]{:S(2)}, u32[]{:S(2)}) %all-to-all-start.1) | async-done | bytes 262176 | tf_op jit(solution)/shard_map/all_to_all | solution.py:385
  34.2 1.6 %gated_norm.1 = bf16[4,128,128]{2,1,0:T(8,128)(2,1)} custom-call(bf16[4,128,256]{2,1,0:T(8,128)(2,1)S(1)} %all-to-all-done.1.rows_ref, f32[128,256]{1,0:T(8,128)S(1)} %get-tuple-element.20.ahead_ref, bf16[128,256]{1,0:T(8,128)(2,1)S(1)} %get-tuple-element.21.first_ref, f32[3,256,128]{2,1,0:T(8,128)S(1)} %get-tuple-element.23.keep_ref, ...), custom_call_target="tpu_custom_call" | custom-call | flops 100000000 | bytes 1000000 | tf_op jit(solution)/shard_map/gated_norm/pallas_call | solution.py:311
  35.8 3.2 %collective-permute-done.w2_ref = bf16[128,2048]{1,0:T(8,128)(2,1)S(1)} collective-permute-done((bf16[128,2048]{1,0:T(8,128)(2,1)S(1)}, bf16[128,2048]{1,0:T(8,128)(2,1)S(1)}, u32[]{:S(2)}, u32[]{:S(2)}) %collective-permute-start) | collective-permute-done | bytes 524320 | tf_op jit(solution)/shard_map/ppermute | solution.py:376
  39.0 2.6 %collective-permute-start.3 = (bf16[128,2048]{1,0:T(8,128)(2,1)S(1)}, bf16[128,2048]{1,0:T(8,128)(2,1)S(1)}, u32[]{:S(2)}, u32[]{:S(2)}) collective-permute-start(bf16[128,2048]{1,0:T(8,128)(2,1)S(1)} %collective-permute-done.w2_ref), channel_id=1, source_target_pairs={{0,1},{1,0},{2,3},{3,2},{4,5},{5,4},{6,7},{7,6},{8,9},{9,8},{10,11... | collective-permute-start | bytes 1572872 | tf_op jit(solution)/shard_map/ppermute | solution.py:397
  41.6 4.7 %all-to-all-start.2 = ((bf16[4,128,128]{2,1,0:T(8,128)(2,1)}), bf16[4,128,128]{2,1,0:T(8,128)(2,1)S(1)}, u32[]{:S(2)}, u32[]{:S(2)}) async-start(bf16[4,128,128]{2,1,0:T(8,128)(2,1)} %gated_norm.1), calls=%async_computation.2 | async-start | bytes 262144 | tf_op jit(solution)/shard_map/all_to_all | solution.py:399
  46.3 4.3 %collective-permute-done.2.w1_ref = bf16[128,2048]{1,0:T(8,128)(2,1)S(1)} collective-permute-done((bf16[128,2048]{1,0:T(8,128)(2,1)S(1)}, bf16[128,2048]{1,0:T(8,128)(2,1)S(1)}, u32[]{:S(2)}, u32[]{:S(2)}) %collective-permute-start.2) | collective-permute-done | bytes 524320 | tf_op jit(solution)/shard_map/ppermute | solution.py:375
  50.6 12.9 %all-to-all-done.2.normed_ref = bf16[4,128,128]{2,1,0:T(8,128)(2,1)S(1)} async-done(((bf16[4,128,128]{2,1,0:T(8,128)(2,1)}), bf16[4,128,128]{2,1,0:T(8,128)(2,1)S(1)}, u32[]{:S(2)}, u32[]{:S(2)}) %all-to-all-start.2) | async-done | bytes 131104 | tf_op jit(solution)/shard_map/all_to_all | solution.py:399
  63.5 0.0 collective-permute-done.3.w3_ref
  63.5 0.7 project.1
  64.2 1.9 %collective-permute-start.4 = (bf16[64,2048]{1,0:T(8,128)(2,1)S(1)}, bf16[64,2048]{1,0:T(8,128)(2,1)S(1)}, u32[]{:S(2)}, u32[]{:S(2)}) collective-permute-start(bf16[64,2048]{1,0:T(8,128)(2,1)S(1)} %get-tuple-element.28), channel_id=1, source_target_pairs={{0,16},{16,0},{32,48},{48,32},{64,80},{80,64},{96,112},{112,96},{1... | collective-permute-start | bytes 786440 | tf_op jit(solution)/shard_map/ppermute | solution.py:410
  66.1 1.5 %collective-permute-done.4.came_ref = bf16[64,2048]{1,0:T(8,128)(2,1)S(1)} collective-permute-done((bf16[64,2048]{1,0:T(8,128)(2,1)S(1)}, bf16[64,2048]{1,0:T(8,128)(2,1)S(1)}, u32[]{:S(2)}, u32[]{:S(2)}) %collective-permute-start.4) | collective-permute-done | bytes 262176 | tf_op jit(solution)/shard_map/ppermute | solution.py:410
  67.7 31.5 %all_to_all.20.parts_ref = bf16[4,16,2048]{2,1,0:T(8,128)(2,1)S(1)} all-to-all(bf16[4,16,2048]{2,1,0:T(8,128)(2,1)S(1)} %join.1), channel_id=1, replica_groups={{0,4,11,15},{1,5,10,14},{2,6,9,13},{3,7,8,12},{16,20,27,31},{17,21,26,3..., dimensions={0} | all-to-all | bytes 524288 | tf_op jit(solution)/shard_map/all_to_all | solution.py:413
  99.2 0.7 sum_shares.1
  (1 shorter events, 0.0 us)
Async XLA Ops:
  5.3 4.5 %copy-start = (bf16[128,2048]{1,0:T(8,128)(2,1)S(1)}, bf16[128,2048]{1,0:T(8,128)(2,1)}, u32[]{:S(2)}) copy-start(bf16[128,2048]{1,0:T(8,128)(2,1)} %get-tuple-element.17.w0_ref) | copy-start | bytes 1572868
  5.3 9.7 %copy-start.1 = (bf16[256,256]{1,0:T(8,128)(2,1)S(1)}, bf16[256,256]{1,0:T(8,128)(2,1)}, u32[]{:S(2)}) copy-start(bf16[256,256]{1,0:T(8,128)(2,1)} %gate_ref.1) | copy-start | bytes 393220
  5.3 9.7 %copy-start.2 = (bf16[256,128]{1,0:T(8,128)(2,1)S(1)}, bf16[256,128]{1,0:T(8,128)(2,1)}, u32[]{:S(2)}) copy-start(bf16[256,128]{1,0:T(8,128)(2,1)} %k_ref.1) | copy-start | bytes 196612
  5.3 9.7 %copy-start.3 = (bf16[256,128]{1,0:T(8,128)(2,1)S(1)}, bf16[256,128]{1,0:T(8,128)(2,1)}, u32[]{:S(2)}) copy-start(bf16[256,128]{1,0:T(8,128)(2,1)} %q_ref.1) | copy-start | bytes 196612
  5.3 14.8 %all-to-all-start = ((bf16[8,128,256]{2,1,0:T(8,128)(2,1)}), bf16[8,128,256]{2,1,0:T(8,128)(2,1)S(1)}, u32[]{:S(2)}, u32[]{:S(2)}) async-start(bf16[8,128,256]{2,1,0:T(8,128)(2,1)} %get-tuple-element.18), calls=%async_computation | async-start | bytes 1048576 | tf_op jit(solution)/shard_map/all_to_all | solution.py:359
  9.8 5.2 %copy-start.4 = (f32[256,2]{0,1:T(2,128)S(1)}, f32[256,2]{0,1:T(2,128)}, u32[]{:S(2)}) copy-start(f32[256,2]{0,1:T(2,128)} %param.13) | copy-start | bytes 6148
  9.8 29.2 %collective-permute-start = (bf16[128,2048]{1,0:T(8,128)(2,1)S(1)}, bf16[128,2048]{1,0:T(8,128)(2,1)S(1)}, u32[]{:S(2)}, u32[]{:S(2)}) collective-permute-start(bf16[128,2048]{1,0:T(8,128)(2,1)S(1)} %copy-done), channel_id=1, source_target_pairs={{0,2},{1,3},{2,0},{3,1},{4,6},{5,7},{6,4},{7,5},{8,10},{9,11},{10,... | collective-permute-start | bytes 1572872 | tf_op jit(solution)/shard_map/ppermute | solution.py:376
  15.0 0.7 copy-start.5
  15.6 1.0 %copy-start.6 = (f32[2,256,256]{2,1,0:T(8,128)S(1)}, f32[2,256,256]{2,1,0:T(8,128)}, u32[]{:S(2)}) copy-start(f32[2,256,256]{2,1,0:T(8,128)} %get-tuple-element.22.solved_ref) | copy-start | bytes 1572868
  17.4 14.1 %collective-permute-start.1 = (bf16[3,256,128]{2,1,0:T(8,128)(2,1)S(1)}, bf16[3,256,128]{2,1,0:T(8,128)(2,1)S(1)}, u32[]{:S(2)}, u32[]{:S(2)}) collective-permute-start(bf16[3,256,128]{2,1,0:T(8,128)(2,1)S(1)} %get-tuple-element.24), channel_id=1, source_target_pairs={{0,16},{16,0},{32,48},{48,32},{64,80},{80,64},{96,112},{112,96},{1... | collective-permute-start | bytes 589832 | tf_op jit(solution)/shard_map/ppermute | solution.py:373
  21.5 12.8 %all-to-all-start.1 = ((bf16[4,128,256]{2,1,0:T(8,128)(2,1)}), bf16[4,128,256]{2,1,0:T(8,128)(2,1)S(1)}, u32[]{:S(2)}, u32[]{:S(2)}) async-start(bf16[4,128,256]{2,1,0:T(8,128)(2,1)} %get-tuple-element.19), calls=%async_computation.1 | async-start | bytes 524288 | tf_op jit(solution)/shard_map/all_to_all | solution.py:385
  29.5 21.0 %collective-permute-start.2 = (bf16[128,2048]{1,0:T(8,128)(2,1)S(1)}, bf16[128,2048]{1,0:T(8,128)(2,1)S(1)}, u32[]{:S(2)}, u32[]{:S(2)}) collective-permute-start(bf16[128,2048]{1,0:T(8,128)(2,1)S(1)} %copy-done), channel_id=1, source_target_pairs={{0,1},{1,0},{2,3},{3,2},{4,5},{5,4},{6,7},{7,6},{8,9},{9,8},{10,11... | collective-permute-start | bytes 1572872 | tf_op jit(solution)/shard_map/ppermute | solution.py:375
  39.0 24.5 %collective-permute-start.3 = (bf16[128,2048]{1,0:T(8,128)(2,1)S(1)}, bf16[128,2048]{1,0:T(8,128)(2,1)S(1)}, u32[]{:S(2)}, u32[]{:S(2)}) collective-permute-start(bf16[128,2048]{1,0:T(8,128)(2,1)S(1)} %collective-permute-done.w2_ref), channel_id=1, source_target_pairs={{0,1},{1,0},{2,3},{3,2},{4,5},{5,4},{6,7},{7,6},{8,9},{9,8},{10,11... | collective-permute-start | bytes 1572872 | tf_op jit(solution)/shard_map/ppermute | solution.py:397
  41.6 21.9 %all-to-all-start.2 = ((bf16[4,128,128]{2,1,0:T(8,128)(2,1)}), bf16[4,128,128]{2,1,0:T(8,128)(2,1)S(1)}, u32[]{:S(2)}, u32[]{:S(2)}) async-start(bf16[4,128,128]{2,1,0:T(8,128)(2,1)} %gated_norm.1), calls=%async_computation.2 | async-start | bytes 262144 | tf_op jit(solution)/shard_map/all_to_all | solution.py:399
  64.2 3.4 %collective-permute-start.4 = (bf16[64,2048]{1,0:T(8,128)(2,1)S(1)}, bf16[64,2048]{1,0:T(8,128)(2,1)S(1)}, u32[]{:S(2)}, u32[]{:S(2)}) collective-permute-start(bf16[64,2048]{1,0:T(8,128)(2,1)S(1)} %get-tuple-element.28), channel_id=1, source_target_pairs={{0,16},{16,0},{32,48},{48,32},{64,80},{80,64},{96,112},{112,96},{1... | collective-permute-start | bytes 786440 | tf_op jit(solution)/shard_map/ppermute | solution.py:410

commit v5 on v4

--- a/solution.py
+++ b/solution.py
@@ -72,33 +72,37 @@
     return lax.rsqrt(jnp.sum(full * full, axis=1, keepdims=True) + 1e-06)
 
 
+def slice_kernel(weight_far, half_ref, sem):
+    rows = half_ref.shape[0]
+    begin = pl.multiple_of(places()[2] * rows, rows)
+    copy = pltpu.make_async_copy(weight_far.at[pl.ds(begin, rows)], half_ref, sem)
+    copy.start()
+    copy.wait()
+
+
 def map_kernel(
     k_far,
     v_far,
     rate_far,
     decay_far,
-    weight_far,
+    ahead_of,
     maps_ref,
     solved_ref,
-    half_ref,
     k_ref,
     v_ref,
     rate_ref,
     decay_ref,
     sems,
 ):
-    rows = half_ref.shape[0]
-    begin = pl.multiple_of(places()[2] * rows, rows)
     copies = [
         pltpu.make_async_copy(k_far, k_ref, sems.at[0]),
         pltpu.make_async_copy(decay_far, decay_ref, sems.at[1]),
         pltpu.make_async_copy(rate_far, rate_ref, sems.at[2]),
         pltpu.make_async_copy(v_far, v_ref, sems.at[3]),
-        pltpu.make_async_copy(weight_far.at[pl.ds(begin, rows)], half_ref, sems.at[4]),
     ]
     for copy in copies:
         copy.start()
-    for copy in copies[:4]:
+    for copy in copies:
         copy.wait()
     keys = k_ref[...]
     keys_f = keys.astype(F32)
@@ -169,7 +173,6 @@
         maps_ref[place] = maps[place % 2]
     for head in range(2):
         solved_ref[head] = solved[head]
-    copies[4].wait()
 
 
 def read_kernel(
@@ -305,7 +308,7 @@
     return pl.BlockSpec(memory_space=pltpu.HBM)
 
 
-def call(kernel, outs, *args, flops=10**8, name=None, ins=None, out_specs=None, scratch=(), room=32):
+def call(kernel, outs, *args, flops=10**3, name=None, ins=None, out_specs=None, scratch=(), room=32):
     if ins is None:
         ins = [in_vmem()] * len(args)
     return pl.pallas_call(
@@ -315,7 +318,7 @@
         out_specs=jax.tree.map(lambda _: in_vmem(), outs) if out_specs is None else out_specs,
         scratch_shapes=scratch,
         compiler_params=pltpu.CompilerParams(vmem_limit_bytes=room * 1024 * 1024),
-        cost_estimate=pl.CostEstimate(flops=flops, bytes_accessed=10**6, transcendentals=0),
+        cost_estimate=pl.CostEstimate(flops=flops, bytes_accessed=10**3, transcendentals=0),
         name=name,
     )(*args)
 
@@ -330,28 +333,36 @@
     width = out_weight.shape[1]
     rate, decay = write_rate.T, log_decay.T
 
-    maps, solved, w0 = call(
+    w0 = call(
+        slice_kernel,
+        shape((DV, width), BF),
+        out_weight,
+        ins=[in_hbm()],
+        scratch=[pltpu.SemaphoreType.DMA],
+        room=60,
+        name="own_rows",
+    )
+    w2 = lax.ppermute(w0, "tp", [(j, j ^ 2) for j in range(16)])
+    maps, solved = call(
         map_kernel,
         (
             shape((8, DK, DK + DV), BF),
             shape((2, TOK, DK + DV), F32),
-            shape((DV, width), BF),
         ),
         key_vectors,
         value_vectors,
         rate,
         decay,
-        out_weight,
-        ins=[in_hbm()] * 5,
-        out_specs=(in_vmem(), in_vmem(), in_vmem()),
+        w0,
+        ins=[in_hbm()] * 4 + [pl.BlockSpec(memory_space=pl.ANY)],
         scratch=[
             pltpu.VMEM((TOK, DK), BF),
             pltpu.VMEM((TOK, 2 * DV), BF),
             pltpu.VMEM((2, TOK), F32),
             pltpu.VMEM((2, TOK), F32),
-            pltpu.SemaphoreType.DMA((5,)),
+            pltpu.SemaphoreType.DMA((4,)),
         ],
-        flops=10**9,
+        flops=10**10,
         room=60,
         name="shard_maps",
     )
@@ -366,21 +377,24 @@
         output_gate,
         norm_gain.reshape(1, DV),
         solved,
-        flops=10**9,
+        flops=10**3,
         name="read_parts",
     )
     across = [(i, i ^ 1) for i in range(32)]
     came = lax.ppermute(send, "ctx", across)
 
-    w1 = lax.ppermute(w0, "tp", [(j, j ^ 1) for j in range(16)])
-    w2 = lax.ppermute(w0, "tp", [(j, j ^ 2) for j in range(16)])
-
+    w0_later, solved = lax.optimization_barrier((w0, solved))
+    w1 = lax.ppermute(w0_later, "tp", [(j, j ^ 1) for j in range(16)])
+
+    parts, w2 = lax.optimization_barrier((parts, w2))
     total, ahead, first = call(
         row_kernel,
         (shape((4, DK, DK + DV), BF), shape((DK, DK + DV), F32), shape((DK, DK + DV), BF)),
         parts,
         name="row_maps",
     )
+    w1, w2, ahead = lax.optimization_barrier((w1, w2, ahead))
+    w3 = lax.ppermute(w2, "tp", [(j, j ^ 1) for j in range(16)])
     columns = [[8 * y + i for y in range(4)] for i in range(8)]
     rows = lax.all_to_all(total, "ctx", 0, 0, axis_index_groups=columns)
     normed = call(
@@ -393,8 +407,6 @@
         came,
         name="gated_norm",
     )
-    w2, normed = lax.optimization_barrier((w2, normed))
-    w3 = lax.ppermute(w2, "tp", [(j, j ^ 1) for j in range(16)])
     close = [[token_of(g, m) for m in range(4)] for g in range(4)]
     gathered = lax.all_to_all(normed, "tp", 0, 0, axis_index_groups=close)
     half, other_half = call(

time: 101 us -> 96.7 us (0.957)
  Pallas kernels: 10.3 us -> 12.6 us
  waiting for transfers between devices: 25.1 us -> 23 us
  local copies, waits for them, and re-layouts: 1.68 us -> 0.04 us
  starting transfers between devices: 31.1 us -> 29.6 us
    all_to_all x1, waiting for transfers between devices: 12.9 us -> 1.97 us  [local(): gathered = lax.all_to_all(normed, 'tp', 0, 0, axis_index_groups=close)]
    ppermute x1, waiting for transfers between devices: 0.01 us -> 7.95 us  [local(): w3 = lax.ppermute(w2, 'tp', [(j, j ^ 1) for j in range(16)])]
    all_to_all x1, starting transfers between devices: 8.08 us -> 4.68 us  [local(): rows = lax.all_to_all(total, 'ctx', 0, 0, axis_index_groups=columns)]
    all_to_all x1, waiting for transfers between devices: 2.75 us -> 0.01 us  [local(): rows = lax.all_to_all(total, 'ctx', 0, 0, axis_index_groups=columns)]
    all_to_all x1, waiting for transfers between devices: 0.48 us -> 2.73 us  [local(): parts = lax.all_to_all(maps, 'ctx', 0, 0, axis_index_groups=lines)]
    pallas_call x7 -> x8, Pallas kernels: 10.3 us -> 12.6 us  [call(): pl.pallas_call(kernel, out_shape=outs, in_specs=ins, out_specs=jax.tree.m...]
    ppermute x1, starting transfers between devices: 1.91 us -> 3.84 us  [local(): w1 = lax.ppermute(w0_later, 'tp', [(j, j ^ 1) for j in range(16)])]
    unnamed x14, local copies, waits for them, and re-layouts: 1.68 us -> 0.04 us
  transfers between devices with their start and end apart: 8 -> 8, of which waited for: 6 -> 6; matrix products, arithmetic and copies ran while one was open for 0% -> 0% of each run, Pallas kernels for 4% -> 10%
where the time goes in v5:
time: 96.7 us; the launch traced here: 96.1 us
  blocking collectives  30.8 us (32%)
  starting transfers between devices  29.6 us (31%)
  waiting for transfers between devices  23 us (24%)
  Pallas kernels  12.6 us (13%)
    all_to_all x1, blocking collectives, local(): shares = lax.all_to_all(partial, 'tp', 0, 0, axis_index_groups=far)  30.8 us
    pallas_call x8, Pallas kernels, call(): pl.pallas_call(kernel, out_shape=outs, in_specs=ins, out_specs=jax.tree.m...  12.6 us
    ppermute x1, waiting for transfers between devices, local(): w3 = lax.ppermute(w2, 'tp', [(j, j ^ 1) for j in range(16)])  7.95 us
    all_to_all x1, starting transfers between devices, local(): gathered = lax.all_to_all(normed, 'tp', 0, 0, axis_index_groups=close)  5.35 us
    ppermute x1, starting transfers between devices, local(): w2 = lax.ppermute(w0, 'tp', [(j, j ^ 2) for j in range(16)])  5.18 us
    ppermute x1, waiting for transfers between devices, local(): w1 = lax.ppermute(w0_later, 'tp', [(j, j ^ 1) for j in range(16)])  5.11 us
    all_to_all x1, starting transfers between devices, local(): rows = lax.all_to_all(total, 'ctx', 0, 0, axis_index_groups=columns)  4.68 us
    all_to_all x1, starting transfers between devices, local(): parts = lax.all_to_all(maps, 'ctx', 0, 0, axis_index_groups=lines)  4.44 us
  transfers between devices with their start and end apart: 8, of which 6 were waited for; matrix products, arithmetic and copies ran while one was open for 0% of the time, Pallas kernels for 10%

profile of v5, /device:TPU:24, one launch (start us, length us, event | category | flops | bytes accessed | tf_op | source)
XLA Modules:
  0.0 96.1 jit_solution(3536906444095415285)
XLA Ops:
  0.0 1.9 %own_rows.1.ahead_of.w0_ref = bf16[128,2048]{1,0:T(8,128)(2,1)} custom-call(bf16[256,2048]{1,0:T(8,128)(2,1)} %weight_far.1), custom_call_target="tpu_custom_call" | custom-call | flops 1000 | bytes 1000 | tf_op jit(solution)/shard_map/own_rows/pallas_call | solution.py:314
  1.9 5.2 %collective-permute-start = (bf16[128,2048]{1,0:T(8,128)(2,1)}, bf16[128,2048]{1,0:T(8,128)(2,1)S(1)}, u32[]{:S(2)}, u32[]{:S(2)}) collective-permute-start(bf16[128,2048]{1,0:T(8,128)(2,1)} %own_rows.1.ahead_of.w0_ref), channel_id=1, source_target_pairs={{0,2},{1,3},{2,0},{3,1},{4,6},{5,7},{6,4},{7,5},{8,10},{9,11},{10,... | collective-permute-start | bytes 1572872 | tf_op jit(solution)/shard_map/ppermute | solution.py:345
  7.0 0.0 copy-start.2
  7.1 0.0 copy-start.3
  7.1 0.0 copy-start.4
  7.1 4.9 %shard_maps.1 = (bf16[8,128,256]{2,1,0:T(8,128)(2,1)}, f32[2,256,256]{2,1,0:T(8,128)}) custom-call(bf16[256,128]{1,0:T(8,128)(2,1)} %k_ref.1, bf16[256,256]{1,0:T(8,128)(2,1)} %v_far.1, f32[2,256]{1,0:T(2,128)} %bitcast.6, f32[2,256]{1,0:T(2,128)} %bitcast.3, bf16[128,2048]{1,0:T(8,128)(2,1)} %own_rows.1.ahead_of.w0_ref), custom_call_target="tpu_custom_call" | custom-call | flops 10000000000 | bytes 1000 | tf_op jit(solution)/shard_map/shard_maps/pallas_call | solution.py:314
  12.0 0.0 copy-start
  12.0 0.0 copy-start.1
  12.0 4.4 %all-to-all-start = ((bf16[8,128,256]{2,1,0:T(8,128)(2,1)}), bf16[8,128,256]{2,1,0:T(8,128)(2,1)S(1)}, u32[]{:S(2)}, u32[]{:S(2)}) async-start(bf16[8,128,256]{2,1,0:T(8,128)(2,1)} %get-tuple-element.20), calls=%async_computation | async-start | bytes 1048576 | tf_op jit(solution)/shard_map/all_to_all | solution.py:370
  16.5 0.0 copy-start.5
  16.5 0.0 copy-done
  16.5 0.0 copy-start.6
  16.5 3.8 %collective-permute-start.1 = (bf16[128,2048]{1,0:T(8,128)(2,1)S(1)}, bf16[128,2048]{1,0:T(8,128)(2,1)S(1)}, u32[]{:S(2)}, u32[]{:S(2)}) collective-permute-start(bf16[128,2048]{1,0:T(8,128)(2,1)S(1)} %copy-done), channel_id=1, source_target_pairs={{0,1},{1,0},{2,3},{3,2},{4,5},{5,4},{6,7},{7,6},{8,9},{9,8},{10,11... | collective-permute-start | bytes 1572872 | tf_op jit(solution)/shard_map/ppermute | solution.py:387
  20.3 0.0 copy-done.2
  20.4 0.0 copy-done.3
  20.4 0.0 copy-done.4
  20.4 0.0 copy-done.1
  20.4 0.0 copy-done.5
  20.4 0.0 copy-done.6
  20.4 1.4 %read_parts.1 = (f32[3,256,128]{2,1,0:T(8,128)S(1)}, bf16[3,256,128]{2,1,0:T(8,128)(2,1)}) custom-call(bf16[256,128]{1,0:T(8,128)(2,1)S(1)} %copy-done.4, bf16[256,128]{1,0:T(8,128)(2,1)S(1)} %copy-done.3, f32[2,256]{1,0:T(2,128)S(1)} %bitcast.4, bf16[256,256]{1,0:T(8,128)(2,1)S(1)} %copy-done.2, f32[1,128]{1,0:T(1,128)S(1)} %bitcast.5, ...), custom_call_target="tpu_custom_call" | custom-call | flops 1000 | bytes 1000 | tf_op jit(solution)/shard_map/read_parts/pallas_call | solution.py:314
  21.8 2.2 %collective-permute-start.2 = (bf16[3,256,128]{2,1,0:T(8,128)(2,1)}, bf16[3,256,128]{2,1,0:T(8,128)(2,1)S(1)}, u32[]{:S(2)}, u32[]{:S(2)}) collective-permute-start(bf16[3,256,128]{2,1,0:T(8,128)(2,1)} %get-tuple-element.30), channel_id=1, source_target_pairs={{0,16},{16,0},{32,48},{48,32},{64,80},{80,64},{96,112},{112,96},{1... | collective-permute-start | bytes 589832 | tf_op jit(solution)/shard_map/ppermute | solution.py:384
  24.1 2.7 %all-to-all-done.parts_ref = bf16[8,128,256]{2,1,0:T(8,128)(2,1)S(1)} async-done(((bf16[8,128,256]{2,1,0:T(8,128)(2,1)}), bf16[8,128,256]{2,1,0:T(8,128)(2,1)S(1)}, u32[]{:S(2)}, u32[]{:S(2)}) %all-to-all-start) | async-done | bytes 524320 | tf_op jit(solution)/shard_map/all_to_all | solution.py:370
  26.8 3.7 %collective-permute-done.w2_ref = bf16[128,2048]{1,0:T(8,128)(2,1)S(1)} collective-permute-done((bf16[128,2048]{1,0:T(8,128)(2,1)}, bf16[128,2048]{1,0:T(8,128)(2,1)S(1)}, u32[]{:S(2)}, u32[]{:S(2)}) %collective-permute-start) | collective-permute-done | bytes 524320 | tf_op jit(solution)/shard_map/ppermute | solution.py:345
  30.5 1.3 %row_maps.1 = (bf16[4,128,256]{2,1,0:T(8,128)(2,1)}, f32[128,256]{1,0:T(8,128)S(1)}, bf16[128,256]{1,0:T(8,128)(2,1)S(1)}) custom-call(bf16[8,128,256]{2,1,0:T(8,128)(2,1)S(1)} %all-to-all-done.parts_ref), custom_call_target="tpu_custom_call" | custom-call | flops 1000 | bytes 1000 | tf_op jit(solution)/shard_map/row_maps/pallas_call | solution.py:314
  31.8 4.7 %all-to-all-start.1 = ((bf16[4,128,256]{2,1,0:T(8,128)(2,1)}), bf16[4,128,256]{2,1,0:T(8,128)(2,1)S(1)}, u32[]{:S(2)}, u32[]{:S(2)}) async-start(bf16[4,128,256]{2,1,0:T(8,128)(2,1)} %get-tuple-element.22), calls=%async_computation.1 | async-start | bytes 524288 | tf_op jit(solution)/shard_map/all_to_all | solution.py:399
  36.5 5.1 %collective-permute-done.1.w1_ref = bf16[128,2048]{1,0:T(8,128)(2,1)S(1)} collective-permute-done((bf16[128,2048]{1,0:T(8,128)(2,1)S(1)}, bf16[128,2048]{1,0:T(8,128)(2,1)S(1)}, u32[]{:S(2)}, u32[]{:S(2)}) %collective-permute-start.1) | collective-permute-done | bytes 524320 | tf_op jit(solution)/shard_map/ppermute | solution.py:387
  41.6 1.9 %collective-permute-start.3 = (bf16[128,2048]{1,0:T(8,128)(2,1)S(1)}, bf16[128,2048]{1,0:T(8,128)(2,1)S(1)}, u32[]{:S(2)}, u32[]{:S(2)}) collective-permute-start(bf16[128,2048]{1,0:T(8,128)(2,1)S(1)} %collective-permute-done.w2_ref), channel_id=1, source_target_pairs={{0,1},{1,0},{2,3},{3,2},{4,5},{5,4},{6,7},{7,6},{8,9},{9,8},{10,11... | collective-permute-start | bytes 1572872 | tf_op jit(solution)/shard_map/ppermute | solution.py:397
  43.6 0.0 collective-permute-done.2.came_ref
  43.6 0.0 all-to-all-done.1.rows_ref
  43.6 1.6 %gated_norm.1 = bf16[4,128,128]{2,1,0:T(8,128)(2,1)} custom-call(bf16[4,128,256]{2,1,0:T(8,128)(2,1)S(1)} %all-to-all-done.1.rows_ref, f32[128,256]{1,0:T(8,128)S(1)} %get-tuple-element.27.ahead_ref, bf16[128,256]{1,0:T(8,128)(2,1)S(1)} %get-tuple-element.28.first_ref, f32[3,256,128]{2,1,0:T(8,128)S(1)} %get-tuple-element.29.keep_ref, ...), custom_call_target="tpu_custom_call" | custom-call | flops 1000 | bytes 1000 | tf_op jit(solution)/shard_map/gated_norm/pallas_call | solution.py:314
  45.2 5.4 %all-to-all-start.2 = ((bf16[4,128,128]{2,1,0:T(8,128)(2,1)}), bf16[4,128,128]{2,1,0:T(8,128)(2,1)S(1)}, u32[]{:S(2)}, u32[]{:S(2)}) async-start(bf16[4,128,128]{2,1,0:T(8,128)(2,1)} %gated_norm.1), calls=%async_computation.2 | async-start | bytes 262144 | tf_op jit(solution)/shard_map/all_to_all | solution.py:411
  50.6 8.0 %collective-permute-done.3.w3_ref = bf16[128,2048]{1,0:T(8,128)(2,1)S(1)} collective-permute-done((bf16[128,2048]{1,0:T(8,128)(2,1)S(1)}, bf16[128,2048]{1,0:T(8,128)(2,1)S(1)}, u32[]{:S(2)}, u32[]{:S(2)}) %collective-permute-start.3) | collective-permute-done | bytes 524320 | tf_op jit(solution)/shard_map/ppermute | solution.py:397
  58.5 2.0 %all-to-all-done.2.normed_ref = bf16[4,128,128]{2,1,0:T(8,128)(2,1)S(1)} async-done(((bf16[4,128,128]{2,1,0:T(8,128)(2,1)}), bf16[4,128,128]{2,1,0:T(8,128)(2,1)S(1)}, u32[]{:S(2)}, u32[]{:S(2)}) %all-to-all-start.2) | async-done | bytes 131104 | tf_op jit(solution)/shard_map/all_to_all | solution.py:411
  60.5 0.7 project.1
  61.2 1.9 %collective-permute-start.4 = (bf16[64,2048]{1,0:T(8,128)(2,1)S(1)}, bf16[64,2048]{1,0:T(8,128)(2,1)S(1)}, u32[]{:S(2)}, u32[]{:S(2)}) collective-permute-start(bf16[64,2048]{1,0:T(8,128)(2,1)S(1)} %get-tuple-element.34), channel_id=1, source_target_pairs={{0,16},{16,0},{32,48},{48,32},{64,80},{80,64},{96,112},{112,96},{1... | collective-permute-start | bytes 786440 | tf_op jit(solution)/shard_map/ppermute | solution.py:422
  63.1 1.5 %collective-permute-done.4.came_ref = bf16[64,2048]{1,0:T(8,128)(2,1)S(1)} collective-permute-done((bf16[64,2048]{1,0:T(8,128)(2,1)S(1)}, bf16[64,2048]{1,0:T(8,128)(2,1)S(1)}, u32[]{:S(2)}, u32[]{:S(2)}) %collective-permute-start.4) | collective-permute-done | bytes 262176 | tf_op jit(solution)/shard_map/ppermute | solution.py:422
  64.7 30.8 %all_to_all.20.parts_ref = bf16[4,16,2048]{2,1,0:T(8,128)(2,1)S(1)} all-to-all(bf16[4,16,2048]{2,1,0:T(8,128)(2,1)S(1)} %join.1), channel_id=1, replica_groups={{0,4,11,15},{1,5,10,14},{2,6,9,13},{3,7,8,12},{16,20,27,31},{17,21,26,3..., dimensions={0} | all-to-all | bytes 524288 | tf_op jit(solution)/shard_map/all_to_all | solution.py:425
  95.4 0.7 sum_shares.1
  (1 shorter events, 0.0 us)
Async XLA Ops:
  1.9 28.6 %collective-permute-start = (bf16[128,2048]{1,0:T(8,128)(2,1)}, bf16[128,2048]{1,0:T(8,128)(2,1)S(1)}, u32[]{:S(2)}, u32[]{:S(2)}) collective-permute-start(bf16[128,2048]{1,0:T(8,128)(2,1)} %own_rows.1.ahead_of.w0_ref), channel_id=1, source_target_pairs={{0,2},{1,3},{2,0},{3,1},{4,6},{5,7},{6,4},{7,5},{8,10},{9,11},{10,... | collective-permute-start | bytes 1572872 | tf_op jit(solution)/shard_map/ppermute | solution.py:345
  7.0 13.3 %copy-start.2 = (bf16[256,256]{1,0:T(8,128)(2,1)S(1)}, bf16[256,256]{1,0:T(8,128)(2,1)}, u32[]{:S(2)}) copy-start(bf16[256,256]{1,0:T(8,128)(2,1)} %gate_ref.1) | copy-start | bytes 393220
  7.1 13.3 %copy-start.3 = (bf16[256,128]{1,0:T(8,128)(2,1)S(1)}, bf16[256,128]{1,0:T(8,128)(2,1)}, u32[]{:S(2)}) copy-start(bf16[256,128]{1,0:T(8,128)(2,1)} %k_ref.1) | copy-start | bytes 196612
  7.1 13.3 %copy-start.4 = (bf16[256,128]{1,0:T(8,128)(2,1)S(1)}, bf16[256,128]{1,0:T(8,128)(2,1)}, u32[]{:S(2)}) copy-start(bf16[256,128]{1,0:T(8,128)(2,1)} %q_ref.1) | copy-start | bytes 196612
  12.0 4.5 %copy-start = (bf16[128,2048]{1,0:T(8,128)(2,1)S(1)}, bf16[128,2048]{1,0:T(8,128)(2,1)}, u32[]{:S(2)}) copy-start(bf16[128,2048]{1,0:T(8,128)(2,1)} %own_rows.1.ahead_of.w0_ref) | copy-start | bytes 1572868
  12.0 8.4 %copy-start.1 = (f32[2,256,256]{2,1,0:T(8,128)S(1)}, f32[2,256,256]{2,1,0:T(8,128)}, u32[]{:S(2)}) copy-start(f32[2,256,256]{2,1,0:T(8,128)} %get-tuple-element.23.solved_ref) | copy-start | bytes 1572868
  12.0 14.8 %all-to-all-start = ((bf16[8,128,256]{2,1,0:T(8,128)(2,1)}), bf16[8,128,256]{2,1,0:T(8,128)(2,1)S(1)}, u32[]{:S(2)}, u32[]{:S(2)}) async-start(bf16[8,128,256]{2,1,0:T(8,128)(2,1)} %get-tuple-element.20), calls=%async_computation | async-start | bytes 1048576 | tf_op jit(solution)/shard_map/all_to_all | solution.py:370
  16.5 3.9 %copy-start.5 = (f32[256,2]{0,1:T(2,128)S(1)}, f32[256,2]{0,1:T(2,128)}, u32[]{:S(2)}) copy-start(f32[256,2]{0,1:T(2,128)} %param.13) | copy-start | bytes 6148
  16.5 3.9 %copy-start.6 = (f32[128]{0:T(128)S(1)}, f32[128]{0:T(128)}, u32[]{:S(2)}) copy-start(f32[128]{0:T(128)} %param.14) | copy-start | bytes 1540
  16.5 25.1 %collective-permute-start.1 = (bf16[128,2048]{1,0:T(8,128)(2,1)S(1)}, bf16[128,2048]{1,0:T(8,128)(2,1)S(1)}, u32[]{:S(2)}, u32[]{:S(2)}) collective-permute-start(bf16[128,2048]{1,0:T(8,128)(2,1)S(1)} %copy-done), channel_id=1, source_target_pairs={{0,1},{1,0},{2,3},{3,2},{4,5},{5,4},{6,7},{7,6},{8,9},{9,8},{10,11... | collective-permute-start | bytes 1572872 | tf_op jit(solution)/shard_map/ppermute | solution.py:387
  21.8 21.7 %collective-permute-start.2 = (bf16[3,256,128]{2,1,0:T(8,128)(2,1)}, bf16[3,256,128]{2,1,0:T(8,128)(2,1)S(1)}, u32[]{:S(2)}, u32[]{:S(2)}) collective-permute-start(bf16[3,256,128]{2,1,0:T(8,128)(2,1)} %get-tuple-element.30), channel_id=1, source_target_pairs={{0,16},{16,0},{32,48},{48,32},{64,80},{80,64},{96,112},{112,96},{1... | collective-permute-start | bytes 589832 | tf_op jit(solution)/shard_map/ppermute | solution.py:384
  31.8 11.7 %all-to-all-start.1 = ((bf16[4,128,256]{2,1,0:T(8,128)(2,1)}), bf16[4,128,256]{2,1,0:T(8,128)(2,1)S(1)}, u32[]{:S(2)}, u32[]{:S(2)}) async-start(bf16[4,128,256]{2,1,0:T(8,128)(2,1)} %get-tuple-element.22), calls=%async_computation.1 | async-start | bytes 524288 | tf_op jit(solution)/shard_map/all_to_all | solution.py:399
  41.6 16.9 %collective-permute-start.3 = (bf16[128,2048]{1,0:T(8,128)(2,1)S(1)}, bf16[128,2048]{1,0:T(8,128)(2,1)S(1)}, u32[]{:S(2)}, u32[]{:S(2)}) collective-permute-start(bf16[128,2048]{1,0:T(8,128)(2,1)S(1)} %collective-permute-done.w2_ref), channel_id=1, source_target_pairs={{0,1},{1,0},{2,3},{3,2},{4,5},{5,4},{6,7},{7,6},{8,9},{9,8},{10,11... | collective-permute-start | bytes 1572872 | tf_op jit(solution)/shard_map/ppermute | solution.py:397
  45.2 15.3 %all-to-all-start.2 = ((bf16[4,128,128]{2,1,0:T(8,128)(2,1)}), bf16[4,128,128]{2,1,0:T(8,128)(2,1)S(1)}, u32[]{:S(2)}, u32[]{:S(2)}) async-start(bf16[4,128,128]{2,1,0:T(8,128)(2,1)} %gated_norm.1), calls=%async_computation.2 | async-start | bytes 262144 | tf_op jit(solution)/shard_map/all_to_all | solution.py:411
  61.2 3.4 %collective-permute-start.4 = (bf16[64,2048]{1,0:T(8,128)(2,1)S(1)}, bf16[64,2048]{1,0:T(8,128)(2,1)S(1)}, u32[]{:S(2)}, u32[]{:S(2)}) collective-permute-start(bf16[64,2048]{1,0:T(8,128)(2,1)S(1)} %get-tuple-element.34), channel_id=1, source_target_pairs={{0,16},{16,0},{32,48},{48,32},{64,80},{80,64},{96,112},{112,96},{1... | collective-permute-start | bytes 786440 | tf_op jit(solution)/shard_map/ppermute | solution.py:422

commit v6 on v4

--- a/solution.py
+++ b/solution.py
@@ -80,6 +80,7 @@
     weight_far,
     maps_ref,
     solved_ref,
+    rows_ref,
     half_ref,
     k_ref,
     v_ref,
@@ -87,14 +88,17 @@
     decay_ref,
     sems,
 ):
-    rows = half_ref.shape[0]
-    begin = pl.multiple_of(places()[2] * rows, rows)
+    _, x, core = places()
+    rows, some = rows_ref.shape[0], half_ref.shape[0]
+    begin = pl.multiple_of(core * rows, rows)
+    begin_half = pl.multiple_of(core * rows + (x % 2) * some, some)
     copies = [
         pltpu.make_async_copy(k_far, k_ref, sems.at[0]),
         pltpu.make_async_copy(decay_far, decay_ref, sems.at[1]),
         pltpu.make_async_copy(rate_far, rate_ref, sems.at[2]),
         pltpu.make_async_copy(v_far, v_ref, sems.at[3]),
-        pltpu.make_async_copy(weight_far.at[pl.ds(begin, rows)], half_ref, sems.at[4]),
+        pltpu.make_async_copy(weight_far.at[pl.ds(begin, rows)], rows_ref, sems.at[4]),
+        pltpu.make_async_copy(weight_far.at[pl.ds(begin_half, some)], half_ref, sems.at[5]),
     ]
     for copy in copies:
         copy.start()
@@ -169,7 +173,8 @@
         maps_ref[place] = maps[place % 2]
     for head in range(2):
         solved_ref[head] = solved[head]
-    copies[4].wait()
+    for copy in copies[4:]:
+        copy.wait()
 
 
 def read_kernel(
@@ -267,14 +272,23 @@
                 out_ref[label, target : target + 16] = shards[shard][source : source + 16]
 
 
-def project_kernel(normed_ref, w0_ref, w1_ref, w2_ref, w3_ref, keep_ref, send_ref):
-    core = places()[2]
+def project_kernel(
+    normed_ref, own_ref, near_ref, half3_ref, side_ref, side3_ref, keep_ref, send_ref
+):
+    _, x, core = places()
     along = lax.axis_index("tp")
-    total = None
-    for i, weight_ref in enumerate((w0_ref, w1_ref, w2_ref, w3_ref)):
+
+    def rows_from(i):
         near = (along % 4) ^ i
-        term = dot(normed_ref[jnp.where(along < 8, near, 3 - near)], weight_ref[...])
-        total = term if total is None else total + term
+        return normed_ref[jnp.where(along < 8, near, 3 - near)]
+
+    total = dot(rows_from(0), own_ref[...])
+    halves = ((near_ref[0], side_ref[0]), (near_ref[1], side_ref[1]), (half3_ref[...], side3_ref[...]))
+    for i, (mine, other) in enumerate(halves):
+        left = rows_from(i + 1).astype(F32)
+        swapped = jnp.concatenate([left[:, DV // 2 :], left[:, : DV // 2]], axis=1)
+        left = jnp.where(x % 2 == 0, left, swapped).astype(BF)
+        total = total + dot(left, jnp.concatenate([mine, other], axis=0))
     keep_ref[...] = jnp.where(core == 0, total[:64], total[64:])
     send_ref[...] = jnp.where(core == 0, total[64:], total[:64]).astype(BF)
 
@@ -305,7 +319,7 @@
     return pl.BlockSpec(memory_space=pltpu.HBM)
 
 
-def call(kernel, outs, *args, flops=10**8, name=None, ins=None, out_specs=None, scratch=(), room=32):
+def call(kernel, outs, *args, flops=10**3, name=None, ins=None, out_specs=None, scratch=(), room=32):
     if ins is None:
         ins = [in_vmem()] * len(args)
     return pl.pallas_call(
@@ -315,7 +329,7 @@
         out_specs=jax.tree.map(lambda _: in_vmem(), outs) if out_specs is None else out_specs,
         scratch_shapes=scratch,
         compiler_params=pltpu.CompilerParams(vmem_limit_bytes=room * 1024 * 1024),
-        cost_estimate=pl.CostEstimate(flops=flops, bytes_accessed=10**6, transcendentals=0),
+        cost_estimate=pl.CostEstimate(flops=flops, bytes_accessed=10**3, transcendentals=0),
         name=name,
     )(*args)
 
@@ -330,12 +344,13 @@
     width = out_weight.shape[1]
     rate, decay = write_rate.T, log_decay.T
 
-    maps, solved, w0 = call(
+    maps, solved, w0, half0 = call(
         map_kernel,
         (
             shape((8, DK, DK + DV), BF),
             shape((2, TOK, DK + DV), F32),
             shape((DV, width), BF),
+            shape((DV // 2, width), BF),
         ),
         key_vectors,
         value_vectors,
@@ -343,13 +358,13 @@
         decay,
         out_weight,
         ins=[in_hbm()] * 5,
-        out_specs=(in_vmem(), in_vmem(), in_vmem()),
+        out_specs=(in_vmem(), in_vmem(), in_vmem(), in_vmem()),
         scratch=[
             pltpu.VMEM((TOK, DK), BF),
             pltpu.VMEM((TOK, 2 * DV), BF),
             pltpu.VMEM((2, TOK), F32),
             pltpu.VMEM((2, TOK), F32),
-            pltpu.SemaphoreType.DMA((5,)),
+            pltpu.SemaphoreType.DMA((6,)),
         ],
         flops=10**9,
         room=60,
@@ -372,8 +387,9 @@
     across = [(i, i ^ 1) for i in range(32)]
     came = lax.ppermute(send, "ctx", across)
 
-    w1 = lax.ppermute(w0, "tp", [(j, j ^ 1) for j in range(16)])
-    w2 = lax.ppermute(w0, "tp", [(j, j ^ 2) for j in range(16)])
+    one_off = [(j, j ^ 1) for j in range(16)]
+    half1 = lax.ppermute(half0, "tp", one_off)
+    half2 = lax.ppermute(half0, "tp", [(j, j ^ 2) for j in range(16)])
 
     total, ahead, first = call(
         row_kernel,
@@ -381,6 +397,11 @@
         parts,
         name="row_maps",
     )
+    half0, ahead = lax.optimization_barrier((half0, ahead))
+    half3 = lax.ppermute(half0, "tp", [(j, j ^ 3) for j in range(16)])
+    sideways = [(i, i ^ 2) for i in range(32)]
+    near12 = jnp.stack([half1, half2])
+    side12 = lax.ppermute(near12, "ctx", sideways)
     columns = [[8 * y + i for y in range(4)] for i in range(8)]
     rows = lax.all_to_all(total, "ctx", 0, 0, axis_index_groups=columns)
     normed = call(
@@ -393,18 +414,19 @@
         came,
         name="gated_norm",
     )
-    w2, normed = lax.optimization_barrier((w2, normed))
-    w3 = lax.ppermute(w2, "tp", [(j, j ^ 1) for j in range(16)])
     close = [[token_of(g, m) for m in range(4)] for g in range(4)]
+    half3, normed = lax.optimization_barrier((half3, normed))
+    side3 = lax.ppermute(half3, "ctx", sideways)
     gathered = lax.all_to_all(normed, "tp", 0, 0, axis_index_groups=close)
     half, other_half = call(
         project_kernel,
         (shape((64, width), F32), shape((64, width), BF)),
         gathered,
         w0,
-        w1,
-        w2,
-        w3,
+        near12,
+        half3,
+        side12,
+        side3,
         name="project",
     )
     other_half = lax.ppermute(other_half, "ctx", across)

time: 101 us -> 91.6 us (0.907)
  the two profiles are of different devices: /device:TPU:24 before, /device:TPU:35 now
where the time goes in v6:
time: 91.6 us; the launch traced here: 90.9 us
  starting transfers between devices  33.8 us (37%)
  blocking collectives  28.8 us (31%)
  waiting for transfers between devices  16.9 us (18%)
  Pallas kernels  10.5 us (11%)
    all_to_all x1, blocking collectives, local(): shares = lax.all_to_all(partial, 'tp', 0, 0, axis_index_groups=far)  28.8 us
    pallas_call x7, Pallas kernels, call(): pl.pallas_call(kernel, out_shape=outs, in_specs=ins, out_specs=jax.tree.m...  10.5 us
    ppermute x1, waiting for transfers between devices, local(): half3 = lax.ppermute(half0, 'tp', [(j, j ^ 3) for j in range(16)])  7.46 us
    ppermute x1, waiting for transfers between devices, local(): side3 = lax.ppermute(half3, 'ctx', sideways)  6.56 us
    ppermute x1, starting transfers between devices, local(): half1 = lax.ppermute(half0, 'tp', one_off)  6.34 us
    all_to_all x1, starting transfers between devices, local(): parts = lax.all_to_all(maps, 'ctx', 0, 0, axis_index_groups=lines)  5.29 us
    ppermute x1, starting transfers between devices, local(): other_half = lax.ppermute(other_half, 'ctx', across)  4.02 us
    all_to_all x1, starting transfers between devices, local(): rows = lax.all_to_all(total, 'ctx', 0, 0, axis_index_groups=columns)  3.4 us
  transfers between devices with their start and end apart: 10, of which 4 were waited for; matrix products, arithmetic and copies ran while one was open for 0% of the time, Pallas kernels for 4%

profile of v6, /device:TPU:35, one launch (start us, length us, event | category | flops | bytes accessed | tf_op | source)
XLA Modules:
  0.0 90.9 jit_solution(1387781643276159817)
XLA Ops:
  0.0 5.4 %shard_maps.1 = (bf16[8,128,256]{2,1,0:T(8,128)(2,1)}, f32[2,256,256]{2,1,0:T(8,128)}, bf16[128,2048]{1,0:T(8,128)(2,1)}, bf16[64,2048]{1,0:T(8,128)(2,1)}) custom-call(bf16[256,128]{1,0:T(8,128)(2,1)} %k_ref.1, bf16[256,256]{1,0:T(8,128)(2,1)} %v_far.1, f32[2,256]{1,0:T(2,128)} %bitcast.10, f32[2,256]{1,0:T(2,128)} %bitcast.5, bf16[256,2048]{1,0:T(8,128)(2,1)} %weight_far.1), custom_call_target="tpu_custom_call" | custom-call | flops 1000000000 | bytes 1000 | tf_op jit(solution)/shard_map/shard_maps/pallas_call | solution.py:325
  5.4 0.0 copy-start.7
  5.4 0.0 copy-start.1
  5.4 0.0 copy-start.2
  5.4 0.0 copy-start.3
  5.4 0.0 copy-start.6
  5.4 5.3 %all-to-all-start = ((bf16[8,128,256]{2,1,0:T(8,128)(2,1)}), bf16[8,128,256]{2,1,0:T(8,128)(2,1)S(1)}, u32[]{:S(2)}, u32[]{:S(2)}) async-start(bf16[8,128,256]{2,1,0:T(8,128)(2,1)} %get-tuple-element.21), calls=%async_computation | async-start | bytes 1048576 | tf_op jit(solution)/shard_map/all_to_all | solution.py:374
  10.7 0.0 copy-done.7
  10.7 0.0 copy-start.4
  10.7 6.3 %collective-permute-start.2 = (bf16[64,2048]{1,0:T(8,128)(2,1)S(1)}, bf16[64,2048]{1,0:T(8,128)(2,1)S(1)}, u32[]{:S(2)}, u32[]{:S(2)}) collective-permute-start(bf16[64,2048]{1,0:T(8,128)(2,1)S(1)} %copy-done.7), channel_id=1, source_target_pairs={{0,1},{1,0},{2,3},{3,2},{4,5},{5,4},{6,7},{7,6},{8,9},{9,8},{10,11... | collective-permute-start | bytes 786440 | tf_op jit(solution)/shard_map/ppermute | solution.py:391
  17.1 1.9 %collective-permute-start.3 = (bf16[64,2048]{1,0:T(8,128)(2,1)S(1)}, bf16[64,2048]{1,0:T(8,128)(2,1)S(1)}, u32[]{:S(2)}, u32[]{:S(2)}) collective-permute-start(bf16[64,2048]{1,0:T(8,128)(2,1)S(1)} %copy-done.7), channel_id=1, source_target_pairs={{0,2},{1,3},{2,0},{3,1},{4,6},{5,7},{6,4},{7,5},{8,10},{9,11},{10,... | collective-permute-start | bytes 786440 | tf_op jit(solution)/shard_map/ppermute | solution.py:392
  19.0 0.0 copy-start.5
  19.0 0.0 copy-done.1
  19.0 0.0 copy-done.2
  19.1 0.0 copy-done.3
  19.1 0.0 copy-done.6
  19.1 0.0 copy-done.4
  19.1 0.6 copy-done.5
  19.7 0.7 read_parts.1
  20.4 2.5 %collective-permute-start.1 = (bf16[3,256,128]{2,1,0:T(8,128)(2,1)S(1)}, bf16[3,256,128]{2,1,0:T(8,128)(2,1)S(1)}, u32[]{:S(2)}, u32[]{:S(2)}) collective-permute-start(bf16[3,256,128]{2,1,0:T(8,128)(2,1)S(1)} %get-tuple-element.29), channel_id=1, source_target_pairs={{0,16},{16,0},{32,48},{48,32},{64,80},{80,64},{96,112},{112,96},{1... | collective-permute-start | bytes 589832 | tf_op jit(solution)/shard_map/ppermute | solution.py:388
  23.0 0.0 all-to-all-done.parts_ref
  23.0 1.3 %row_maps.1 = (bf16[4,128,256]{2,1,0:T(8,128)(2,1)}, f32[128,256]{1,0:T(8,128)S(1)}, bf16[128,256]{1,0:T(8,128)(2,1)S(1)}) custom-call(bf16[8,128,256]{2,1,0:T(8,128)(2,1)S(1)} %all-to-all-done.parts_ref), custom_call_target="tpu_custom_call" | custom-call | flops 1000 | bytes 1000 | tf_op jit(solution)/shard_map/row_maps/pallas_call | solution.py:325
  24.3 3.4 %all-to-all-start.1 = ((bf16[4,128,256]{2,1,0:T(8,128)(2,1)}), bf16[4,128,256]{2,1,0:T(8,128)(2,1)S(1)}, u32[]{:S(2)}, u32[]{:S(2)}) async-start(bf16[4,128,256]{2,1,0:T(8,128)(2,1)} %get-tuple-element.24), calls=%async_computation.1 | async-start | bytes 524288 | tf_op jit(solution)/shard_map/all_to_all | solution.py:406
  27.7 3.1 %collective-permute-start = (bf16[64,2048]{1,0:T(8,128)(2,1)S(1)}, bf16[64,2048]{1,0:T(8,128)(2,1)S(1)}, u32[]{:S(2)}, u32[]{:S(2)}) collective-permute-start(bf16[64,2048]{1,0:T(8,128)(2,1)S(1)} %copy-done.7), channel_id=1, source_target_pairs={{0,3},{1,2},{2,1},{3,0},{4,7},{5,6},{6,5},{7,4},{8,11},{9,10},{10,... | collective-permute-start | bytes 786440 | tf_op jit(solution)/shard_map/ppermute | solution.py:401
  30.8 0.0 collective-permute-done.2
  30.8 0.0 collective-permute-done.3
  30.8 0.1 pad_maximum_fusion.near_ref
  30.9 1.9 %collective-permute-start.4 = (bf16[2,64,2048]{2,1,0:T(8,128)(2,1)S(1)}, bf16[2,64,2048]{2,1,0:T(8,128)(2,1)S(1)}, u32[]{:S(2)}, u32[]{:S(2)}) collective-permute-start(bf16[2,64,2048]{2,1,0:T(8,128)(2,1)S(1)} %pad_maximum_fusion.near_ref), channel_id=1, source_target_pairs={{0,32},{16,48},{32,0},{48,16},{64,96},{80,112},{96,64},{112,80},{1... | collective-permute-start | bytes 1572872 | tf_op jit(solution)/shard_map/ppermute | solution.py:404
  32.8 0.0 collective-permute-done.1.came_ref
  32.8 1.7 %all-to-all-done.1.rows_ref = bf16[4,128,256]{2,1,0:T(8,128)(2,1)S(1)} async-done(((bf16[4,128,256]{2,1,0:T(8,128)(2,1)}), bf16[4,128,256]{2,1,0:T(8,128)(2,1)S(1)}, u32[]{:S(2)}, u32[]{:S(2)}) %all-to-all-start.1) | async-done | bytes 262176 | tf_op jit(solution)/shard_map/all_to_all | solution.py:406
  34.5 0.0 copy-start
  34.5 1.6 %gated_norm.1 = bf16[4,128,128]{2,1,0:T(8,128)(2,1)} custom-call(bf16[4,128,256]{2,1,0:T(8,128)(2,1)S(1)} %all-to-all-done.1.rows_ref, f32[128,256]{1,0:T(8,128)S(1)} %get-tuple-element.25.ahead_ref, bf16[128,256]{1,0:T(8,128)(2,1)S(1)} %get-tuple-element.26.first_ref, f32[3,256,128]{2,1,0:T(8,128)S(1)} %get-tuple-element.28.keep_ref, ...), custom_call_target="tpu_custom_call" | custom-call | flops 1000 | bytes 1000 | tf_op jit(solution)/shard_map/gated_norm/pallas_call | solution.py:325
  36.2 7.5 %collective-permute-done.half3_ref = bf16[64,2048]{1,0:T(8,128)(2,1)S(1)} collective-permute-done((bf16[64,2048]{1,0:T(8,128)(2,1)S(1)}, bf16[64,2048]{1,0:T(8,128)(2,1)S(1)}, u32[]{:S(2)}, u32[]{:S(2)}) %collective-permute-start) | collective-permute-done | bytes 262176 | tf_op jit(solution)/shard_map/ppermute | solution.py:401
  43.6 3.3 %all-to-all-start.2 = ((bf16[4,128,128]{2,1,0:T(8,128)(2,1)}), bf16[4,128,128]{2,1,0:T(8,128)(2,1)S(1)}, u32[]{:S(2)}, u32[]{:S(2)}) async-start(bf16[4,128,128]{2,1,0:T(8,128)(2,1)} %gated_norm.1), calls=%async_computation.2 | async-start | bytes 262144 | tf_op jit(solution)/shard_map/all_to_all | solution.py:420
  46.9 1.9 %collective-permute-start.5 = (bf16[64,2048]{1,0:T(8,128)(2,1)S(1)}, bf16[64,2048]{1,0:T(8,128)(2,1)S(1)}, u32[]{:S(2)}, u32[]{:S(2)}) collective-permute-start(bf16[64,2048]{1,0:T(8,128)(2,1)S(1)} %collective-permute-done.half3_ref), channel_id=1, source_target_pairs={{0,32},{16,48},{32,0},{48,16},{64,96},{80,112},{96,64},{112,80},{1... | collective-permute-start | bytes 786440 | tf_op jit(solution)/shard_map/ppermute | solution.py:419
  48.9 0.0 collective-permute-done.4.side_ref
  48.9 6.6 %collective-permute-done.5.side3_ref = bf16[64,2048]{1,0:T(8,128)(2,1)S(1)} collective-permute-done((bf16[64,2048]{1,0:T(8,128)(2,1)S(1)}, bf16[64,2048]{1,0:T(8,128)(2,1)S(1)}, u32[]{:S(2)}, u32[]{:S(2)}) %collective-permute-start.5) | collective-permute-done | bytes 262176 | tf_op jit(solution)/shard_map/ppermute | solution.py:419
  55.4 0.0 all-to-all-done.2.normed_ref
  55.4 0.0 copy-done
  55.5 0.8 project.1
  56.2 4.0 %collective-permute-start.6 = (bf16[64,2048]{1,0:T(8,128)(2,1)S(1)}, bf16[64,2048]{1,0:T(8,128)(2,1)S(1)}, u32[]{:S(2)}, u32[]{:S(2)}) collective-permute-start(bf16[64,2048]{1,0:T(8,128)(2,1)S(1)} %get-tuple-element.34), channel_id=1, source_target_pairs={{0,16},{16,0},{32,48},{48,32},{64,80},{80,64},{96,112},{112,96},{1... | collective-permute-start | bytes 786440 | tf_op jit(solution)/shard_map/ppermute | solution.py:432
  60.2 1.1 %collective-permute-done.6.came_ref = bf16[64,2048]{1,0:T(8,128)(2,1)S(1)} collective-permute-done((bf16[64,2048]{1,0:T(8,128)(2,1)S(1)}, bf16[64,2048]{1,0:T(8,128)(2,1)S(1)}, u32[]{:S(2)}, u32[]{:S(2)}) %collective-permute-start.6) | collective-permute-done | bytes 262176 | tf_op jit(solution)/shard_map/ppermute | solution.py:432
  61.4 28.8 %all_to_all.20.parts_ref = bf16[4,16,2048]{2,1,0:T(8,128)(2,1)S(1)} all-to-all(bf16[4,16,2048]{2,1,0:T(8,128)(2,1)S(1)} %join.1), channel_id=1, replica_groups={{0,4,11,15},{1,5,10,14},{2,6,9,13},{3,7,8,12},{16,20,27,31},{17,21,26,3..., dimensions={0} | all-to-all | bytes 524288 | tf_op jit(solution)/shard_map/all_to_all | solution.py:435
  90.3 0.7 sum_shares.1
  (1 shorter events, 0.0 us)
Async XLA Ops:
  5.4 5.3 %copy-start.7 = (bf16[64,2048]{1,0:T(8,128)(2,1)S(1)}, bf16[64,2048]{1,0:T(8,128)(2,1)}, u32[]{:S(2)}) copy-start(bf16[64,2048]{1,0:T(8,128)(2,1)} %get-tuple-element.23) | copy-start | bytes 786436
  5.4 13.6 %copy-start.1 = (bf16[256,256]{1,0:T(8,128)(2,1)S(1)}, bf16[256,256]{1,0:T(8,128)(2,1)}, u32[]{:S(2)}) copy-start(bf16[256,256]{1,0:T(8,128)(2,1)} %gate_ref.1) | copy-start | bytes 393220
  5.4 13.6 %copy-start.2 = (bf16[256,128]{1,0:T(8,128)(2,1)S(1)}, bf16[256,128]{1,0:T(8,128)(2,1)}, u32[]{:S(2)}) copy-start(bf16[256,128]{1,0:T(8,128)(2,1)} %k_ref.1) | copy-start | bytes 196612
  5.4 13.6 %copy-start.3 = (bf16[256,128]{1,0:T(8,128)(2,1)S(1)}, bf16[256,128]{1,0:T(8,128)(2,1)}, u32[]{:S(2)}) copy-start(bf16[256,128]{1,0:T(8,128)(2,1)} %q_ref.1) | copy-start | bytes 196612
  5.4 13.6 %copy-start.6 = (f32[2,256,256]{2,1,0:T(8,128)S(1)}, f32[2,256,256]{2,1,0:T(8,128)}, u32[]{:S(2)}) copy-start(f32[2,256,256]{2,1,0:T(8,128)} %get-tuple-element.27.solved_ref) | copy-start | bytes 1572868
  5.4 17.5 %all-to-all-start = ((bf16[8,128,256]{2,1,0:T(8,128)(2,1)}), bf16[8,128,256]{2,1,0:T(8,128)(2,1)S(1)}, u32[]{:S(2)}, u32[]{:S(2)}) async-start(bf16[8,128,256]{2,1,0:T(8,128)(2,1)} %get-tuple-element.21), calls=%async_computation | async-start | bytes 1048576 | tf_op jit(solution)/shard_map/all_to_all | solution.py:374
  10.7 8.3 %copy-start.4 = (f32[256,2]{0,1:T(2,128)S(1)}, f32[256,2]{0,1:T(2,128)}, u32[]{:S(2)}) copy-start(f32[256,2]{0,1:T(2,128)} %param.13) | copy-start | bytes 6148
  10.7 20.1 %collective-permute-start.2 = (bf16[64,2048]{1,0:T(8,128)(2,1)S(1)}, bf16[64,2048]{1,0:T(8,128)(2,1)S(1)}, u32[]{:S(2)}, u32[]{:S(2)}) collective-permute-start(bf16[64,2048]{1,0:T(8,128)(2,1)S(1)} %copy-done.7), channel_id=1, source_target_pairs={{0,1},{1,0},{2,3},{3,2},{4,5},{5,4},{6,7},{7,6},{8,9},{9,8},{10,11... | collective-permute-start | bytes 786440 | tf_op jit(solution)/shard_map/ppermute | solution.py:391
  17.1 13.7 %collective-permute-start.3 = (bf16[64,2048]{1,0:T(8,128)(2,1)S(1)}, bf16[64,2048]{1,0:T(8,128)(2,1)S(1)}, u32[]{:S(2)}, u32[]{:S(2)}) collective-permute-start(bf16[64,2048]{1,0:T(8,128)(2,1)S(1)} %copy-done.7), channel_id=1, source_target_pairs={{0,2},{1,3},{2,0},{3,1},{4,6},{5,7},{6,4},{7,5},{8,10},{9,11},{10,... | collective-permute-start | bytes 786440 | tf_op jit(solution)/shard_map/ppermute | solution.py:392
  19.0 0.7 copy-start.5
  20.4 12.4 %collective-permute-start.1 = (bf16[3,256,128]{2,1,0:T(8,128)(2,1)S(1)}, bf16[3,256,128]{2,1,0:T(8,128)(2,1)S(1)}, u32[]{:S(2)}, u32[]{:S(2)}) collective-permute-start(bf16[3,256,128]{2,1,0:T(8,128)(2,1)S(1)} %get-tuple-element.29), channel_id=1, source_target_pairs={{0,16},{16,0},{32,48},{48,32},{64,80},{80,64},{96,112},{112,96},{1... | collective-permute-start | bytes 589832 | tf_op jit(solution)/shard_map/ppermute | solution.py:388
  24.3 10.2 %all-to-all-start.1 = ((bf16[4,128,256]{2,1,0:T(8,128)(2,1)}), bf16[4,128,256]{2,1,0:T(8,128)(2,1)S(1)}, u32[]{:S(2)}, u32[]{:S(2)}) async-start(bf16[4,128,256]{2,1,0:T(8,128)(2,1)} %get-tuple-element.24), calls=%async_computation.1 | async-start | bytes 524288 | tf_op jit(solution)/shard_map/all_to_all | solution.py:406
  27.7 15.9 %collective-permute-start = (bf16[64,2048]{1,0:T(8,128)(2,1)S(1)}, bf16[64,2048]{1,0:T(8,128)(2,1)S(1)}, u32[]{:S(2)}, u32[]{:S(2)}) collective-permute-start(bf16[64,2048]{1,0:T(8,128)(2,1)S(1)} %copy-done.7), channel_id=1, source_target_pairs={{0,3},{1,2},{2,1},{3,0},{4,7},{5,6},{6,5},{7,4},{8,11},{9,10},{10,... | collective-permute-start | bytes 786440 | tf_op jit(solution)/shard_map/ppermute | solution.py:401
  30.9 18.0 %collective-permute-start.4 = (bf16[2,64,2048]{2,1,0:T(8,128)(2,1)S(1)}, bf16[2,64,2048]{2,1,0:T(8,128)(2,1)S(1)}, u32[]{:S(2)}, u32[]{:S(2)}) collective-permute-start(bf16[2,64,2048]{2,1,0:T(8,128)(2,1)S(1)} %pad_maximum_fusion.near_ref), channel_id=1, source_target_pairs={{0,32},{16,48},{32,0},{48,16},{64,96},{80,112},{96,64},{112,80},{1... | collective-permute-start | bytes 1572872 | tf_op jit(solution)/shard_map/ppermute | solution.py:404
  34.5 20.9 %copy-start = (bf16[128,2048]{1,0:T(8,128)(2,1)S(1)}, bf16[128,2048]{1,0:T(8,128)(2,1)}, u32[]{:S(2)}) copy-start(bf16[128,2048]{1,0:T(8,128)(2,1)} %get-tuple-element.31.own_ref) | copy-start | bytes 1572868
  43.6 11.8 %all-to-all-start.2 = ((bf16[4,128,128]{2,1,0:T(8,128)(2,1)}), bf16[4,128,128]{2,1,0:T(8,128)(2,1)S(1)}, u32[]{:S(2)}, u32[]{:S(2)}) async-start(bf16[4,128,128]{2,1,0:T(8,128)(2,1)} %gated_norm.1), calls=%async_computation.2 | async-start | bytes 262144 | tf_op jit(solution)/shard_map/all_to_all | solution.py:420
  46.9 8.5 %collective-permute-start.5 = (bf16[64,2048]{1,0:T(8,128)(2,1)S(1)}, bf16[64,2048]{1,0:T(8,128)(2,1)S(1)}, u32[]{:S(2)}, u32[]{:S(2)}) collective-permute-start(bf16[64,2048]{1,0:T(8,128)(2,1)S(1)} %collective-permute-done.half3_ref), channel_id=1, source_target_pairs={{0,32},{16,48},{32,0},{48,16},{64,96},{80,112},{96,64},{112,80},{1... | collective-permute-start | bytes 786440 | tf_op jit(solution)/shard_map/ppermute | solution.py:419
  56.2 5.2 %collective-permute-start.6 = (bf16[64,2048]{1,0:T(8,128)(2,1)S(1)}, bf16[64,2048]{1,0:T(8,128)(2,1)S(1)}, u32[]{:S(2)}, u32[]{:S(2)}) collective-permute-start(bf16[64,2048]{1,0:T(8,128)(2,1)S(1)} %get-tuple-element.34), channel_id=1, source_target_pairs={{0,16},{16,0},{32,48},{48,32},{64,80},{80,64},{96,112},{112,96},{1... | collective-permute-start | bytes 786440 | tf_op jit(solution)/shard_map/ppermute | solution.py:432

commit v7 on v6

--- a/solution.py
+++ b/solution.py
@@ -397,7 +397,6 @@
         parts,
         name="row_maps",
     )
-    half0, ahead = lax.optimization_barrier((half0, ahead))
     half3 = lax.ppermute(half0, "tp", [(j, j ^ 3) for j in range(16)])
     sideways = [(i, i ^ 2) for i in range(32)]
     near12 = jnp.stack([half1, half2])
@@ -415,7 +414,6 @@
         name="gated_norm",
     )
     close = [[token_of(g, m) for m in range(4)] for g in range(4)]
-    half3, normed = lax.optimization_barrier((half3, normed))
     side3 = lax.ppermute(half3, "ctx", sideways)
     gathered = lax.all_to_all(normed, "tp", 0, 0, axis_index_groups=close)
     half, other_half = call(

time: 91.6 us -> 94.9 us (1.036)
  the two profiles are of different devices: /device:TPU:35 before, /device:TPU:24 now
where the time goes in v7:
time: 94.9 us; the launch traced here: 94.1 us
  starting transfers between devices  36.3 us (38%)
  blocking collectives  30.9 us (33%)
  waiting for transfers between devices  15.4 us (16%)
  Pallas kernels  10.5 us (11%)
    all_to_all x1, blocking collectives, local(): shares = lax.all_to_all(partial, 'tp', 0, 0, axis_index_groups=far)  30.9 us
    pallas_call x7, Pallas kernels, call(): pl.pallas_call(kernel, out_shape=outs, in_specs=ins, out_specs=jax.tree.m...  10.5 us
    ppermute x1, waiting for transfers between devices, local(): side3 = lax.ppermute(half3, 'ctx', sideways)  9.5 us
    all_to_all x1, starting transfers between devices, local(): rows = lax.all_to_all(total, 'ctx', 0, 0, axis_index_groups=columns)  7.32 us
    ppermute x1, starting transfers between devices, local(): half2 = lax.ppermute(half0, 'tp', [(j, j ^ 2) for j in range(16)])  5.18 us
    all_to_all x1, starting transfers between devices, local(): parts = lax.all_to_all(maps, 'ctx', 0, 0, axis_index_groups=lines)  4.45 us
    ppermute x1, waiting for transfers between devices, local(): half2 = lax.ppermute(half0, 'tp', [(j, j ^ 2) for j in range(16)])  4.37 us
    ppermute x1, starting transfers between devices, local(): side12 = lax.ppermute(near12, 'ctx', sideways)  4.11 us
  transfers between devices with their start and end apart: 10, of which 3 were waited for; matrix products, arithmetic and copies ran while one was open for 0% of the time, Pallas kernels for 4%

profile of v7, /device:TPU:24, one launch (start us, length us, event | category | flops | bytes accessed | tf_op | source)
XLA Modules:
  0.0 94.1 jit_solution(4467570818713296958)
XLA Ops:
  0.0 5.4 %shard_maps.1 = (bf16[8,128,256]{2,1,0:T(8,128)(2,1)}, f32[2,256,256]{2,1,0:T(8,128)}, bf16[128,2048]{1,0:T(8,128)(2,1)}, bf16[64,2048]{1,0:T(8,128)(2,1)}) custom-call(bf16[256,128]{1,0:T(8,128)(2,1)} %k_ref.1, bf16[256,256]{1,0:T(8,128)(2,1)} %v_far.1, f32[2,256]{1,0:T(2,128)} %bitcast.10, f32[2,256]{1,0:T(2,128)} %bitcast.5, bf16[256,2048]{1,0:T(8,128)(2,1)} %weight_far.1), custom_call_target="tpu_custom_call" | custom-call | flops 1000000000 | bytes 1000 | tf_op jit(solution)/shard_map/shard_maps/pallas_call | solution.py:325
  5.4 0.0 copy-start.7
  5.4 0.0 copy-start.1
  5.4 0.0 copy-start.2
  5.4 0.0 copy-start.3
  5.4 0.0 copy-start.6
  5.4 4.4 %all-to-all-start = ((bf16[8,128,256]{2,1,0:T(8,128)(2,1)}), bf16[8,128,256]{2,1,0:T(8,128)(2,1)S(1)}, u32[]{:S(2)}, u32[]{:S(2)}) async-start(bf16[8,128,256]{2,1,0:T(8,128)(2,1)} %get-tuple-element.16), calls=%async_computation | async-start | bytes 1048576 | tf_op jit(solution)/shard_map/all_to_all | solution.py:374
  9.9 0.0 copy-done.7
  9.9 0.0 copy-start.4
  9.9 3.8 %collective-permute-start.1 = (bf16[64,2048]{1,0:T(8,128)(2,1)S(1)}, bf16[64,2048]{1,0:T(8,128)(2,1)S(1)}, u32[]{:S(2)}, u32[]{:S(2)}) collective-permute-start(bf16[64,2048]{1,0:T(8,128)(2,1)S(1)} %copy-done.7), channel_id=1, source_target_pairs={{0,1},{1,0},{2,3},{3,2},{4,5},{5,4},{6,7},{7,6},{8,9},{9,8},{10,11... | collective-permute-start | bytes 786440 | tf_op jit(solution)/shard_map/ppermute | solution.py:391
  13.7 5.2 %collective-permute-start.2 = (bf16[64,2048]{1,0:T(8,128)(2,1)S(1)}, bf16[64,2048]{1,0:T(8,128)(2,1)S(1)}, u32[]{:S(2)}, u32[]{:S(2)}) collective-permute-start(bf16[64,2048]{1,0:T(8,128)(2,1)S(1)} %copy-done.7), channel_id=1, source_target_pairs={{0,2},{1,3},{2,0},{3,1},{4,6},{5,7},{6,4},{7,5},{8,10},{9,11},{10,... | collective-permute-start | bytes 786440 | tf_op jit(solution)/shard_map/ppermute | solution.py:392
  18.9 1.9 %collective-permute-start.3 = (bf16[64,2048]{1,0:T(8,128)(2,1)S(1)}, bf16[64,2048]{1,0:T(8,128)(2,1)S(1)}, u32[]{:S(2)}, u32[]{:S(2)}) collective-permute-start(bf16[64,2048]{1,0:T(8,128)(2,1)S(1)} %copy-done.7), channel_id=1, source_target_pairs={{0,3},{1,2},{2,1},{3,0},{4,7},{5,6},{6,5},{7,4},{8,11},{9,10},{10,... | collective-permute-start | bytes 786440 | tf_op jit(solution)/shard_map/ppermute | solution.py:400
  20.9 0.0 copy-start.5
  20.9 0.0 copy-done.1
  20.9 0.0 copy-done.2
  20.9 0.0 copy-done.3
  20.9 0.0 copy-done.6
  20.9 0.0 copy-done.4
  20.9 0.6 copy-done.5
  21.5 0.7 read_parts.1
  22.2 2.0 %collective-permute-start = (bf16[3,256,128]{2,1,0:T(8,128)(2,1)S(1)}, bf16[3,256,128]{2,1,0:T(8,128)(2,1)S(1)}, u32[]{:S(2)}, u32[]{:S(2)}) collective-permute-start(bf16[3,256,128]{2,1,0:T(8,128)(2,1)S(1)} %get-tuple-element.22), channel_id=1, source_target_pairs={{0,16},{16,0},{32,48},{48,32},{64,80},{80,64},{96,112},{112,96},{1... | collective-permute-start | bytes 589832 | tf_op jit(solution)/shard_map/ppermute | solution.py:388
  24.2 0.0 all-to-all-done.parts_ref
  24.2 1.3 %row_maps.1 = (bf16[4,128,256]{2,1,0:T(8,128)(2,1)}, f32[128,256]{1,0:T(8,128)S(1)}, bf16[128,256]{1,0:T(8,128)(2,1)S(1)}) custom-call(bf16[8,128,256]{2,1,0:T(8,128)(2,1)S(1)} %all-to-all-done.parts_ref), custom_call_target="tpu_custom_call" | custom-call | flops 1000 | bytes 1000 | tf_op jit(solution)/shard_map/row_maps/pallas_call | solution.py:325
  25.6 7.3 %all-to-all-start.1 = ((bf16[4,128,256]{2,1,0:T(8,128)(2,1)}), bf16[4,128,256]{2,1,0:T(8,128)(2,1)S(1)}, u32[]{:S(2)}, u32[]{:S(2)}) async-start(bf16[4,128,256]{2,1,0:T(8,128)(2,1)} %get-tuple-element.17), calls=%async_computation.1 | async-start | bytes 524288 | tf_op jit(solution)/shard_map/all_to_all | solution.py:405
  32.9 0.0 collective-permute-done.1
  32.9 4.4 %collective-permute-done.2 = bf16[64,2048]{1,0:T(8,128)(2,1)S(1)} collective-permute-done((bf16[64,2048]{1,0:T(8,128)(2,1)S(1)}, bf16[64,2048]{1,0:T(8,128)(2,1)S(1)}, u32[]{:S(2)}, u32[]{:S(2)}) %collective-permute-start.2) | collective-permute-done | bytes 262176 | tf_op jit(solution)/shard_map/ppermute | solution.py:392
  37.3 0.1 pad_maximum_fusion.near_ref
  37.3 4.1 %collective-permute-start.4 = (bf16[2,64,2048]{2,1,0:T(8,128)(2,1)S(1)}, bf16[2,64,2048]{2,1,0:T(8,128)(2,1)S(1)}, u32[]{:S(2)}, u32[]{:S(2)}) collective-permute-start(bf16[2,64,2048]{2,1,0:T(8,128)(2,1)S(1)} %pad_maximum_fusion.near_ref), channel_id=1, source_target_pairs={{0,32},{16,48},{32,0},{48,16},{64,96},{80,112},{96,64},{112,80},{1... | collective-permute-start | bytes 1572872 | tf_op jit(solution)/shard_map/ppermute | solution.py:403
  41.4 0.0 collective-permute-done.came_ref
  41.4 0.0 all-to-all-done.1.rows_ref
  41.4 0.0 copy-start
  41.5 1.6 %gated_norm.1 = bf16[4,128,128]{2,1,0:T(8,128)(2,1)} custom-call(bf16[4,128,256]{2,1,0:T(8,128)(2,1)S(1)} %all-to-all-done.1.rows_ref, f32[128,256]{1,0:T(8,128)S(1)} %get-tuple-element.18.ahead_ref, bf16[128,256]{1,0:T(8,128)(2,1)S(1)} %get-tuple-element.19.first_ref, f32[3,256,128]{2,1,0:T(8,128)S(1)} %get-tuple-element.21.keep_ref, ...), custom_call_target="tpu_custom_call" | custom-call | flops 1000 | bytes 1000 | tf_op jit(solution)/shard_map/gated_norm/pallas_call | solution.py:325
  43.1 3.7 %all-to-all-start.2 = ((bf16[4,128,128]{2,1,0:T(8,128)(2,1)}), bf16[4,128,128]{2,1,0:T(8,128)(2,1)S(1)}, u32[]{:S(2)}, u32[]{:S(2)}) async-start(bf16[4,128,128]{2,1,0:T(8,128)(2,1)} %gated_norm.1), calls=%async_computation.2 | async-start | bytes 262144 | tf_op jit(solution)/shard_map/all_to_all | solution.py:418
  46.8 0.0 collective-permute-done.3.half3_ref
  46.8 1.9 %collective-permute-start.5 = (bf16[64,2048]{1,0:T(8,128)(2,1)S(1)}, bf16[64,2048]{1,0:T(8,128)(2,1)S(1)}, u32[]{:S(2)}, u32[]{:S(2)}) collective-permute-start(bf16[64,2048]{1,0:T(8,128)(2,1)S(1)} %collective-permute-done.3.half3_ref), channel_id=1, source_target_pairs={{0,32},{16,48},{32,0},{48,16},{64,96},{80,112},{96,64},{112,80},{1... | collective-permute-start | bytes 786440 | tf_op jit(solution)/shard_map/ppermute | solution.py:417
  48.8 9.5 %collective-permute-done.5.side3_ref = bf16[64,2048]{1,0:T(8,128)(2,1)S(1)} collective-permute-done((bf16[64,2048]{1,0:T(8,128)(2,1)S(1)}, bf16[64,2048]{1,0:T(8,128)(2,1)S(1)}, u32[]{:S(2)}, u32[]{:S(2)}) %collective-permute-start.5) | collective-permute-done | bytes 262176 | tf_op jit(solution)/shard_map/ppermute | solution.py:417
  58.3 0.0 collective-permute-done.4.side_ref
  58.3 0.0 all-to-all-done.2.normed_ref
  58.3 0.0 copy-done
  58.3 0.8 project.1
  59.0 1.9 %collective-permute-start.6 = (bf16[64,2048]{1,0:T(8,128)(2,1)S(1)}, bf16[64,2048]{1,0:T(8,128)(2,1)S(1)}, u32[]{:S(2)}, u32[]{:S(2)}) collective-permute-start(bf16[64,2048]{1,0:T(8,128)(2,1)S(1)} %get-tuple-element.26), channel_id=1, source_target_pairs={{0,16},{16,0},{32,48},{48,32},{64,80},{80,64},{96,112},{112,96},{1... | collective-permute-start | bytes 786440 | tf_op jit(solution)/shard_map/ppermute | solution.py:430
  61.0 1.5 %collective-permute-done.6.came_ref = bf16[64,2048]{1,0:T(8,128)(2,1)S(1)} collective-permute-done((bf16[64,2048]{1,0:T(8,128)(2,1)S(1)}, bf16[64,2048]{1,0:T(8,128)(2,1)S(1)}, u32[]{:S(2)}, u32[]{:S(2)}) %collective-permute-start.6) | collective-permute-done | bytes 262176 | tf_op jit(solution)/shard_map/ppermute | solution.py:430
  62.5 30.9 %all_to_all.20.parts_ref = bf16[4,16,2048]{2,1,0:T(8,128)(2,1)S(1)} all-to-all(bf16[4,16,2048]{2,1,0:T(8,128)(2,1)S(1)} %join.1), channel_id=1, replica_groups={{0,4,11,15},{1,5,10,14},{2,6,9,13},{3,7,8,12},{16,20,27,31},{17,21,26,3..., dimensions={0} | all-to-all | bytes 524288 | tf_op jit(solution)/shard_map/all_to_all | solution.py:433
  93.4 0.7 sum_shares.1
  (1 shorter events, 0.0 us)
Async XLA Ops:
  5.4 4.5 %copy-start.7 = (bf16[64,2048]{1,0:T(8,128)(2,1)S(1)}, bf16[64,2048]{1,0:T(8,128)(2,1)}, u32[]{:S(2)}) copy-start(bf16[64,2048]{1,0:T(8,128)(2,1)} %get-tuple-element.24) | copy-start | bytes 786436
  5.4 15.5 %copy-start.1 = (bf16[256,256]{1,0:T(8,128)(2,1)S(1)}, bf16[256,256]{1,0:T(8,128)(2,1)}, u32[]{:S(2)}) copy-start(bf16[256,256]{1,0:T(8,128)(2,1)} %gate_ref.1) | copy-start | bytes 393220
  5.4 15.5 %copy-start.2 = (bf16[256,128]{1,0:T(8,128)(2,1)S(1)}, bf16[256,128]{1,0:T(8,128)(2,1)}, u32[]{:S(2)}) copy-start(bf16[256,128]{1,0:T(8,128)(2,1)} %k_ref.1) | copy-start | bytes 196612
  5.4 15.5 %copy-start.3 = (bf16[256,128]{1,0:T(8,128)(2,1)S(1)}, bf16[256,128]{1,0:T(8,128)(2,1)}, u32[]{:S(2)}) copy-start(bf16[256,128]{1,0:T(8,128)(2,1)} %q_ref.1) | copy-start | bytes 196612
  5.4 15.5 %copy-start.6 = (f32[2,256,256]{2,1,0:T(8,128)S(1)}, f32[2,256,256]{2,1,0:T(8,128)}, u32[]{:S(2)}) copy-start(f32[2,256,256]{2,1,0:T(8,128)} %get-tuple-element.20.solved_ref) | copy-start | bytes 1572868
  5.4 18.8 %all-to-all-start = ((bf16[8,128,256]{2,1,0:T(8,128)(2,1)}), bf16[8,128,256]{2,1,0:T(8,128)(2,1)S(1)}, u32[]{:S(2)}, u32[]{:S(2)}) async-start(bf16[8,128,256]{2,1,0:T(8,128)(2,1)} %get-tuple-element.16), calls=%async_computation | async-start | bytes 1048576 | tf_op jit(solution)/shard_map/all_to_all | solution.py:374
  9.9 11.0 %copy-start.4 = (f32[256,2]{0,1:T(2,128)S(1)}, f32[256,2]{0,1:T(2,128)}, u32[]{:S(2)}) copy-start(f32[256,2]{0,1:T(2,128)} %param.13) | copy-start | bytes 6148
  9.9 23.0 %collective-permute-start.1 = (bf16[64,2048]{1,0:T(8,128)(2,1)S(1)}, bf16[64,2048]{1,0:T(8,128)(2,1)S(1)}, u32[]{:S(2)}, u32[]{:S(2)}) collective-permute-start(bf16[64,2048]{1,0:T(8,128)(2,1)S(1)} %copy-done.7), channel_id=1, source_target_pairs={{0,1},{1,0},{2,3},{3,2},{4,5},{5,4},{6,7},{7,6},{8,9},{9,8},{10,11... | collective-permute-start | bytes 786440 | tf_op jit(solution)/shard_map/ppermute | solution.py:391
  13.7 23.5 %collective-permute-start.2 = (bf16[64,2048]{1,0:T(8,128)(2,1)S(1)}, bf16[64,2048]{1,0:T(8,128)(2,1)S(1)}, u32[]{:S(2)}, u32[]{:S(2)}) collective-permute-start(bf16[64,2048]{1,0:T(8,128)(2,1)S(1)} %copy-done.7), channel_id=1, source_target_pairs={{0,2},{1,3},{2,0},{3,1},{4,6},{5,7},{6,4},{7,5},{8,10},{9,11},{10,... | collective-permute-start | bytes 786440 | tf_op jit(solution)/shard_map/ppermute | solution.py:392
  18.9 27.9 %collective-permute-start.3 = (bf16[64,2048]{1,0:T(8,128)(2,1)S(1)}, bf16[64,2048]{1,0:T(8,128)(2,1)S(1)}, u32[]{:S(2)}, u32[]{:S(2)}) collective-permute-start(bf16[64,2048]{1,0:T(8,128)(2,1)S(1)} %copy-done.7), channel_id=1, source_target_pairs={{0,3},{1,2},{2,1},{3,0},{4,7},{5,6},{6,5},{7,4},{8,11},{9,10},{10,... | collective-permute-start | bytes 786440 | tf_op jit(solution)/shard_map/ppermute | solution.py:400
  20.9 0.7 copy-start.5
  22.2 19.2 %collective-permute-start = (bf16[3,256,128]{2,1,0:T(8,128)(2,1)S(1)}, bf16[3,256,128]{2,1,0:T(8,128)(2,1)S(1)}, u32[]{:S(2)}, u32[]{:S(2)}) collective-permute-start(bf16[3,256,128]{2,1,0:T(8,128)(2,1)S(1)} %get-tuple-element.22), channel_id=1, source_target_pairs={{0,16},{16,0},{32,48},{48,32},{64,80},{80,64},{96,112},{112,96},{1... | collective-permute-start | bytes 589832 | tf_op jit(solution)/shard_map/ppermute | solution.py:388
  25.6 15.9 %all-to-all-start.1 = ((bf16[4,128,256]{2,1,0:T(8,128)(2,1)}), bf16[4,128,256]{2,1,0:T(8,128)(2,1)S(1)}, u32[]{:S(2)}, u32[]{:S(2)}) async-start(bf16[4,128,256]{2,1,0:T(8,128)(2,1)} %get-tuple-element.17), calls=%async_computation.1 | async-start | bytes 524288 | tf_op jit(solution)/shard_map/all_to_all | solution.py:405
  37.3 20.9 %collective-permute-start.4 = (bf16[2,64,2048]{2,1,0:T(8,128)(2,1)S(1)}, bf16[2,64,2048]{2,1,0:T(8,128)(2,1)S(1)}, u32[]{:S(2)}, u32[]{:S(2)}) collective-permute-start(bf16[2,64,2048]{2,1,0:T(8,128)(2,1)S(1)} %pad_maximum_fusion.near_ref), channel_id=1, source_target_pairs={{0,32},{16,48},{32,0},{48,16},{64,96},{80,112},{96,64},{112,80},{1... | collective-permute-start | bytes 1572872 | tf_op jit(solution)/shard_map/ppermute | solution.py:403
  41.4 16.8 %copy-start = (bf16[128,2048]{1,0:T(8,128)(2,1)S(1)}, bf16[128,2048]{1,0:T(8,128)(2,1)}, u32[]{:S(2)}) copy-start(bf16[128,2048]{1,0:T(8,128)(2,1)} %get-tuple-element.23.own_ref) | copy-start | bytes 1572868
  43.1 15.2 %all-to-all-start.2 = ((bf16[4,128,128]{2,1,0:T(8,128)(2,1)}), bf16[4,128,128]{2,1,0:T(8,128)(2,1)S(1)}, u32[]{:S(2)}, u32[]{:S(2)}) async-start(bf16[4,128,128]{2,1,0:T(8,128)(2,1)} %gated_norm.1), calls=%async_computation.2 | async-start | bytes 262144 | tf_op jit(solution)/shard_map/all_to_all | solution.py:418
  46.8 11.4 %collective-permute-start.5 = (bf16[64,2048]{1,0:T(8,128)(2,1)S(1)}, bf16[64,2048]{1,0:T(8,128)(2,1)S(1)}, u32[]{:S(2)}, u32[]{:S(2)}) collective-permute-start(bf16[64,2048]{1,0:T(8,128)(2,1)S(1)} %collective-permute-done.3.half3_ref), channel_id=1, source_target_pairs={{0,32},{16,48},{32,0},{48,16},{64,96},{80,112},{96,64},{112,80},{1... | collective-permute-start | bytes 786440 | tf_op jit(solution)/shard_map/ppermute | solution.py:417
  59.0 3.4 %collective-permute-start.6 = (bf16[64,2048]{1,0:T(8,128)(2,1)S(1)}, bf16[64,2048]{1,0:T(8,128)(2,1)S(1)}, u32[]{:S(2)}, u32[]{:S(2)}) collective-permute-start(bf16[64,2048]{1,0:T(8,128)(2,1)S(1)} %get-tuple-element.26), channel_id=1, source_target_pairs={{0,16},{16,0},{32,48},{48,32},{64,80},{80,64},{96,112},{112,96},{1... | collective-permute-start | bytes 786440 | tf_op jit(solution)/shard_map/ppermute | solution.py:430

commit v8 on v4

--- a/solution.py
+++ b/solution.py
@@ -87,14 +87,18 @@
     decay_ref,
     sems,
 ):
-    rows = half_ref.shape[0]
-    begin = pl.multiple_of(places()[2] * rows, rows)
+    _, x, core = places()
+    rows, columns = half_ref.shape
+    begin = pl.multiple_of(core * rows, rows)
+    left = pl.multiple_of((x % 2) * columns, columns)
     copies = [
         pltpu.make_async_copy(k_far, k_ref, sems.at[0]),
         pltpu.make_async_copy(decay_far, decay_ref, sems.at[1]),
         pltpu.make_async_copy(rate_far, rate_ref, sems.at[2]),
         pltpu.make_async_copy(v_far, v_ref, sems.at[3]),
-        pltpu.make_async_copy(weight_far.at[pl.ds(begin, rows)], half_ref, sems.at[4]),
+        pltpu.make_async_copy(
+            weight_far.at[pl.ds(begin, rows), pl.ds(left, columns)], half_ref, sems.at[4]
+        ),
     ]
     for copy in copies:
         copy.start()
@@ -264,32 +268,40 @@
             for group in range(4):
                 source = 16 * token_of(group, label)
                 target = 64 * shard + 16 * group
-                out_ref[label, target : target + 16] = shards[shard][source : source + 16]
+                piece = shards[shard][source : source + 16]
+                for side in range(2):
+                    out_ref[4 * side + label, target : target + 16] = piece
 
 
 def project_kernel(normed_ref, w0_ref, w1_ref, w2_ref, w3_ref, keep_ref, send_ref):
-    core = places()[2]
+    _, _, core = places()
     along = lax.axis_index("tp")
-    total = None
-    for i, weight_ref in enumerate((w0_ref, w1_ref, w2_ref, w3_ref)):
-        near = (along % 4) ^ i
-        term = dot(normed_ref[jnp.where(along < 8, near, 3 - near)], weight_ref[...])
-        total = term if total is None else total + term
-    keep_ref[...] = jnp.where(core == 0, total[:64], total[64:])
-    send_ref[...] = jnp.where(core == 0, total[64:], total[:64]).astype(BF)
+    weights = [ref[...] for ref in (w0_ref, w1_ref, w2_ref, w3_ref)]
+    for side in range(2):
+        total = None
+        for i, weight in enumerate(weights):
+            near = (along % 4) ^ i
+            label = jnp.where(along < 8, near, 3 - near)
+            term = dot(normed_ref[4 * side + label], weight)
+            total = term if total is None else total + term
+        keep_ref[side] = jnp.where(core == 0, total[:64], total[64:])
+        send_ref[side] = jnp.where(core == 0, total[64:], total[:64]).astype(BF)
 
 
 def join_kernel(keep_ref, came_ref, out_ref):
-    total = (keep_ref[...] + came_ref[...].astype(F32)).astype(BF)
-    for group in range(4):
-        out_ref[group] = total[16 * group : 16 * (group + 1)]
+    for side in range(2):
+        total = (keep_ref[side] + came_ref[side].astype(F32)).astype(BF)
+        for group in range(4):
+            out_ref[4 * side + group] = total[16 * group : 16 * (group + 1)]
 
 
 def sum_kernel(parts_ref, out_ref):
-    total = parts_ref[0].astype(F32)
-    for group in range(1, 4):
-        total = total + parts_ref[group].astype(F32)
-    out_ref[...] = total.astype(BF)
+    columns = parts_ref.shape[2]
+    for side in range(2):
+        total = parts_ref[4 * side].astype(F32)
+        for group in range(1, 4):
+            total = total + parts_ref[4 * side + group].astype(F32)
+        out_ref[:, side * columns : (side + 1) * columns] = total.astype(BF)
 
 
 def places():
@@ -305,7 +317,7 @@
     return pl.BlockSpec(memory_space=pltpu.HBM)
 
 
-def call(kernel, outs, *args, flops=10**8, name=None, ins=None, out_specs=None, scratch=(), room=32):
+def call(kernel, outs, *args, flops=10**3, name=None, ins=None, out_specs=None, scratch=(), room=32):
     if ins is None:
         ins = [in_vmem()] * len(args)
     return pl.pallas_call(
@@ -315,7 +327,7 @@
         out_specs=jax.tree.map(lambda _: in_vmem(), outs) if out_specs is None else out_specs,
         scratch_shapes=scratch,
         compiler_params=pltpu.CompilerParams(vmem_limit_bytes=room * 1024 * 1024),
-        cost_estimate=pl.CostEstimate(flops=flops, bytes_accessed=10**6, transcendentals=0),
+        cost_estimate=pl.CostEstimate(flops=flops, bytes_accessed=10**3, transcendentals=0),
         name=name,
     )(*args)
 
@@ -328,6 +340,7 @@
     queries, key_vectors, value_vectors, output_gate, write_rate, log_decay, norm_gain, out_weight
 ):
     width = out_weight.shape[1]
+    half_width = width // 2
     rate, decay = write_rate.T, log_decay.T
 
     maps, solved, w0 = call(
@@ -335,7 +348,7 @@
         (
             shape((8, DK, DK + DV), BF),
             shape((2, TOK, DK + DV), F32),
-            shape((DV, width), BF),
+            shape((DV, half_width), BF),
         ),
         key_vectors,
         value_vectors,
@@ -381,11 +394,14 @@
         parts,
         name="row_maps",
     )
+    w2, ahead = lax.optimization_barrier((w2, ahead))
+    w3 = lax.ppermute(w2, "tp", [(j, j ^ 1) for j in range(16)])
     columns = [[8 * y + i for y in range(4)] for i in range(8)]
     rows = lax.all_to_all(total, "ctx", 0, 0, axis_index_groups=columns)
+    rows, w1 = lax.optimization_barrier((rows, w1))
     normed = call(
         out_kernel,
-        shape((4, 128, DV), BF),
+        shape((8, 128, DV), BF),
         rows,
         ahead,
         first,
@@ -393,13 +409,18 @@
         came,
         name="gated_norm",
     )
-    w2, normed = lax.optimization_barrier((w2, normed))
-    w3 = lax.ppermute(w2, "tp", [(j, j ^ 1) for j in range(16)])
-    close = [[token_of(g, m) for m in range(4)] for g in range(4)]
-    gathered = lax.all_to_all(normed, "tp", 0, 0, axis_index_groups=close)
-    half, other_half = call(
+    pairs = [[8 * y + 4 * pair + 2 * side + core for side in range(2)]
+             for y in range(4) for pair in range(2) for core in range(2)]
+    close = [[16 * at + token_of(g, m) for at in pair for m in range(4)]
+             for pair in pairs for g in range(4)]
+    far = [[16 * at + token_of(g, m) for at in pair for g in range(4)]
+           for pair in pairs for m in range(4)]
+    both = ("ctx", "tp")
+    normed, w3 = lax.optimization_barrier((normed, w3))
+    gathered = lax.all_to_all(normed, both, 0, 0, axis_index_groups=close)
+    part, other_part = call(
         project_kernel,
-        (shape((64, width), F32), shape((64, width), BF)),
+        (shape((2, 64, half_width), F32), shape((2, 64, half_width), BF)),
         gathered,
         w0,
         w1,
@@ -407,10 +428,9 @@
         w3,
         name="project",
     )
-    other_half = lax.ppermute(other_half, "ctx", across)
-    partial = call(join_kernel, shape((4, 16, width), BF), half, other_half, name="join")
-    far = [[token_of(g, m) for g in range(4)] for m in range(4)]
-    shares = lax.all_to_all(partial, "tp", 0, 0, axis_index_groups=far)
+    other_part = lax.ppermute(other_part, "ctx", across)
+    partial = call(join_kernel, shape((8, 16, half_width), BF), part, other_part, name="join")
+    shares = lax.all_to_all(partial, both, 0, 0, axis_index_groups=far)
     return call(sum_kernel, shape((16, width), BF), shares, name="sum_shares")
 
 

time: 101 us -> 87.9 us (0.87)
  waiting for transfers between devices: 25.1 us -> 5.92 us
  blocking collectives: 31.5 us -> 43.3 us
  starting transfers between devices: 31.1 us -> 27.7 us
  local copies, waits for them, and re-layouts: 1.68 us -> 0.62 us
    all_to_all x1 -> x0, waiting for transfers between devices: 12.9 us -> none  [local(): gathered = lax.all_to_all(normed, 'tp', 0, 0, axis_index_groups=close)]
    all_to_all x1 -> x2, blocking collectives: 31.5 us -> 43.3 us  [the longest x1 29.7 us: local(): shares = lax.all_to_all(partial, both, 0, 0, axis_index_groups=far)]
    all_to_all x1 -> x0, starting transfers between devices: 4.7 us -> none  [local(): gathered = lax.all_to_all(normed, 'tp', 0, 0, axis_index_groups=close)]
    ppermute x1, waiting for transfers between devices: 4.29 us -> 0.01 us  [local(): w1 = lax.ppermute(w0, 'tp', [(j, j ^ 1) for j in range(16)])]
    ppermute x1, waiting for transfers between devices: 3.15 us -> 0.01 us  [local(): w2 = lax.ppermute(w0, 'tp', [(j, j ^ 2) for j in range(16)])]
    all_to_all x1, waiting for transfers between devices: 2.75 us -> 0.01 us  [local(): rows = lax.all_to_all(total, 'ctx', 0, 0, axis_index_groups=columns)]
    ppermute x1, starting transfers between devices: 1.91 us -> 3.83 us  [local(): w1 = lax.ppermute(w0, 'tp', [(j, j ^ 1) for j in range(16)])]
    ppermute x1, waiting for transfers between devices: 0.01 us -> 1.83 us  [local(): w3 = lax.ppermute(w2, 'tp', [(j, j ^ 1) for j in range(16)])]
  transfers between devices with their start and end apart: 8 -> 7, of which waited for: 6 -> 4; matrix products, arithmetic and copies ran while one was open for 0% -> 0% of each run, Pallas kernels for 4% -> 3%
where the time goes in v8:
time: 87.9 us; the launch traced here: 87.3 us
  blocking collectives  43.3 us (49%)
  starting transfers between devices  27.7 us (32%)
  Pallas kernels  9.61 us (11%)
  waiting for transfers between devices  5.92 us (7%)
    all_to_all x1, blocking collectives, local(): shares = lax.all_to_all(partial, both, 0, 0, axis_index_groups=far)  29.7 us
    all_to_all x1, blocking collectives, local(): gathered = lax.all_to_all(normed, both, 0, 0, axis_index_groups=close)  13.7 us
    pallas_call x7, Pallas kernels, call(): pl.pallas_call(kernel, out_shape=outs, in_specs=ins, out_specs=jax.tree.m...  9.61 us
    all_to_all x1, starting transfers between devices, local(): rows = lax.all_to_all(total, 'ctx', 0, 0, axis_index_groups=columns)  8.22 us
    ppermute x1, starting transfers between devices, local(): w2 = lax.ppermute(w0, 'tp', [(j, j ^ 2) for j in range(16)])  5.3 us
    all_to_all x1, starting transfers between devices, local(): parts = lax.all_to_all(maps, 'ctx', 0, 0, axis_index_groups=lines)  4.45 us
    ppermute x1, starting transfers between devices, local(): w1 = lax.ppermute(w0, 'tp', [(j, j ^ 1) for j in range(16)])  3.83 us
    ppermute x1, starting transfers between devices, local(): w3 = lax.ppermute(w2, 'tp', [(j, j ^ 1) for j in range(16)])  2.04 us
  transfers between devices with their start and end apart: 7, of which 4 were waited for; matrix products, arithmetic and copies ran while one was open for 0% of the time, Pallas kernels for 3%

profile of v8, /device:TPU:24, one launch (start us, length us, event | category | flops | bytes accessed | tf_op | source)
XLA Modules:
  0.0 87.3 jit_solution(6626033984631065908)
XLA Ops:
  0.0 5.2 %shard_maps.1 = (bf16[8,128,256]{2,1,0:T(8,128)(2,1)}, f32[2,256,256]{2,1,0:T(8,128)}, bf16[128,1024]{1,0:T(8,128)(2,1)}) custom-call(bf16[256,128]{1,0:T(8,128)(2,1)} %k_ref.1, bf16[256,256]{1,0:T(8,128)(2,1)} %v_far.1, f32[2,256]{1,0:T(2,128)} %bitcast.6, f32[2,256]{1,0:T(2,128)} %bitcast.3, bf16[256,2048]{1,0:T(8,128)(2,1)} %weight_far.1), custom_call_target="tpu_custom_call" | custom-call | flops 1000000000 | bytes 1000 | tf_op jit(solution)/shard_map/shard_maps/pallas_call | solution.py:323
  5.2 0.0 copy-start
  5.2 4.5 %all-to-all-start = ((bf16[8,128,256]{2,1,0:T(8,128)(2,1)}), bf16[8,128,256]{2,1,0:T(8,128)(2,1)S(1)}, u32[]{:S(2)}, u32[]{:S(2)}) async-start(bf16[8,128,256]{2,1,0:T(8,128)(2,1)} %get-tuple-element.21), calls=%async_computation | async-start | bytes 1048576 | tf_op jit(solution)/shard_map/all_to_all | solution.py:372
  9.7 0.0 copy-done
  9.7 0.0 copy-start.6
  9.7 5.3 %collective-permute-start.1 = (bf16[128,1024]{1,0:T(8,128)(2,1)S(1)}, bf16[128,1024]{1,0:T(8,128)(2,1)S(1)}, u32[]{:S(2)}, u32[]{:S(2)}) collective-permute-start(bf16[128,1024]{1,0:T(8,128)(2,1)S(1)} %copy-done), channel_id=1, source_target_pairs={{0,2},{1,3},{2,0},{3,1},{4,6},{5,7},{6,4},{7,5},{8,10},{9,11},{10,... | collective-permute-start | bytes 786440 | tf_op jit(solution)/shard_map/ppermute | solution.py:389
  15.0 3.8 %collective-permute-start = (bf16[128,1024]{1,0:T(8,128)(2,1)S(1)}, bf16[128,1024]{1,0:T(8,128)(2,1)S(1)}, u32[]{:S(2)}, u32[]{:S(2)}) collective-permute-start(bf16[128,1024]{1,0:T(8,128)(2,1)S(1)} %copy-done), channel_id=1, source_target_pairs={{0,1},{1,0},{2,3},{3,2},{4,5},{5,4},{6,7},{7,6},{8,9},{9,8},{10,11... | collective-permute-start | bytes 786440 | tf_op jit(solution)/shard_map/ppermute | solution.py:388
  18.8 1.2 %all-to-all-done.parts_ref = bf16[8,128,256]{2,1,0:T(8,128)(2,1)S(1)} async-done(((bf16[8,128,256]{2,1,0:T(8,128)(2,1)}), bf16[8,128,256]{2,1,0:T(8,128)(2,1)S(1)}, u32[]{:S(2)}, u32[]{:S(2)}) %all-to-all-start) | async-done | bytes 524320 | tf_op jit(solution)/shard_map/all_to_all | solution.py:372
  20.0 1.3 %row_maps.1 = (bf16[4,128,256]{2,1,0:T(8,128)(2,1)}, f32[128,256]{1,0:T(8,128)S(1)}, bf16[128,256]{1,0:T(8,128)(2,1)S(1)}) custom-call(bf16[8,128,256]{2,1,0:T(8,128)(2,1)S(1)} %all-to-all-done.parts_ref), custom_call_target="tpu_custom_call" | custom-call | flops 1000 | bytes 1000 | tf_op jit(solution)/shard_map/row_maps/pallas_call | solution.py:323
  21.3 0.0 copy-start.1
  21.3 0.0 copy-start.2
  21.3 0.0 copy-start.3
  21.3 8.2 %all-to-all-start.1 = ((bf16[4,128,256]{2,1,0:T(8,128)(2,1)}), bf16[4,128,256]{2,1,0:T(8,128)(2,1)S(1)}, u32[]{:S(2)}, u32[]{:S(2)}) async-start(bf16[4,128,256]{2,1,0:T(8,128)(2,1)} %get-tuple-element.22), calls=%async_computation.1 | async-start | bytes 524288 | tf_op jit(solution)/shard_map/all_to_all | solution.py:400
  29.6 0.0 collective-permute-done.1.w2_ref
  29.6 0.0 copy-start.4
  29.6 2.0 %collective-permute-start.3 = (bf16[128,1024]{1,0:T(8,128)(2,1)S(1)}, bf16[128,1024]{1,0:T(8,128)(2,1)S(1)}, u32[]{:S(2)}, u32[]{:S(2)}) collective-permute-start(bf16[128,1024]{1,0:T(8,128)(2,1)S(1)} %collective-permute-done.1.w2_ref), channel_id=1, source_target_pairs={{0,1},{1,0},{2,3},{3,2},{4,5},{5,4},{6,7},{7,6},{8,9},{9,8},{10,11... | collective-permute-start | bytes 786440 | tf_op jit(solution)/shard_map/ppermute | solution.py:398
  31.6 0.0 copy-start.5
  31.6 0.0 copy-done.6
  31.6 0.0 copy-done.1
  31.6 0.0 copy-done.2
  31.7 0.0 copy-done.3
  31.7 0.0 copy-done.4
  31.7 0.6 copy-done.5
  32.3 0.7 read_parts.1
  33.0 1.9 %collective-permute-start.2 = (bf16[3,256,128]{2,1,0:T(8,128)(2,1)S(1)}, bf16[3,256,128]{2,1,0:T(8,128)(2,1)S(1)}, u32[]{:S(2)}, u32[]{:S(2)}) collective-permute-start(bf16[3,256,128]{2,1,0:T(8,128)(2,1)S(1)} %get-tuple-element.30), channel_id=1, source_target_pairs={{0,16},{16,0},{32,48},{48,32},{64,80},{80,64},{96,112},{112,96},{1... | collective-permute-start | bytes 589832 | tf_op jit(solution)/shard_map/ppermute | solution.py:386
  34.9 0.0 collective-permute-done.w1_ref
  34.9 0.0 all-to-all-done.1.rows_ref
  34.9 1.4 %collective-permute-done.2.came_ref = bf16[3,256,128]{2,1,0:T(8,128)(2,1)S(1)} collective-permute-done((bf16[3,256,128]{2,1,0:T(8,128)(2,1)S(1)}, bf16[3,256,128]{2,1,0:T(8,128)(2,1)S(1)}, u32[]{:S(2)}, u32[]{:S(2)}) %collective-permute-start.2) | collective-permute-done | bytes 196640 | tf_op jit(solution)/shard_map/ppermute | solution.py:386
  36.3 1.0 %gated_norm.1 = bf16[8,128,128]{2,1,0:T(8,128)(2,1)S(1)} custom-call(bf16[4,128,256]{2,1,0:T(8,128)(2,1)S(1)} %all-to-all-done.1.rows_ref, f32[128,256]{1,0:T(8,128)S(1)} %get-tuple-element.26.ahead_ref, bf16[128,256]{1,0:T(8,128)(2,1)S(1)} %get-tuple-element.27.first_ref, f32[3,256,128]{2,1,0:T(8,128)S(1)} %get-tuple-element.29.keep_ref, ...), custom_call_target="tpu_custom_call" | custom-call | flops 1000 | bytes 1000 | tf_op jit(solution)/shard_map/gated_norm/pallas_call | solution.py:323
  37.3 1.8 %collective-permute-done.3.w3_ref = bf16[128,1024]{1,0:T(8,128)(2,1)S(1)} collective-permute-done((bf16[128,1024]{1,0:T(8,128)(2,1)S(1)}, bf16[128,1024]{1,0:T(8,128)(2,1)S(1)}, u32[]{:S(2)}, u32[]{:S(2)}) %collective-permute-start.3) | collective-permute-done | bytes 262176 | tf_op jit(solution)/shard_map/ppermute | solution.py:398
  39.1 13.7 %all_to_all.20.normed_ref = bf16[8,128,128]{2,1,0:T(8,128)(2,1)S(1)} all-to-all(bf16[8,128,128]{2,1,0:T(8,128)(2,1)S(1)} %gated_norm.1), channel_id=1, replica_groups={{0,1,2,3,32,33,34,35},{4,5,6,7,36,37,38,39},{11,10,9,8,43,42,41,40},{15..., dimensions={0} | all-to-all | bytes 524288 | tf_op jit(solution)/shard_map/all_to_all | solution.py:420
  52.8 0.7 project.1
  53.5 1.9 %collective-permute-start.4 = (bf16[2,64,1024]{2,1,0:T(8,128)(2,1)S(1)}, bf16[2,64,1024]{2,1,0:T(8,128)(2,1)S(1)}, u32[]{:S(2)}, u32[]{:S(2)}) collective-permute-start(bf16[2,64,1024]{2,1,0:T(8,128)(2,1)S(1)} %get-tuple-element.36), channel_id=1, source_target_pairs={{0,16},{16,0},{32,48},{48,32},{64,80},{80,64},{96,112},{112,96},{1... | collective-permute-start | bytes 786440 | tf_op jit(solution)/shard_map/ppermute | solution.py:431
  55.4 1.5 %collective-permute-done.4.came_ref = bf16[2,64,1024]{2,1,0:T(8,128)(2,1)S(1)} collective-permute-done((bf16[2,64,1024]{2,1,0:T(8,128)(2,1)S(1)}, bf16[2,64,1024]{2,1,0:T(8,128)(2,1)S(1)}, u32[]{:S(2)}, u32[]{:S(2)}) %collective-permute-start.4) | collective-permute-done | bytes 262176 | tf_op jit(solution)/shard_map/ppermute | solution.py:431
  57.0 29.7 %all_to_all.21.parts_ref = bf16[8,16,1024]{2,1,0:T(8,128)(2,1)S(1)} all-to-all(bf16[8,16,1024]{2,1,0:T(8,128)(2,1)S(1)} %join.1), channel_id=1, replica_groups={{0,4,11,15,32,36,43,47},{1,5,10,14,33,37,42,46},{2,6,9,13,34,38,41,45},..., dimensions={0} | all-to-all | bytes 524288 | tf_op jit(solution)/shard_map/all_to_all | solution.py:433
  86.7 0.7 sum_shares.1
  (1 shorter events, 0.0 us)
Async XLA Ops:
  5.2 4.5 %copy-start = (bf16[128,1024]{1,0:T(8,128)(2,1)S(1)}, bf16[128,1024]{1,0:T(8,128)(2,1)}, u32[]{:S(2)}) copy-start(bf16[128,1024]{1,0:T(8,128)(2,1)} %get-tuple-element.23.w0_ref) | copy-start | bytes 786436
  5.2 14.8 %all-to-all-start = ((bf16[8,128,256]{2,1,0:T(8,128)(2,1)}), bf16[8,128,256]{2,1,0:T(8,128)(2,1)S(1)}, u32[]{:S(2)}, u32[]{:S(2)}) async-start(bf16[8,128,256]{2,1,0:T(8,128)(2,1)} %get-tuple-element.21), calls=%async_computation | async-start | bytes 1048576 | tf_op jit(solution)/shard_map/all_to_all | solution.py:372
  9.7 22.0 %copy-start.6 = (f32[2,256,256]{2,1,0:T(8,128)S(1)}, f32[2,256,256]{2,1,0:T(8,128)}, u32[]{:S(2)}) copy-start(f32[2,256,256]{2,1,0:T(8,128)} %get-tuple-element.28.solved_ref) | copy-start | bytes 1572868
  9.7 19.9 %collective-permute-start.1 = (bf16[128,1024]{1,0:T(8,128)(2,1)S(1)}, bf16[128,1024]{1,0:T(8,128)(2,1)S(1)}, u32[]{:S(2)}, u32[]{:S(2)}) collective-permute-start(bf16[128,1024]{1,0:T(8,128)(2,1)S(1)} %copy-done), channel_id=1, source_target_pairs={{0,2},{1,3},{2,0},{3,1},{4,6},{5,7},{6,4},{7,5},{8,10},{9,11},{10,... | collective-permute-start | bytes 786440 | tf_op jit(solution)/shard_map/ppermute | solution.py:389
  15.0 19.9 %collective-permute-start = (bf16[128,1024]{1,0:T(8,128)(2,1)S(1)}, bf16[128,1024]{1,0:T(8,128)(2,1)S(1)}, u32[]{:S(2)}, u32[]{:S(2)}) collective-permute-start(bf16[128,1024]{1,0:T(8,128)(2,1)S(1)} %copy-done), channel_id=1, source_target_pairs={{0,1},{1,0},{2,3},{3,2},{4,5},{5,4},{6,7},{7,6},{8,9},{9,8},{10,11... | collective-permute-start | bytes 786440 | tf_op jit(solution)/shard_map/ppermute | solution.py:388
  21.3 10.3 %copy-start.1 = (bf16[256,256]{1,0:T(8,128)(2,1)S(1)}, bf16[256,256]{1,0:T(8,128)(2,1)}, u32[]{:S(2)}) copy-start(bf16[256,256]{1,0:T(8,128)(2,1)} %gate_ref.1) | copy-start | bytes 393220
  21.3 10.3 %copy-start.2 = (bf16[256,128]{1,0:T(8,128)(2,1)S(1)}, bf16[256,128]{1,0:T(8,128)(2,1)}, u32[]{:S(2)}) copy-start(bf16[256,128]{1,0:T(8,128)(2,1)} %k_ref.1) | copy-start | bytes 196612
  21.3 10.3 %copy-start.3 = (bf16[256,128]{1,0:T(8,128)(2,1)S(1)}, bf16[256,128]{1,0:T(8,128)(2,1)}, u32[]{:S(2)}) copy-start(bf16[256,128]{1,0:T(8,128)(2,1)} %q_ref.1) | copy-start | bytes 196612
  21.3 13.6 %all-to-all-start.1 = ((bf16[4,128,256]{2,1,0:T(8,128)(2,1)}), bf16[4,128,256]{2,1,0:T(8,128)(2,1)S(1)}, u32[]{:S(2)}, u32[]{:S(2)}) async-start(bf16[4,128,256]{2,1,0:T(8,128)(2,1)} %get-tuple-element.22), calls=%async_computation.1 | async-start | bytes 524288 | tf_op jit(solution)/shard_map/all_to_all | solution.py:400
  29.6 2.1 %copy-start.4 = (f32[256,2]{0,1:T(2,128)S(1)}, f32[256,2]{0,1:T(2,128)}, u32[]{:S(2)}) copy-start(f32[256,2]{0,1:T(2,128)} %param.13) | copy-start | bytes 6148
  29.6 9.6 %collective-permute-start.3 = (bf16[128,1024]{1,0:T(8,128)(2,1)S(1)}, bf16[128,1024]{1,0:T(8,128)(2,1)S(1)}, u32[]{:S(2)}, u32[]{:S(2)}) collective-permute-start(bf16[128,1024]{1,0:T(8,128)(2,1)S(1)} %collective-permute-done.1.w2_ref), channel_id=1, source_target_pairs={{0,1},{1,0},{2,3},{3,2},{4,5},{5,4},{6,7},{7,6},{8,9},{9,8},{10,11... | collective-permute-start | bytes 786440 | tf_op jit(solution)/shard_map/ppermute | solution.py:398
  31.6 0.7 copy-start.5
  33.0 3.3 %collective-permute-start.2 = (bf16[3,256,128]{2,1,0:T(8,128)(2,1)S(1)}, bf16[3,256,128]{2,1,0:T(8,128)(2,1)S(1)}, u32[]{:S(2)}, u32[]{:S(2)}) collective-permute-start(bf16[3,256,128]{2,1,0:T(8,128)(2,1)S(1)} %get-tuple-element.30), channel_id=1, source_target_pairs={{0,16},{16,0},{32,48},{48,32},{64,80},{80,64},{96,112},{112,96},{1... | collective-permute-start | bytes 589832 | tf_op jit(solution)/shard_map/ppermute | solution.py:386
  53.5 3.4 %collective-permute-start.4 = (bf16[2,64,1024]{2,1,0:T(8,128)(2,1)S(1)}, bf16[2,64,1024]{2,1,0:T(8,128)(2,1)S(1)}, u32[]{:S(2)}, u32[]{:S(2)}) collective-permute-start(bf16[2,64,1024]{2,1,0:T(8,128)(2,1)S(1)} %get-tuple-element.36), channel_id=1, source_target_pairs={{0,16},{16,0},{32,48},{48,32},{64,80},{80,64},{96,112},{112,96},{1... | collective-permute-start | bytes 786440 | tf_op jit(solution)/shard_map/ppermute | solution.py:431

commit v9 on v8

--- a/solution.py
+++ b/solution.py
@@ -388,6 +388,7 @@
     w1 = lax.ppermute(w0, "tp", [(j, j ^ 1) for j in range(16)])
     w2 = lax.ppermute(w0, "tp", [(j, j ^ 2) for j in range(16)])
 
+    parts, keep, send = lax.optimization_barrier((parts, keep, send))
     total, ahead, first = call(
         row_kernel,
         (shape((4, DK, DK + DV), BF), shape((DK, DK + DV), F32), shape((DK, DK + DV), BF)),
@@ -407,6 +408,7 @@
         first,
         keep,
         came,
+        flops=10**9,
         name="gated_norm",
     )
     pairs = [[8 * y + 4 * pair + 2 * side + core for side in range(2)]

time: 87.9 us -> 89.2 us (1.015)
  waiting for transfers between devices: 5.92 us -> 9.19 us
  blocking collectives: 43.3 us -> 41.7 us
    ppermute x1, waiting for transfers between devices: 1.83 us -> 6.86 us  [local(): w3 = lax.ppermute(w2, 'tp', [(j, j ^ 1) for j in range(16)])]
    ppermute x1, waiting for transfers between devices: 1.39 us -> 0.01 us  [local(): came = lax.ppermute(send, 'ctx', across)]
    all_to_all x1, blocking collectives: 13.7 us -> 12.3 us  [local(): gathered = lax.all_to_all(normed, both, 0, 0, axis_index_groups=close)]
    all_to_all x1, waiting for transfers between devices: 1.19 us -> 0.01 us  [local(): parts = lax.all_to_all(maps, 'ctx', 0, 0, axis_index_groups=lines)]
  transfers between devices with their start and end apart: 7 -> 7, of which waited for: 4 -> 3; matrix products, arithmetic and copies ran while one was open for 0% -> 0% of each run, Pallas kernels for 3% -> 3%
where the time goes in v9:
time: 89.2 us; the launch traced here: 88.5 us
  blocking collectives  41.7 us (47%)
  starting transfers between devices  27.2 us (30%)
  Pallas kernels  9.58 us (11%)
  waiting for transfers between devices  9.19 us (10%)
    all_to_all x1, blocking collectives, local(): shares = lax.all_to_all(partial, both, 0, 0, axis_index_groups=far)  29.3 us
    all_to_all x1, blocking collectives, local(): gathered = lax.all_to_all(normed, both, 0, 0, axis_index_groups=close)  12.3 us
    pallas_call x7, Pallas kernels, call(): pl.pallas_call(kernel, out_shape=outs, in_specs=ins, out_specs=jax.tree.m...  9.58 us
    all_to_all x1, starting transfers between devices, local(): rows = lax.all_to_all(total, 'ctx', 0, 0, axis_index_groups=columns)  8.02 us
    ppermute x1, waiting for transfers between devices, local(): w3 = lax.ppermute(w2, 'tp', [(j, j ^ 1) for j in range(16)])  6.86 us
    ppermute x1, starting transfers between devices, local(): w2 = lax.ppermute(w0, 'tp', [(j, j ^ 2) for j in range(16)])  5.17 us
    all_to_all x1, starting transfers between devices, local(): parts = lax.all_to_all(maps, 'ctx', 0, 0, axis_index_groups=lines)  4.45 us
    ppermute x1, starting transfers between devices, local(): w1 = lax.ppermute(w0, 'tp', [(j, j ^ 1) for j in range(16)])  3.83 us
  transfers between devices with their start and end apart: 7, of which 3 were waited for; matrix products, arithmetic and copies ran while one was open for 0% of the time, Pallas kernels for 3%

profile of v9, /device:TPU:24, one launch (start us, length us, event | category | flops | bytes accessed | tf_op | source)
XLA Modules:
  0.0 88.5 jit_solution(18166100796596003462)
XLA Ops:
  0.0 5.2 %shard_maps.1 = (bf16[8,128,256]{2,1,0:T(8,128)(2,1)}, f32[2,256,256]{2,1,0:T(8,128)}, bf16[128,1024]{1,0:T(8,128)(2,1)}) custom-call(bf16[256,128]{1,0:T(8,128)(2,1)} %k_ref.1, bf16[256,256]{1,0:T(8,128)(2,1)} %v_far.1, f32[2,256]{1,0:T(2,128)} %bitcast.6, f32[2,256]{1,0:T(2,128)} %bitcast.3, bf16[256,2048]{1,0:T(8,128)(2,1)} %weight_far.1), custom_call_target="tpu_custom_call" | custom-call | flops 1000000000 | bytes 1000 | tf_op jit(solution)/shard_map/shard_maps/pallas_call | solution.py:323
  5.2 0.0 copy-start
  5.2 0.0 copy-start.1
  5.2 0.0 copy-start.2
  5.2 0.0 copy-start.3
  5.2 0.0 copy-start.6
  5.2 4.5 %all-to-all-start = ((bf16[8,128,256]{2,1,0:T(8,128)(2,1)}), bf16[8,128,256]{2,1,0:T(8,128)(2,1)S(1)}, u32[]{:S(2)}, u32[]{:S(2)}) async-start(bf16[8,128,256]{2,1,0:T(8,128)(2,1)} %get-tuple-element.23), calls=%async_computation | async-start | bytes 1048576 | tf_op jit(solution)/shard_map/all_to_all | solution.py:372
  9.7 0.0 copy-done
  9.7 0.0 copy-start.4
  9.7 5.2 %collective-permute-start.1 = (bf16[128,1024]{1,0:T(8,128)(2,1)S(1)}, bf16[128,1024]{1,0:T(8,128)(2,1)S(1)}, u32[]{:S(2)}, u32[]{:S(2)}) collective-permute-start(bf16[128,1024]{1,0:T(8,128)(2,1)S(1)} %copy-done), channel_id=1, source_target_pairs={{0,2},{1,3},{2,0},{3,1},{4,6},{5,7},{6,4},{7,5},{8,10},{9,11},{10,... | collective-permute-start | bytes 786440 | tf_op jit(solution)/shard_map/ppermute | solution.py:389
  14.9 3.8 %collective-permute-start = (bf16[128,1024]{1,0:T(8,128)(2,1)S(1)}, bf16[128,1024]{1,0:T(8,128)(2,1)S(1)}, u32[]{:S(2)}, u32[]{:S(2)}) collective-permute-start(bf16[128,1024]{1,0:T(8,128)(2,1)S(1)} %copy-done), channel_id=1, source_target_pairs={{0,1},{1,0},{2,3},{3,2},{4,5},{5,4},{6,7},{7,6},{8,9},{9,8},{10,11... | collective-permute-start | bytes 786440 | tf_op jit(solution)/shard_map/ppermute | solution.py:388
  18.7 0.0 copy-start.5
  18.7 0.0 copy-done.1
  18.7 0.0 copy-done.2
  18.7 0.0 copy-done.3
  18.7 0.0 copy-done.6
  18.8 0.0 copy-done.4
  18.8 0.6 copy-done.5
  19.4 0.7 read_parts.1
  20.1 0.0 all-to-all-done.parts_ref
  20.1 1.3 %row_maps.1 = (bf16[4,128,256]{2,1,0:T(8,128)(2,1)}, f32[128,256]{1,0:T(8,128)S(1)}, bf16[128,256]{1,0:T(8,128)(2,1)S(1)}) custom-call(bf16[8,128,256]{2,1,0:T(8,128)(2,1)S(1)} %all-to-all-done.parts_ref), custom_call_target="tpu_custom_call" | custom-call | flops 1000 | bytes 1000 | tf_op jit(solution)/shard_map/row_maps/pallas_call | solution.py:323
  21.4 8.0 %all-to-all-start.1 = ((bf16[4,128,256]{2,1,0:T(8,128)(2,1)}), bf16[4,128,256]{2,1,0:T(8,128)(2,1)S(1)}, u32[]{:S(2)}, u32[]{:S(2)}) async-start(bf16[4,128,256]{2,1,0:T(8,128)(2,1)} %get-tuple-element.28), calls=%async_computation.1 | async-start | bytes 524288 | tf_op jit(solution)/shard_map/all_to_all | solution.py:401
  29.4 1.9 %collective-permute-start.2 = (bf16[3,256,128]{2,1,0:T(8,128)(2,1)S(1)}, bf16[3,256,128]{2,1,0:T(8,128)(2,1)S(1)}, u32[]{:S(2)}, u32[]{:S(2)}) collective-permute-start(bf16[3,256,128]{2,1,0:T(8,128)(2,1)S(1)} %get-tuple-element.26), channel_id=1, source_target_pairs={{0,16},{16,0},{32,48},{48,32},{64,80},{80,64},{96,112},{112,96},{1... | collective-permute-start | bytes 589832 | tf_op jit(solution)/shard_map/ppermute | solution.py:386
  31.4 0.0 collective-permute-done.1.w2_ref
  31.4 1.9 %collective-permute-start.3 = (bf16[128,1024]{1,0:T(8,128)(2,1)S(1)}, bf16[128,1024]{1,0:T(8,128)(2,1)S(1)}, u32[]{:S(2)}, u32[]{:S(2)}) collective-permute-start(bf16[128,1024]{1,0:T(8,128)(2,1)S(1)} %collective-permute-done.1.w2_ref), channel_id=1, source_target_pairs={{0,1},{1,0},{2,3},{3,2},{4,5},{5,4},{6,7},{7,6},{8,9},{9,8},{10,11... | collective-permute-start | bytes 786440 | tf_op jit(solution)/shard_map/ppermute | solution.py:399
  33.3 0.0 collective-permute-done.w1_ref
  33.3 0.8 all-to-all-done.1.rows_ref
  34.1 0.0 collective-permute-done.2.came_ref
  34.1 1.0 %gated_norm.1 = bf16[8,128,128]{2,1,0:T(8,128)(2,1)S(1)} custom-call(bf16[4,128,256]{2,1,0:T(8,128)(2,1)S(1)} %all-to-all-done.1.rows_ref, f32[128,256]{1,0:T(8,128)S(1)} %get-tuple-element.32.ahead_ref, bf16[128,256]{1,0:T(8,128)(2,1)S(1)} %get-tuple-element.33.first_ref, f32[3,256,128]{2,1,0:T(8,128)S(1)} %get-tuple-element.34.keep_ref, ...), custom_call_target="tpu_custom_call" | custom-call | flops 1000000000 | bytes 1000 | tf_op jit(solution)/shard_map/gated_norm/pallas_call | solution.py:323
  35.1 6.9 %collective-permute-done.3.w3_ref = bf16[128,1024]{1,0:T(8,128)(2,1)S(1)} collective-permute-done((bf16[128,1024]{1,0:T(8,128)(2,1)S(1)}, bf16[128,1024]{1,0:T(8,128)(2,1)S(1)}, u32[]{:S(2)}, u32[]{:S(2)}) %collective-permute-start.3) | collective-permute-done | bytes 262176 | tf_op jit(solution)/shard_map/ppermute | solution.py:399
  42.0 12.3 %all_to_all.20.normed_ref = bf16[8,128,128]{2,1,0:T(8,128)(2,1)S(1)} all-to-all(bf16[8,128,128]{2,1,0:T(8,128)(2,1)S(1)} %gated_norm.1), channel_id=1, replica_groups={{0,1,2,3,32,33,34,35},{4,5,6,7,36,37,38,39},{11,10,9,8,43,42,41,40},{15..., dimensions={0} | all-to-all | bytes 524288 | tf_op jit(solution)/shard_map/all_to_all | solution.py:422
  54.3 0.7 project.1
  55.0 1.9 %collective-permute-start.4 = (bf16[2,64,1024]{2,1,0:T(8,128)(2,1)S(1)}, bf16[2,64,1024]{2,1,0:T(8,128)(2,1)S(1)}, u32[]{:S(2)}, u32[]{:S(2)}) collective-permute-start(bf16[2,64,1024]{2,1,0:T(8,128)(2,1)S(1)} %get-tuple-element.40), channel_id=1, source_target_pairs={{0,16},{16,0},{32,48},{48,32},{64,80},{80,64},{96,112},{112,96},{1... | collective-permute-start | bytes 786440 | tf_op jit(solution)/shard_map/ppermute | solution.py:433
  56.9 1.5 %collective-permute-done.4.came_ref = bf16[2,64,1024]{2,1,0:T(8,128)(2,1)S(1)} collective-permute-done((bf16[2,64,1024]{2,1,0:T(8,128)(2,1)S(1)}, bf16[2,64,1024]{2,1,0:T(8,128)(2,1)S(1)}, u32[]{:S(2)}, u32[]{:S(2)}) %collective-permute-start.4) | collective-permute-done | bytes 262176 | tf_op jit(solution)/shard_map/ppermute | solution.py:433
  58.5 29.3 %all_to_all.21.parts_ref = bf16[8,16,1024]{2,1,0:T(8,128)(2,1)S(1)} all-to-all(bf16[8,16,1024]{2,1,0:T(8,128)(2,1)S(1)} %join.1), channel_id=1, replica_groups={{0,4,11,15,32,36,43,47},{1,5,10,14,33,37,42,46},{2,6,9,13,34,38,41,45},..., dimensions={0} | all-to-all | bytes 524288 | tf_op jit(solution)/shard_map/all_to_all | solution.py:435
  87.8 0.7 sum_shares.1
  (1 shorter events, 0.0 us)
Async XLA Ops:
  5.2 4.5 %copy-start = (bf16[128,1024]{1,0:T(8,128)(2,1)S(1)}, bf16[128,1024]{1,0:T(8,128)(2,1)}, u32[]{:S(2)}) copy-start(bf16[128,1024]{1,0:T(8,128)(2,1)} %get-tuple-element.29.w0_ref) | copy-start | bytes 786436
  5.2 13.5 %copy-start.1 = (bf16[256,256]{1,0:T(8,128)(2,1)S(1)}, bf16[256,256]{1,0:T(8,128)(2,1)}, u32[]{:S(2)}) copy-start(bf16[256,256]{1,0:T(8,128)(2,1)} %gate_ref.1) | copy-start | bytes 393220
  5.2 13.5 %copy-start.2 = (bf16[256,128]{1,0:T(8,128)(2,1)S(1)}, bf16[256,128]{1,0:T(8,128)(2,1)}, u32[]{:S(2)}) copy-start(bf16[256,128]{1,0:T(8,128)(2,1)} %k_ref.1) | copy-start | bytes 196612
  5.2 13.5 %copy-start.3 = (bf16[256,128]{1,0:T(8,128)(2,1)S(1)}, bf16[256,128]{1,0:T(8,128)(2,1)}, u32[]{:S(2)}) copy-start(bf16[256,128]{1,0:T(8,128)(2,1)} %q_ref.1) | copy-start | bytes 196612
  5.2 13.5 %copy-start.6 = (f32[2,256,256]{2,1,0:T(8,128)S(1)}, f32[2,256,256]{2,1,0:T(8,128)}, u32[]{:S(2)}) copy-start(f32[2,256,256]{2,1,0:T(8,128)} %get-tuple-element.24.solved_ref) | copy-start | bytes 1572868
  5.2 14.9 %all-to-all-start = ((bf16[8,128,256]{2,1,0:T(8,128)(2,1)}), bf16[8,128,256]{2,1,0:T(8,128)(2,1)S(1)}, u32[]{:S(2)}, u32[]{:S(2)}) async-start(bf16[8,128,256]{2,1,0:T(8,128)(2,1)} %get-tuple-element.23), calls=%async_computation | async-start | bytes 1048576 | tf_op jit(solution)/shard_map/all_to_all | solution.py:372
  9.7 9.1 %copy-start.4 = (f32[256,2]{0,1:T(2,128)S(1)}, f32[256,2]{0,1:T(2,128)}, u32[]{:S(2)}) copy-start(f32[256,2]{0,1:T(2,128)} %param.13) | copy-start | bytes 6148
  9.7 21.7 %collective-permute-start.1 = (bf16[128,1024]{1,0:T(8,128)(2,1)S(1)}, bf16[128,1024]{1,0:T(8,128)(2,1)S(1)}, u32[]{:S(2)}, u32[]{:S(2)}) collective-permute-start(bf16[128,1024]{1,0:T(8,128)(2,1)S(1)} %copy-done), channel_id=1, source_target_pairs={{0,2},{1,3},{2,0},{3,1},{4,6},{5,7},{6,4},{7,5},{8,10},{9,11},{10,... | collective-permute-start | bytes 786440 | tf_op jit(solution)/shard_map/ppermute | solution.py:389
  14.9 18.4 %collective-permute-start = (bf16[128,1024]{1,0:T(8,128)(2,1)S(1)}, bf16[128,1024]{1,0:T(8,128)(2,1)S(1)}, u32[]{:S(2)}, u32[]{:S(2)}) collective-permute-start(bf16[128,1024]{1,0:T(8,128)(2,1)S(1)} %copy-done), channel_id=1, source_target_pairs={{0,1},{1,0},{2,3},{3,2},{4,5},{5,4},{6,7},{7,6},{8,9},{9,8},{10,11... | collective-permute-start | bytes 786440 | tf_op jit(solution)/shard_map/ppermute | solution.py:388
  18.7 0.7 copy-start.5
  21.4 12.7 %all-to-all-start.1 = ((bf16[4,128,256]{2,1,0:T(8,128)(2,1)}), bf16[4,128,256]{2,1,0:T(8,128)(2,1)S(1)}, u32[]{:S(2)}, u32[]{:S(2)}) async-start(bf16[4,128,256]{2,1,0:T(8,128)(2,1)} %get-tuple-element.28), calls=%async_computation.1 | async-start | bytes 524288 | tf_op jit(solution)/shard_map/all_to_all | solution.py:401
  29.4 4.7 %collective-permute-start.2 = (bf16[3,256,128]{2,1,0:T(8,128)(2,1)S(1)}, bf16[3,256,128]{2,1,0:T(8,128)(2,1)S(1)}, u32[]{:S(2)}, u32[]{:S(2)}) collective-permute-start(bf16[3,256,128]{2,1,0:T(8,128)(2,1)S(1)} %get-tuple-element.26), channel_id=1, source_target_pairs={{0,16},{16,0},{32,48},{48,32},{64,80},{80,64},{96,112},{112,96},{1... | collective-permute-start | bytes 589832 | tf_op jit(solution)/shard_map/ppermute | solution.py:386
  31.4 10.6 %collective-permute-start.3 = (bf16[128,1024]{1,0:T(8,128)(2,1)S(1)}, bf16[128,1024]{1,0:T(8,128)(2,1)S(1)}, u32[]{:S(2)}, u32[]{:S(2)}) collective-permute-start(bf16[128,1024]{1,0:T(8,128)(2,1)S(1)} %collective-permute-done.1.w2_ref), channel_id=1, source_target_pairs={{0,1},{1,0},{2,3},{3,2},{4,5},{5,4},{6,7},{7,6},{8,9},{9,8},{10,11... | collective-permute-start | bytes 786440 | tf_op jit(solution)/shard_map/ppermute | solution.py:399
  55.0 3.4 %collective-permute-start.4 = (bf16[2,64,1024]{2,1,0:T(8,128)(2,1)S(1)}, bf16[2,64,1024]{2,1,0:T(8,128)(2,1)S(1)}, u32[]{:S(2)}, u32[]{:S(2)}) collective-permute-start(bf16[2,64,1024]{2,1,0:T(8,128)(2,1)S(1)} %get-tuple-element.40), channel_id=1, source_target_pairs={{0,16},{16,0},{32,48},{48,32},{64,80},{80,64},{96,112},{112,96},{1... | collective-permute-start | bytes 786440 | tf_op jit(solution)/shard_map/ppermute | solution.py:433

commit v10 on v9

--- a/solution.py
+++ b/solution.py
@@ -388,7 +388,7 @@
     w1 = lax.ppermute(w0, "tp", [(j, j ^ 1) for j in range(16)])
     w2 = lax.ppermute(w0, "tp", [(j, j ^ 2) for j in range(16)])
 
-    parts, keep, send = lax.optimization_barrier((parts, keep, send))
+    parts, keep, came = lax.optimization_barrier((parts, keep, came))
     total, ahead, first = call(
         row_kernel,
         (shape((4, DK, DK + DV), BF), shape((DK, DK + DV), F32), shape((DK, DK + DV), BF)),

time: 89.2 us -> 89.9 us (level)
  blocking collectives: 41.7 us -> 45.7 us
  starting transfers between devices: 27.2 us -> 25.3 us
  waiting for transfers between devices: 9.19 us -> 8.05 us
    ppermute x1, waiting for transfers between devices: 6.86 us -> 3.79 us  [local(): w3 = lax.ppermute(w2, 'tp', [(j, j ^ 1) for j in range(16)])]
    all_to_all x1, blocking collectives: 12.3 us -> 14.8 us  [local(): gathered = lax.all_to_all(normed, both, 0, 0, axis_index_groups=close)]
    all_to_all x1, starting transfers between devices: 8.02 us -> 5.75 us  [local(): rows = lax.all_to_all(total, 'ctx', 0, 0, axis_index_groups=columns)]
    ppermute x1, waiting for transfers between devices: 0.01 us -> 1.76 us  [local(): w1 = lax.ppermute(w0, 'tp', [(j, j ^ 1) for j in range(16)])]
    all_to_all x1, blocking collectives: 29.3 us -> 30.9 us  [local(): shares = lax.all_to_all(partial, both, 0, 0, axis_index_groups=far)]
  transfers between devices with their start and end apart: 7 -> 7, of which waited for: 3 -> 4; matrix products, arithmetic and copies ran while one was open for 0% -> 0% of each run, Pallas kernels for 3% -> 3%
where the time goes in v10:
time: 89.9 us; the launch traced here: 89.4 us
  blocking collectives  45.7 us (51%)
  starting transfers between devices  25.3 us (28%)
  Pallas kernels  9.58 us (11%)
  waiting for transfers between devices  8.05 us (9%)
    all_to_all x1, blocking collectives, local(): shares = lax.all_to_all(partial, both, 0, 0, axis_index_groups=far)  30.9 us
    all_to_all x1, blocking collectives, local(): gathered = lax.all_to_all(normed, both, 0, 0, axis_index_groups=close)  14.8 us
    pallas_call x7, Pallas kernels, call(): pl.pallas_call(kernel, out_shape=outs, in_specs=ins, out_specs=jax.tree.m...  9.58 us
    all_to_all x1, starting transfers between devices, local(): rows = lax.all_to_all(total, 'ctx', 0, 0, axis_index_groups=columns)  5.75 us
    ppermute x1, starting transfers between devices, local(): w2 = lax.ppermute(w0, 'tp', [(j, j ^ 2) for j in range(16)])  5.17 us
    all_to_all x1, starting transfers between devices, local(): parts = lax.all_to_all(maps, 'ctx', 0, 0, axis_index_groups=lines)  4.45 us
    ppermute x1, starting transfers between devices, local(): w1 = lax.ppermute(w0, 'tp', [(j, j ^ 1) for j in range(16)])  3.83 us
    ppermute x1, waiting for transfers between devices, local(): w3 = lax.ppermute(w2, 'tp', [(j, j ^ 1) for j in range(16)])  3.79 us
  transfers between devices with their start and end apart: 7, of which 4 were waited for; matrix products, arithmetic and copies ran while one was open for 0% of the time, Pallas kernels for 3%

profile of v10, /device:TPU:24, one launch (start us, length us, event | category | flops | bytes accessed | tf_op | source)
XLA Modules:
  0.0 89.4 jit_solution(6805630837780815874)
XLA Ops:
  0.0 5.2 %shard_maps.1 = (bf16[8,128,256]{2,1,0:T(8,128)(2,1)}, f32[2,256,256]{2,1,0:T(8,128)}, bf16[128,1024]{1,0:T(8,128)(2,1)}) custom-call(bf16[256,128]{1,0:T(8,128)(2,1)} %k_ref.1, bf16[256,256]{1,0:T(8,128)(2,1)} %v_far.1, f32[2,256]{1,0:T(2,128)} %bitcast.6, f32[2,256]{1,0:T(2,128)} %bitcast.3, bf16[256,2048]{1,0:T(8,128)(2,1)} %weight_far.1), custom_call_target="tpu_custom_call" | custom-call | flops 1000000000 | bytes 1000 | tf_op jit(solution)/shard_map/shard_maps/pallas_call | solution.py:323
  5.2 0.0 copy-start
  5.2 0.0 copy-start.1
  5.2 0.0 copy-start.2
  5.2 0.0 copy-start.3
  5.2 0.0 copy-start.6
  5.2 4.5 %all-to-all-start = ((bf16[8,128,256]{2,1,0:T(8,128)(2,1)}), bf16[8,128,256]{2,1,0:T(8,128)(2,1)S(1)}, u32[]{:S(2)}, u32[]{:S(2)}) async-start(bf16[8,128,256]{2,1,0:T(8,128)(2,1)} %get-tuple-element.24), calls=%async_computation | async-start | bytes 1048576 | tf_op jit(solution)/shard_map/all_to_all | solution.py:372
  9.7 0.0 copy-done
  9.7 0.0 copy-start.4
  9.7 5.2 %collective-permute-start.2 = (bf16[128,1024]{1,0:T(8,128)(2,1)S(1)}, bf16[128,1024]{1,0:T(8,128)(2,1)S(1)}, u32[]{:S(2)}, u32[]{:S(2)}) collective-permute-start(bf16[128,1024]{1,0:T(8,128)(2,1)S(1)} %copy-done), channel_id=1, source_target_pairs={{0,2},{1,3},{2,0},{3,1},{4,6},{5,7},{6,4},{7,5},{8,10},{9,11},{10,... | collective-permute-start | bytes 786440 | tf_op jit(solution)/shard_map/ppermute | solution.py:389
  14.9 0.0 copy-start.5
  14.9 0.0 copy-done.1
  14.9 0.0 copy-done.2
  14.9 0.0 copy-done.3
  14.9 0.0 copy-done.6
  14.9 0.0 copy-done.4
  14.9 0.6 copy-done.5
  15.5 0.7 read_parts.1
  16.2 2.2 %collective-permute-start = (bf16[3,256,128]{2,1,0:T(8,128)(2,1)S(1)}, bf16[3,256,128]{2,1,0:T(8,128)(2,1)S(1)}, u32[]{:S(2)}, u32[]{:S(2)}) collective-permute-start(bf16[3,256,128]{2,1,0:T(8,128)(2,1)S(1)} %get-tuple-element.27), channel_id=1, source_target_pairs={{0,16},{16,0},{32,48},{48,32},{64,80},{80,64},{96,112},{112,96},{1... | collective-permute-start | bytes 589832 | tf_op jit(solution)/shard_map/ppermute | solution.py:386
  18.5 3.8 %collective-permute-start.1 = (bf16[128,1024]{1,0:T(8,128)(2,1)S(1)}, bf16[128,1024]{1,0:T(8,128)(2,1)S(1)}, u32[]{:S(2)}, u32[]{:S(2)}) collective-permute-start(bf16[128,1024]{1,0:T(8,128)(2,1)S(1)} %copy-done), channel_id=1, source_target_pairs={{0,1},{1,0},{2,3},{3,2},{4,5},{5,4},{6,7},{7,6},{8,9},{9,8},{10,11... | collective-permute-start | bytes 786440 | tf_op jit(solution)/shard_map/ppermute | solution.py:388
  22.3 0.0 collective-permute-done.came_ref
  22.3 0.0 all-to-all-done.parts_ref
  22.4 1.3 %row_maps.1 = (bf16[4,128,256]{2,1,0:T(8,128)(2,1)}, f32[128,256]{1,0:T(8,128)S(1)}, bf16[128,256]{1,0:T(8,128)(2,1)S(1)}) custom-call(bf16[8,128,256]{2,1,0:T(8,128)(2,1)S(1)} %all-to-all-done.parts_ref), custom_call_target="tpu_custom_call" | custom-call | flops 1000 | bytes 1000 | tf_op jit(solution)/shard_map/row_maps/pallas_call | solution.py:323
  23.7 5.8 %all-to-all-start.1 = ((bf16[4,128,256]{2,1,0:T(8,128)(2,1)}), bf16[4,128,256]{2,1,0:T(8,128)(2,1)S(1)}, u32[]{:S(2)}, u32[]{:S(2)}) async-start(bf16[4,128,256]{2,1,0:T(8,128)(2,1)} %get-tuple-element.29), calls=%async_computation.1 | async-start | bytes 524288 | tf_op jit(solution)/shard_map/all_to_all | solution.py:401
  29.4 0.0 collective-permute-done.2.w2_ref
  29.4 1.9 %collective-permute-start.3 = (bf16[128,1024]{1,0:T(8,128)(2,1)S(1)}, bf16[128,1024]{1,0:T(8,128)(2,1)S(1)}, u32[]{:S(2)}, u32[]{:S(2)}) collective-permute-start(bf16[128,1024]{1,0:T(8,128)(2,1)S(1)} %collective-permute-done.2.w2_ref), channel_id=1, source_target_pairs={{0,1},{1,0},{2,3},{3,2},{4,5},{5,4},{6,7},{7,6},{8,9},{9,8},{10,11... | collective-permute-start | bytes 786440 | tf_op jit(solution)/shard_map/ppermute | solution.py:399
  31.4 1.8 %collective-permute-done.1.w1_ref = bf16[128,1024]{1,0:T(8,128)(2,1)S(1)} collective-permute-done((bf16[128,1024]{1,0:T(8,128)(2,1)S(1)}, bf16[128,1024]{1,0:T(8,128)(2,1)S(1)}, u32[]{:S(2)}, u32[]{:S(2)}) %collective-permute-start.1) | collective-permute-done | bytes 262176 | tf_op jit(solution)/shard_map/ppermute | solution.py:388
  33.1 1.0 %all-to-all-done.1.rows_ref = bf16[4,128,256]{2,1,0:T(8,128)(2,1)S(1)} async-done(((bf16[4,128,256]{2,1,0:T(8,128)(2,1)}), bf16[4,128,256]{2,1,0:T(8,128)(2,1)S(1)}, u32[]{:S(2)}, u32[]{:S(2)}) %all-to-all-start.1) | async-done | bytes 262176 | tf_op jit(solution)/shard_map/all_to_all | solution.py:401
  34.1 1.0 %gated_norm.1 = bf16[8,128,128]{2,1,0:T(8,128)(2,1)S(1)} custom-call(bf16[4,128,256]{2,1,0:T(8,128)(2,1)S(1)} %all-to-all-done.1.rows_ref, f32[128,256]{1,0:T(8,128)S(1)} %get-tuple-element.33.ahead_ref, bf16[128,256]{1,0:T(8,128)(2,1)S(1)} %get-tuple-element.34.first_ref, f32[3,256,128]{2,1,0:T(8,128)S(1)} %get-tuple-element.35.keep_ref, ...), custom_call_target="tpu_custom_call" | custom-call | flops 1000000000 | bytes 1000 | tf_op jit(solution)/shard_map/gated_norm/pallas_call | solution.py:323
  35.1 3.8 %collective-permute-done.3.w3_ref = bf16[128,1024]{1,0:T(8,128)(2,1)S(1)} collective-permute-done((bf16[128,1024]{1,0:T(8,128)(2,1)S(1)}, bf16[128,1024]{1,0:T(8,128)(2,1)S(1)}, u32[]{:S(2)}, u32[]{:S(2)}) %collective-permute-start.3) | collective-permute-done | bytes 262176 | tf_op jit(solution)/shard_map/ppermute | solution.py:399
  38.9 14.8 %all_to_all.20.normed_ref = bf16[8,128,128]{2,1,0:T(8,128)(2,1)S(1)} all-to-all(bf16[8,128,128]{2,1,0:T(8,128)(2,1)S(1)} %gated_norm.1), channel_id=1, replica_groups={{0,1,2,3,32,33,34,35},{4,5,6,7,36,37,38,39},{11,10,9,8,43,42,41,40},{15..., dimensions={0} | all-to-all | bytes 524288 | tf_op jit(solution)/shard_map/all_to_all | solution.py:422
  53.7 0.7 project.1
  54.4 1.9 %collective-permute-start.4 = (bf16[2,64,1024]{2,1,0:T(8,128)(2,1)S(1)}, bf16[2,64,1024]{2,1,0:T(8,128)(2,1)S(1)}, u32[]{:S(2)}, u32[]{:S(2)}) collective-permute-start(bf16[2,64,1024]{2,1,0:T(8,128)(2,1)S(1)} %get-tuple-element.42), channel_id=1, source_target_pairs={{0,16},{16,0},{32,48},{48,32},{64,80},{80,64},{96,112},{112,96},{1... | collective-permute-start | bytes 786440 | tf_op jit(solution)/shard_map/ppermute | solution.py:433
  56.3 1.5 %collective-permute-done.4.came_ref = bf16[2,64,1024]{2,1,0:T(8,128)(2,1)S(1)} collective-permute-done((bf16[2,64,1024]{2,1,0:T(8,128)(2,1)S(1)}, bf16[2,64,1024]{2,1,0:T(8,128)(2,1)S(1)}, u32[]{:S(2)}, u32[]{:S(2)}) %collective-permute-start.4) | collective-permute-done | bytes 262176 | tf_op jit(solution)/shard_map/ppermute | solution.py:433
  57.8 30.9 %all_to_all.21.parts_ref = bf16[8,16,1024]{2,1,0:T(8,128)(2,1)S(1)} all-to-all(bf16[8,16,1024]{2,1,0:T(8,128)(2,1)S(1)} %join.1), channel_id=1, replica_groups={{0,4,11,15,32,36,43,47},{1,5,10,14,33,37,42,46},{2,6,9,13,34,38,41,45},..., dimensions={0} | all-to-all | bytes 524288 | tf_op jit(solution)/shard_map/all_to_all | solution.py:435
  88.7 0.7 sum_shares.1
  (1 shorter events, 0.0 us)
Async XLA Ops:
  5.2 4.5 %copy-start = (bf16[128,1024]{1,0:T(8,128)(2,1)S(1)}, bf16[128,1024]{1,0:T(8,128)(2,1)}, u32[]{:S(2)}) copy-start(bf16[128,1024]{1,0:T(8,128)(2,1)} %get-tuple-element.30.w0_ref) | copy-start | bytes 786436
  5.2 9.7 %copy-start.1 = (bf16[256,256]{1,0:T(8,128)(2,1)S(1)}, bf16[256,256]{1,0:T(8,128)(2,1)}, u32[]{:S(2)}) copy-start(bf16[256,256]{1,0:T(8,128)(2,1)} %gate_ref.1) | copy-start | bytes 393220
  5.2 9.7 %copy-start.2 = (bf16[256,128]{1,0:T(8,128)(2,1)S(1)}, bf16[256,128]{1,0:T(8,128)(2,1)}, u32[]{:S(2)}) copy-start(bf16[256,128]{1,0:T(8,128)(2,1)} %k_ref.1) | copy-start | bytes 196612
  5.2 9.7 %copy-start.3 = (bf16[256,128]{1,0:T(8,128)(2,1)S(1)}, bf16[256,128]{1,0:T(8,128)(2,1)}, u32[]{:S(2)}) copy-start(bf16[256,128]{1,0:T(8,128)(2,1)} %q_ref.1) | copy-start | bytes 196612
  5.2 9.7 %copy-start.6 = (f32[2,256,256]{2,1,0:T(8,128)S(1)}, f32[2,256,256]{2,1,0:T(8,128)}, u32[]{:S(2)}) copy-start(f32[2,256,256]{2,1,0:T(8,128)} %get-tuple-element.25.solved_ref) | copy-start | bytes 1572868
  5.2 17.1 %all-to-all-start = ((bf16[8,128,256]{2,1,0:T(8,128)(2,1)}), bf16[8,128,256]{2,1,0:T(8,128)(2,1)S(1)}, u32[]{:S(2)}, u32[]{:S(2)}) async-start(bf16[8,128,256]{2,1,0:T(8,128)(2,1)} %get-tuple-element.24), calls=%async_computation | async-start | bytes 1048576 | tf_op jit(solution)/shard_map/all_to_all | solution.py:372
  9.7 5.2 %copy-start.4 = (f32[256,2]{0,1:T(2,128)S(1)}, f32[256,2]{0,1:T(2,128)}, u32[]{:S(2)}) copy-start(f32[256,2]{0,1:T(2,128)} %param.13) | copy-start | bytes 6148
  9.7 19.8 %collective-permute-start.2 = (bf16[128,1024]{1,0:T(8,128)(2,1)S(1)}, bf16[128,1024]{1,0:T(8,128)(2,1)S(1)}, u32[]{:S(2)}, u32[]{:S(2)}) collective-permute-start(bf16[128,1024]{1,0:T(8,128)(2,1)S(1)} %copy-done), channel_id=1, source_target_pairs={{0,2},{1,3},{2,0},{3,1},{4,6},{5,7},{6,4},{7,5},{8,10},{9,11},{10,... | collective-permute-start | bytes 786440 | tf_op jit(solution)/shard_map/ppermute | solution.py:389
  14.9 0.7 copy-start.5
  16.2 6.1 %collective-permute-start = (bf16[3,256,128]{2,1,0:T(8,128)(2,1)S(1)}, bf16[3,256,128]{2,1,0:T(8,128)(2,1)S(1)}, u32[]{:S(2)}, u32[]{:S(2)}) collective-permute-start(bf16[3,256,128]{2,1,0:T(8,128)(2,1)S(1)} %get-tuple-element.27), channel_id=1, source_target_pairs={{0,16},{16,0},{32,48},{48,32},{64,80},{80,64},{96,112},{112,96},{1... | collective-permute-start | bytes 589832 | tf_op jit(solution)/shard_map/ppermute | solution.py:386
  18.5 14.6 %collective-permute-start.1 = (bf16[128,1024]{1,0:T(8,128)(2,1)S(1)}, bf16[128,1024]{1,0:T(8,128)(2,1)S(1)}, u32[]{:S(2)}, u32[]{:S(2)}) collective-permute-start(bf16[128,1024]{1,0:T(8,128)(2,1)S(1)} %copy-done), channel_id=1, source_target_pairs={{0,1},{1,0},{2,3},{3,2},{4,5},{5,4},{6,7},{7,6},{8,9},{9,8},{10,11... | collective-permute-start | bytes 786440 | tf_op jit(solution)/shard_map/ppermute | solution.py:388
  23.7 10.4 %all-to-all-start.1 = ((bf16[4,128,256]{2,1,0:T(8,128)(2,1)}), bf16[4,128,256]{2,1,0:T(8,128)(2,1)S(1)}, u32[]{:S(2)}, u32[]{:S(2)}) async-start(bf16[4,128,256]{2,1,0:T(8,128)(2,1)} %get-tuple-element.29), calls=%async_computation.1 | async-start | bytes 524288 | tf_op jit(solution)/shard_map/all_to_all | solution.py:401
  29.4 9.4 %collective-permute-start.3 = (bf16[128,1024]{1,0:T(8,128)(2,1)S(1)}, bf16[128,1024]{1,0:T(8,128)(2,1)S(1)}, u32[]{:S(2)}, u32[]{:S(2)}) collective-permute-start(bf16[128,1024]{1,0:T(8,128)(2,1)S(1)} %collective-permute-done.2.w2_ref), channel_id=1, source_target_pairs={{0,1},{1,0},{2,3},{3,2},{4,5},{5,4},{6,7},{7,6},{8,9},{9,8},{10,11... | collective-permute-start | bytes 786440 | tf_op jit(solution)/shard_map/ppermute | solution.py:399
  54.4 3.4 %collective-permute-start.4 = (bf16[2,64,1024]{2,1,0:T(8,128)(2,1)S(1)}, bf16[2,64,1024]{2,1,0:T(8,128)(2,1)S(1)}, u32[]{:S(2)}, u32[]{:S(2)}) collective-permute-start(bf16[2,64,1024]{2,1,0:T(8,128)(2,1)S(1)} %get-tuple-element.42), channel_id=1, source_target_pairs={{0,16},{16,0},{32,48},{48,32},{64,80},{80,64},{96,112},{112,96},{1... | collective-permute-start | bytes 786440 | tf_op jit(solution)/shard_map/ppermute | solution.py:433

commit v11 on v9

--- a/solution.py
+++ b/solution.py
@@ -273,10 +273,15 @@
                     out_ref[4 * side + label, target : target + 16] = piece
 
 
-def project_kernel(normed_ref, w0_ref, w1_ref, w2_ref, w3_ref, keep_ref, send_ref):
+def lay_kernel(w1_ref, w3_ref, out_ref):
+    out_ref[0] = w1_ref[...]
+    out_ref[1] = w3_ref[...]
+
+
+def project_kernel(normed_ref, w0_ref, w2_ref, far_ref, keep_ref, send_ref):
     _, _, core = places()
     along = lax.axis_index("tp")
-    weights = [ref[...] for ref in (w0_ref, w1_ref, w2_ref, w3_ref)]
+    weights = [w0_ref[...], far_ref[0], w2_ref[...], far_ref[1]]
     for side in range(2):
         total = None
         for i, weight in enumerate(weights):
@@ -399,7 +404,6 @@
     w3 = lax.ppermute(w2, "tp", [(j, j ^ 1) for j in range(16)])
     columns = [[8 * y + i for y in range(4)] for i in range(8)]
     rows = lax.all_to_all(total, "ctx", 0, 0, axis_index_groups=columns)
-    rows, w1 = lax.optimization_barrier((rows, w1))
     normed = call(
         out_kernel,
         shape((8, 128, DV), BF),
@@ -418,16 +422,22 @@
     far = [[16 * at + token_of(g, m) for at in pair for g in range(4)]
            for pair in pairs for m in range(4)]
     both = ("ctx", "tp")
-    normed, w3 = lax.optimization_barrier((normed, w3))
     gathered = lax.all_to_all(normed, both, 0, 0, axis_index_groups=close)
+    far_rows = call(
+        lay_kernel,
+        shape((2, DV, half_width), BF),
+        w1,
+        w3,
+        flops=10**10,
+        name="lay_rows",
+    )
     part, other_part = call(
         project_kernel,
         (shape((2, 64, half_width), F32), shape((2, 64, half_width), BF)),
         gathered,
         w0,
-        w1,
         w2,
-        w3,
+        far_rows,
         name="project",
     )
     other_part = lax.ppermute(other_part, "ctx", across)

time: 89.2 us -> 85.3 us (0.956)
  blocking collectives: 41.7 us -> 30.1 us
  starting transfers between devices: 27.2 us -> 31.1 us
  waiting for transfers between devices: 9.19 us -> 12.1 us
    all_to_all x1 -> x0, blocking collectives: 12.3 us -> none  [local(): gathered = lax.all_to_all(normed, both, 0, 0, axis_index_groups=close)]
    all_to_all x0 -> x1, starting transfers between devices: none -> 3.41 us  [local(): gathered = lax.all_to_all(normed, both, 0, 0, axis_index_groups=close)]
    all_to_all x0 -> x1, waiting for transfers between devices: none -> 2.89 us  [local(): gathered = lax.all_to_all(normed, both, 0, 0, axis_index_groups=close)]
    ppermute x1, starting transfers between devices: 1.92 us -> 3.92 us  [local(): w3 = lax.ppermute(w2, 'tp', [(j, j ^ 1) for j in range(16)])]
    ppermute x1, starting transfers between devices: 3.83 us -> 1.91 us  [local(): w1 = lax.ppermute(w0, 'tp', [(j, j ^ 1) for j in range(16)])]
    all_to_all x1, waiting for transfers between devices: 0.01 us -> 1.52 us  [local(): parts = lax.all_to_all(maps, 'ctx', 0, 0, axis_index_groups=lines)]
    pallas_call x7 -> x8, Pallas kernels: 9.58 us -> 10.3 us  [call(): pl.pallas_call(kernel, out_shape=outs, in_specs=ins, out_specs=jax.tree.m...]
  transfers between devices with their start and end apart: 7 -> 8, of which waited for: 3 -> 5; matrix products, arithmetic and copies ran while one was open for 0% -> 0% of each run, Pallas kernels for 3% -> 4%
where the time goes in v11:
time: 85.3 us; the launch traced here: 84.5 us
  starting transfers between devices  31.1 us (36%)
  blocking collectives  30.1 us (35%)
  waiting for transfers between devices  12.1 us (14%)
  Pallas kernels  10.3 us (12%)
    all_to_all x1, blocking collectives, local(): shares = lax.all_to_all(partial, both, 0, 0, axis_index_groups=far)  30.1 us
    pallas_call x8, Pallas kernels, call(): pl.pallas_call(kernel, out_shape=outs, in_specs=ins, out_specs=jax.tree.m...  10.3 us
    all_to_all x1, starting transfers between devices, local(): rows = lax.all_to_all(total, 'ctx', 0, 0, axis_index_groups=columns)  8.08 us
    ppermute x1, waiting for transfers between devices, local(): w3 = lax.ppermute(w2, 'tp', [(j, j ^ 1) for j in range(16)])  6.06 us
    ppermute x1, starting transfers between devices, local(): w2 = lax.ppermute(w0, 'tp', [(j, j ^ 2) for j in range(16)])  5.17 us
    all_to_all x1, starting transfers between devices, local(): parts = lax.all_to_all(maps, 'ctx', 0, 0, axis_index_groups=lines)  4.45 us
    ppermute x1, starting transfers between devices, local(): w3 = lax.ppermute(w2, 'tp', [(j, j ^ 1) for j in range(16)])  3.92 us
    all_to_all x1, starting transfers between devices, local(): gathered = lax.all_to_all(normed, both, 0, 0, axis_index_groups=close)  3.41 us
  transfers between devices with their start and end apart: 8, of which 5 were waited for; matrix products, arithmetic and copies ran while one was open for 0% of the time, Pallas kernels for 4%

profile of v11, /device:TPU:24, one launch (start us, length us, event | category | flops | bytes accessed | tf_op | source)
XLA Modules:
  0.0 84.5 jit_solution(7427466081982296233)
XLA Ops:
  0.0 5.2 %shard_maps.1 = (bf16[8,128,256]{2,1,0:T(8,128)(2,1)}, f32[2,256,256]{2,1,0:T(8,128)}, bf16[128,1024]{1,0:T(8,128)(2,1)}) custom-call(bf16[256,128]{1,0:T(8,128)(2,1)} %k_ref.1, bf16[256,256]{1,0:T(8,128)(2,1)} %v_far.1, f32[2,256]{1,0:T(2,128)} %bitcast.6, f32[2,256]{1,0:T(2,128)} %bitcast.3, bf16[256,2048]{1,0:T(8,128)(2,1)} %weight_far.1), custom_call_target="tpu_custom_call" | custom-call | flops 1000000000 | bytes 1000 | tf_op jit(solution)/shard_map/shard_maps/pallas_call | solution.py:328
  5.2 0.0 copy-start
  5.2 0.0 copy-start.1
  5.2 0.0 copy-start.2
  5.2 0.0 copy-start.3
  5.2 0.0 copy-start.6
  5.2 4.5 %all-to-all-start = ((bf16[8,128,256]{2,1,0:T(8,128)(2,1)}), bf16[8,128,256]{2,1,0:T(8,128)(2,1)S(1)}, u32[]{:S(2)}, u32[]{:S(2)}) async-start(bf16[8,128,256]{2,1,0:T(8,128)(2,1)} %get-tuple-element.19), calls=%async_computation | async-start | bytes 1048576 | tf_op jit(solution)/shard_map/all_to_all | solution.py:377
  9.7 0.0 copy-done
  9.7 0.0 copy-start.4
  9.7 5.2 %collective-permute-start = (bf16[128,1024]{1,0:T(8,128)(2,1)S(1)}, bf16[128,1024]{1,0:T(8,128)(2,1)S(1)}, u32[]{:S(2)}, u32[]{:S(2)}) collective-permute-start(bf16[128,1024]{1,0:T(8,128)(2,1)S(1)} %copy-done), channel_id=1, source_target_pairs={{0,2},{1,3},{2,0},{3,1},{4,6},{5,7},{6,4},{7,5},{8,10},{9,11},{10,... | collective-permute-start | bytes 786440 | tf_op jit(solution)/shard_map/ppermute | solution.py:394
  14.9 0.0 copy-start.5
  14.9 0.0 copy-done.1
  14.9 0.0 copy-done.2
  14.9 0.0 copy-done.3
  14.9 0.0 copy-done.6
  14.9 0.0 copy-done.4
  14.9 0.6 copy-done.5
  15.5 0.7 read_parts.1
  16.3 2.2 %collective-permute-start.1 = (bf16[3,256,128]{2,1,0:T(8,128)(2,1)S(1)}, bf16[3,256,128]{2,1,0:T(8,128)(2,1)S(1)}, u32[]{:S(2)}, u32[]{:S(2)}) collective-permute-start(bf16[3,256,128]{2,1,0:T(8,128)(2,1)S(1)} %get-tuple-element.22), channel_id=1, source_target_pairs={{0,16},{16,0},{32,48},{48,32},{64,80},{80,64},{96,112},{112,96},{1... | collective-permute-start | bytes 589832 | tf_op jit(solution)/shard_map/ppermute | solution.py:391
  18.5 1.5 %all-to-all-done.parts_ref = bf16[8,128,256]{2,1,0:T(8,128)(2,1)S(1)} async-done(((bf16[8,128,256]{2,1,0:T(8,128)(2,1)}), bf16[8,128,256]{2,1,0:T(8,128)(2,1)S(1)}, u32[]{:S(2)}, u32[]{:S(2)}) %all-to-all-start) | async-done | bytes 524320 | tf_op jit(solution)/shard_map/all_to_all | solution.py:377
  20.0 1.3 %row_maps.1 = (bf16[4,128,256]{2,1,0:T(8,128)(2,1)}, f32[128,256]{1,0:T(8,128)S(1)}, bf16[128,256]{1,0:T(8,128)(2,1)S(1)}) custom-call(bf16[8,128,256]{2,1,0:T(8,128)(2,1)S(1)} %all-to-all-done.parts_ref), custom_call_target="tpu_custom_call" | custom-call | flops 1000 | bytes 1000 | tf_op jit(solution)/shard_map/row_maps/pallas_call | solution.py:328
  21.4 8.1 %all-to-all-start.1 = ((bf16[4,128,256]{2,1,0:T(8,128)(2,1)}), bf16[4,128,256]{2,1,0:T(8,128)(2,1)S(1)}, u32[]{:S(2)}, u32[]{:S(2)}) async-start(bf16[4,128,256]{2,1,0:T(8,128)(2,1)} %get-tuple-element.24), calls=%async_computation.1 | async-start | bytes 524288 | tf_op jit(solution)/shard_map/all_to_all | solution.py:406
  29.5 1.9 %collective-permute-start.2 = (bf16[128,1024]{1,0:T(8,128)(2,1)S(1)}, bf16[128,1024]{1,0:T(8,128)(2,1)S(1)}, u32[]{:S(2)}, u32[]{:S(2)}) collective-permute-start(bf16[128,1024]{1,0:T(8,128)(2,1)S(1)} %copy-done), channel_id=1, source_target_pairs={{0,1},{1,0},{2,3},{3,2},{4,5},{5,4},{6,7},{7,6},{8,9},{9,8},{10,11... | collective-permute-start | bytes 786440 | tf_op jit(solution)/shard_map/ppermute | solution.py:393
  31.4 0.0 collective-permute-done.w2_ref
  31.4 3.9 %collective-permute-start.3 = (bf16[128,1024]{1,0:T(8,128)(2,1)S(1)}, bf16[128,1024]{1,0:T(8,128)(2,1)S(1)}, u32[]{:S(2)}, u32[]{:S(2)}) collective-permute-start(bf16[128,1024]{1,0:T(8,128)(2,1)S(1)} %collective-permute-done.w2_ref), channel_id=1, source_target_pairs={{0,1},{1,0},{2,3},{3,2},{4,5},{5,4},{6,7},{7,6},{8,9},{9,8},{10,11... | collective-permute-start | bytes 786440 | tf_op jit(solution)/shard_map/ppermute | solution.py:404
  35.3 0.0 collective-permute-done.1.came_ref
  35.3 0.0 all-to-all-done.1.rows_ref
  35.3 1.7 %gated_norm.1 = bf16[8,128,128]{2,1,0:T(8,128)(2,1)} custom-call(bf16[4,128,256]{2,1,0:T(8,128)(2,1)S(1)} %all-to-all-done.1.rows_ref, f32[128,256]{1,0:T(8,128)S(1)} %get-tuple-element.27.ahead_ref, bf16[128,256]{1,0:T(8,128)(2,1)S(1)} %get-tuple-element.28.first_ref, f32[3,256,128]{2,1,0:T(8,128)S(1)} %get-tuple-element.29.keep_ref, ...), custom_call_target="tpu_custom_call" | custom-call | flops 1000000000 | bytes 1000 | tf_op jit(solution)/shard_map/gated_norm/pallas_call | solution.py:328
  37.0 3.4 %all-to-all-start.2 = ((bf16[8,128,128]{2,1,0:T(8,128)(2,1)}), bf16[8,128,128]{2,1,0:T(8,128)(2,1)S(1)}, u32[]{:S(2)}, u32[]{:S(2)}) async-start(bf16[8,128,128]{2,1,0:T(8,128)(2,1)} %gated_norm.1), calls=%async_computation.2 | async-start | bytes 524288 | tf_op jit(solution)/shard_map/all_to_all | solution.py:425
  40.4 0.2 collective-permute-done.2.w1_ref
  40.6 6.1 %collective-permute-done.3.w3_ref = bf16[128,1024]{1,0:T(8,128)(2,1)S(1)} collective-permute-done((bf16[128,1024]{1,0:T(8,128)(2,1)S(1)}, bf16[128,1024]{1,0:T(8,128)(2,1)S(1)}, u32[]{:S(2)}, u32[]{:S(2)}) %collective-permute-start.3) | collective-permute-done | bytes 262176 | tf_op jit(solution)/shard_map/ppermute | solution.py:404
  46.7 2.9 %all-to-all-done.2.normed_ref = bf16[8,128,128]{2,1,0:T(8,128)(2,1)S(1)} async-done(((bf16[8,128,128]{2,1,0:T(8,128)(2,1)}), bf16[8,128,128]{2,1,0:T(8,128)(2,1)S(1)}, u32[]{:S(2)}, u32[]{:S(2)}) %all-to-all-start.2) | async-done | bytes 262176 | tf_op jit(solution)/shard_map/all_to_all | solution.py:425
  49.6 0.7 project.1
  50.3 1.9 %collective-permute-start.4 = (bf16[2,64,1024]{2,1,0:T(8,128)(2,1)S(1)}, bf16[2,64,1024]{2,1,0:T(8,128)(2,1)S(1)}, u32[]{:S(2)}, u32[]{:S(2)}) collective-permute-start(bf16[2,64,1024]{2,1,0:T(8,128)(2,1)S(1)} %get-tuple-element.32), channel_id=1, source_target_pairs={{0,16},{16,0},{32,48},{48,32},{64,80},{80,64},{96,112},{112,96},{1... | collective-permute-start | bytes 786440 | tf_op jit(solution)/shard_map/ppermute | solution.py:443
  52.2 1.5 %collective-permute-done.4.came_ref = bf16[2,64,1024]{2,1,0:T(8,128)(2,1)S(1)} collective-permute-done((bf16[2,64,1024]{2,1,0:T(8,128)(2,1)S(1)}, bf16[2,64,1024]{2,1,0:T(8,128)(2,1)S(1)}, u32[]{:S(2)}, u32[]{:S(2)}) %collective-permute-start.4) | collective-permute-done | bytes 262176 | tf_op jit(solution)/shard_map/ppermute | solution.py:443
  53.8 30.1 %all_to_all.20.parts_ref = bf16[8,16,1024]{2,1,0:T(8,128)(2,1)S(1)} all-to-all(bf16[8,16,1024]{2,1,0:T(8,128)(2,1)S(1)} %join.1), channel_id=1, replica_groups={{0,4,11,15,32,36,43,47},{1,5,10,14,33,37,42,46},{2,6,9,13,34,38,41,45},..., dimensions={0} | all-to-all | bytes 524288 | tf_op jit(solution)/shard_map/all_to_all | solution.py:445
  83.8 0.7 sum_shares.1
  (2 shorter events, 0.1 us)
Async XLA Ops:
  5.2 4.5 %copy-start = (bf16[128,1024]{1,0:T(8,128)(2,1)S(1)}, bf16[128,1024]{1,0:T(8,128)(2,1)}, u32[]{:S(2)}) copy-start(bf16[128,1024]{1,0:T(8,128)(2,1)} %get-tuple-element.25.w0_ref) | copy-start | bytes 786436
  5.2 9.7 %copy-start.1 = (bf16[256,256]{1,0:T(8,128)(2,1)S(1)}, bf16[256,256]{1,0:T(8,128)(2,1)}, u32[]{:S(2)}) copy-start(bf16[256,256]{1,0:T(8,128)(2,1)} %gate_ref.1) | copy-start | bytes 393220
  5.2 9.7 %copy-start.2 = (bf16[256,128]{1,0:T(8,128)(2,1)S(1)}, bf16[256,128]{1,0:T(8,128)(2,1)}, u32[]{:S(2)}) copy-start(bf16[256,128]{1,0:T(8,128)(2,1)} %k_ref.1) | copy-start | bytes 196612
  5.2 9.7 %copy-start.3 = (bf16[256,128]{1,0:T(8,128)(2,1)S(1)}, bf16[256,128]{1,0:T(8,128)(2,1)}, u32[]{:S(2)}) copy-start(bf16[256,128]{1,0:T(8,128)(2,1)} %q_ref.1) | copy-start | bytes 196612
  5.2 9.7 %copy-start.6 = (f32[2,256,256]{2,1,0:T(8,128)S(1)}, f32[2,256,256]{2,1,0:T(8,128)}, u32[]{:S(2)}) copy-start(f32[2,256,256]{2,1,0:T(8,128)} %get-tuple-element.20.solved_ref) | copy-start | bytes 1572868
  5.2 14.8 %all-to-all-start = ((bf16[8,128,256]{2,1,0:T(8,128)(2,1)}), bf16[8,128,256]{2,1,0:T(8,128)(2,1)S(1)}, u32[]{:S(2)}, u32[]{:S(2)}) async-start(bf16[8,128,256]{2,1,0:T(8,128)(2,1)} %get-tuple-element.19), calls=%async_computation | async-start | bytes 1048576 | tf_op jit(solution)/shard_map/all_to_all | solution.py:377
  9.7 5.2 %copy-start.4 = (f32[256,2]{0,1:T(2,128)S(1)}, f32[256,2]{0,1:T(2,128)}, u32[]{:S(2)}) copy-start(f32[256,2]{0,1:T(2,128)} %param.13) | copy-start | bytes 6148
  9.7 21.7 %collective-permute-start = (bf16[128,1024]{1,0:T(8,128)(2,1)S(1)}, bf16[128,1024]{1,0:T(8,128)(2,1)S(1)}, u32[]{:S(2)}, u32[]{:S(2)}) collective-permute-start(bf16[128,1024]{1,0:T(8,128)(2,1)S(1)} %copy-done), channel_id=1, source_target_pairs={{0,2},{1,3},{2,0},{3,1},{4,6},{5,7},{6,4},{7,5},{8,10},{9,11},{10,... | collective-permute-start | bytes 786440 | tf_op jit(solution)/shard_map/ppermute | solution.py:394
  14.9 0.7 copy-start.5
  16.3 19.1 %collective-permute-start.1 = (bf16[3,256,128]{2,1,0:T(8,128)(2,1)S(1)}, bf16[3,256,128]{2,1,0:T(8,128)(2,1)S(1)}, u32[]{:S(2)}, u32[]{:S(2)}) collective-permute-start(bf16[3,256,128]{2,1,0:T(8,128)(2,1)S(1)} %get-tuple-element.22), channel_id=1, source_target_pairs={{0,16},{16,0},{32,48},{48,32},{64,80},{80,64},{96,112},{112,96},{1... | collective-permute-start | bytes 589832 | tf_op jit(solution)/shard_map/ppermute | solution.py:391
  21.4 14.0 %all-to-all-start.1 = ((bf16[4,128,256]{2,1,0:T(8,128)(2,1)}), bf16[4,128,256]{2,1,0:T(8,128)(2,1)S(1)}, u32[]{:S(2)}, u32[]{:S(2)}) async-start(bf16[4,128,256]{2,1,0:T(8,128)(2,1)} %get-tuple-element.24), calls=%async_computation.1 | async-start | bytes 524288 | tf_op jit(solution)/shard_map/all_to_all | solution.py:406
  29.5 11.1 %collective-permute-start.2 = (bf16[128,1024]{1,0:T(8,128)(2,1)S(1)}, bf16[128,1024]{1,0:T(8,128)(2,1)S(1)}, u32[]{:S(2)}, u32[]{:S(2)}) collective-permute-start(bf16[128,1024]{1,0:T(8,128)(2,1)S(1)} %copy-done), channel_id=1, source_target_pairs={{0,1},{1,0},{2,3},{3,2},{4,5},{5,4},{6,7},{7,6},{8,9},{9,8},{10,11... | collective-permute-start | bytes 786440 | tf_op jit(solution)/shard_map/ppermute | solution.py:393
  31.4 15.3 %collective-permute-start.3 = (bf16[128,1024]{1,0:T(8,128)(2,1)S(1)}, bf16[128,1024]{1,0:T(8,128)(2,1)S(1)}, u32[]{:S(2)}, u32[]{:S(2)}) collective-permute-start(bf16[128,1024]{1,0:T(8,128)(2,1)S(1)} %collective-permute-done.w2_ref), channel_id=1, source_target_pairs={{0,1},{1,0},{2,3},{3,2},{4,5},{5,4},{6,7},{7,6},{8,9},{9,8},{10,11... | collective-permute-start | bytes 786440 | tf_op jit(solution)/shard_map/ppermute | solution.py:404
  37.0 12.6 %all-to-all-start.2 = ((bf16[8,128,128]{2,1,0:T(8,128)(2,1)}), bf16[8,128,128]{2,1,0:T(8,128)(2,1)S(1)}, u32[]{:S(2)}, u32[]{:S(2)}) async-start(bf16[8,128,128]{2,1,0:T(8,128)(2,1)} %gated_norm.1), calls=%async_computation.2 | async-start | bytes 524288 | tf_op jit(solution)/shard_map/all_to_all | solution.py:425
  50.3 3.4 %collective-permute-start.4 = (bf16[2,64,1024]{2,1,0:T(8,128)(2,1)S(1)}, bf16[2,64,1024]{2,1,0:T(8,128)(2,1)S(1)}, u32[]{:S(2)}, u32[]{:S(2)}) collective-permute-start(bf16[2,64,1024]{2,1,0:T(8,128)(2,1)S(1)} %get-tuple-element.32), channel_id=1, source_target_pairs={{0,16},{16,0},{32,48},{48,32},{64,80},{80,64},{96,112},{112,96},{1... | collective-permute-start | bytes 786440 | tf_op jit(solution)/shard_map/ppermute | solution.py:443

commit v12 on v11

--- a/solution.py
+++ b/solution.py
@@ -273,9 +273,8 @@
                     out_ref[4 * side + label, target : target + 16] = piece
 
 
-def lay_kernel(w1_ref, w3_ref, out_ref):
-    out_ref[0] = w1_ref[...]
-    out_ref[1] = w3_ref[...]
+def lay_kernel(rows_ref, out_ref):
+    out_ref[...] = rows_ref[...]
 
 
 def project_kernel(normed_ref, w0_ref, w2_ref, far_ref, keep_ref, send_ref):
@@ -390,7 +389,6 @@
     across = [(i, i ^ 1) for i in range(32)]
     came = lax.ppermute(send, "ctx", across)
 
-    w1 = lax.ppermute(w0, "tp", [(j, j ^ 1) for j in range(16)])
     w2 = lax.ppermute(w0, "tp", [(j, j ^ 2) for j in range(16)])
 
     parts, keep, send = lax.optimization_barrier((parts, keep, send))
@@ -401,7 +399,7 @@
         name="row_maps",
     )
     w2, ahead = lax.optimization_barrier((w2, ahead))
-    w3 = lax.ppermute(w2, "tp", [(j, j ^ 1) for j in range(16)])
+    near13 = lax.ppermute(jnp.stack([w0, w2]), "tp", [(j, j ^ 1) for j in range(16)])
     columns = [[8 * y + i for y in range(4)] for i in range(8)]
     rows = lax.all_to_all(total, "ctx", 0, 0, axis_index_groups=columns)
     normed = call(
@@ -412,7 +410,7 @@
         first,
         keep,
         came,
-        flops=10**9,
+        flops=10*10**9,
         name="gated_norm",
     )
     pairs = [[8 * y + 4 * pair + 2 * side + core for side in range(2)]
@@ -426,9 +424,8 @@
     far_rows = call(
         lay_kernel,
         shape((2, DV, half_width), BF),
-        w1,
-        w3,
-        flops=10**10,
+        near13,
+        flops=10*10**9,
         name="lay_rows",
     )
     part, other_part = call(

time: 85.3 us -> 83.8 us (0.982)
  waiting for transfers between devices: 12.1 us -> 16.9 us
  starting transfers between devices: 31.1 us -> 27.2 us
  blocking collectives: 30.1 us -> 27.1 us
    ppermute x2 -> x1, starting transfers between devices: 5.83 us -> 1.92 us  [local(): lax.ppermute(jnp.stack([w0, w2]), 'tp', [(j, j ^ 1) for j in range(16)])]
    all_to_all x1, blocking collectives: 30.1 us -> 27.1 us  [local(): shares = lax.all_to_all(partial, both, 0, 0, axis_index_groups=far)]
    all_to_all x1, waiting for transfers between devices: 0.01 us -> 2.69 us  [local(): rows = lax.all_to_all(total, 'ctx', 0, 0, axis_index_groups=columns)]
    ppermute x2 -> x1, waiting for transfers between devices: 6.21 us -> 7.46 us  [local(): lax.ppermute(jnp.stack([w0, w2]), 'tp', [(j, j ^ 1) for j in range(16)])]
    all_to_all x1, waiting for transfers between devices: 2.89 us -> 3.75 us  [local(): gathered = lax.all_to_all(normed, both, 0, 0, axis_index_groups=close)]
  transfers between devices with their start and end apart: 8 -> 7, of which waited for: 5 -> 5; matrix products, arithmetic and copies ran while one was open for 0% -> 0% of each run, Pallas kernels for 4% -> 5%
where the time goes in v12:
time: 83.8 us; the launch traced here: 82.5 us
  starting transfers between devices  27.2 us (32%)
  blocking collectives  27.1 us (32%)
  waiting for transfers between devices  16.9 us (20%)
  Pallas kernels  10.3 us (12%)
    all_to_all x1, blocking collectives, local(): shares = lax.all_to_all(partial, both, 0, 0, axis_index_groups=far)  27.1 us
    pallas_call x8, Pallas kernels, call(): pl.pallas_call(kernel, out_shape=outs, in_specs=ins, out_specs=jax.tree.m...  10.3 us
    all_to_all x1, starting transfers between devices, local(): rows = lax.all_to_all(total, 'ctx', 0, 0, axis_index_groups=columns)  8.08 us
    ppermute x1, waiting for transfers between devices, local(): lax.ppermute(jnp.stack([w0, w2]), 'tp', [(j, j ^ 1) for j in range(16)])  7.46 us
    ppermute x1, starting transfers between devices, local(): w2 = lax.ppermute(w0, 'tp', [(j, j ^ 2) for j in range(16)])  5.17 us
    all_to_all x1, starting transfers between devices, local(): parts = lax.all_to_all(maps, 'ctx', 0, 0, axis_index_groups=lines)  4.45 us
    all_to_all x1, waiting for transfers between devices, local(): gathered = lax.all_to_all(normed, both, 0, 0, axis_index_groups=close)  3.75 us
    all_to_all x1, starting transfers between devices, local(): gathered = lax.all_to_all(normed, both, 0, 0, axis_index_groups=close)  3.41 us
  transfers between devices with their start and end apart: 7, of which 5 were waited for; matrix products, arithmetic and copies ran while one was open for 0% of the time, Pallas kernels for 5%

profile of v12, /device:TPU:24, one launch (start us, length us, event | category | flops | bytes accessed | tf_op | source)
XLA Modules:
  0.0 82.5 jit_solution(15888733305622557261)
XLA Ops:
  0.0 5.2 %shard_maps.1 = (bf16[8,128,256]{2,1,0:T(8,128)(2,1)}, f32[2,256,256]{2,1,0:T(8,128)}, bf16[128,1024]{1,0:T(8,128)(2,1)}) custom-call(bf16[256,128]{1,0:T(8,128)(2,1)} %k_ref.1, bf16[256,256]{1,0:T(8,128)(2,1)} %v_far.1, f32[2,256]{1,0:T(2,128)} %bitcast.10, f32[2,256]{1,0:T(2,128)} %bitcast.7, bf16[256,2048]{1,0:T(8,128)(2,1)} %weight_far.1), custom_call_target="tpu_custom_call" | custom-call | flops 1000000000 | bytes 1000 | tf_op jit(solution)/shard_map/shard_maps/pallas_call | solution.py:327
  5.2 0.0 copy-start
  5.2 0.0 copy-start.1
  5.2 0.0 copy-start.2
  5.2 0.0 copy-start.3
  5.2 0.0 copy-start.6
  5.2 4.5 %all-to-all-start = ((bf16[8,128,256]{2,1,0:T(8,128)(2,1)}), bf16[8,128,256]{2,1,0:T(8,128)(2,1)S(1)}, u32[]{:S(2)}, u32[]{:S(2)}) async-start(bf16[8,128,256]{2,1,0:T(8,128)(2,1)} %get-tuple-element.19), calls=%async_computation | async-start | bytes 1048576 | tf_op jit(solution)/shard_map/all_to_all | solution.py:376
  9.7 0.0 copy-done
  9.7 0.0 copy-start.4
  9.7 5.2 %collective-permute-start = (bf16[128,1024]{1,0:T(8,128)(2,1)S(1)}, bf16[128,1024]{1,0:T(8,128)(2,1)S(1)}, u32[]{:S(2)}, u32[]{:S(2)}) collective-permute-start(bf16[128,1024]{1,0:T(8,128)(2,1)S(1)} %copy-done), channel_id=1, source_target_pairs={{0,2},{1,3},{2,0},{3,1},{4,6},{5,7},{6,4},{7,5},{8,10},{9,11},{10,... | collective-permute-start | bytes 786440 | tf_op jit(solution)/shard_map/ppermute | solution.py:392
  14.9 0.0 copy-start.5
  14.9 0.0 copy-done.1
  14.9 0.0 copy-done.2
  14.9 0.0 copy-done.3
  14.9 0.0 copy-done.6
  14.9 0.0 copy-done.4
  14.9 0.6 copy-done.5
  15.5 0.7 read_parts.1
  16.2 2.2 %collective-permute-start.1 = (bf16[3,256,128]{2,1,0:T(8,128)(2,1)S(1)}, bf16[3,256,128]{2,1,0:T(8,128)(2,1)S(1)}, u32[]{:S(2)}, u32[]{:S(2)}) collective-permute-start(bf16[3,256,128]{2,1,0:T(8,128)(2,1)S(1)} %get-tuple-element.22), channel_id=1, source_target_pairs={{0,16},{16,0},{32,48},{48,32},{64,80},{80,64},{96,112},{112,96},{1... | collective-permute-start | bytes 589832 | tf_op jit(solution)/shard_map/ppermute | solution.py:390
  18.5 1.5 %all-to-all-done.parts_ref = bf16[8,128,256]{2,1,0:T(8,128)(2,1)S(1)} async-done(((bf16[8,128,256]{2,1,0:T(8,128)(2,1)}), bf16[8,128,256]{2,1,0:T(8,128)(2,1)S(1)}, u32[]{:S(2)}, u32[]{:S(2)}) %all-to-all-start) | async-done | bytes 524320 | tf_op jit(solution)/shard_map/all_to_all | solution.py:376
  20.0 1.3 %row_maps.1 = (bf16[4,128,256]{2,1,0:T(8,128)(2,1)}, f32[128,256]{1,0:T(8,128)S(1)}, bf16[128,256]{1,0:T(8,128)(2,1)S(1)}) custom-call(bf16[8,128,256]{2,1,0:T(8,128)(2,1)S(1)} %all-to-all-done.parts_ref), custom_call_target="tpu_custom_call" | custom-call | flops 1000 | bytes 1000 | tf_op jit(solution)/shard_map/row_maps/pallas_call | solution.py:327
  21.4 8.1 %all-to-all-start.1 = ((bf16[4,128,256]{2,1,0:T(8,128)(2,1)}), bf16[4,128,256]{2,1,0:T(8,128)(2,1)S(1)}, u32[]{:S(2)}, u32[]{:S(2)}) async-start(bf16[4,128,256]{2,1,0:T(8,128)(2,1)} %get-tuple-element.24), calls=%async_computation.1 | async-start | bytes 524288 | tf_op jit(solution)/shard_map/all_to_all | solution.py:404
  29.4 0.0 collective-permute-done.w2_ref
  29.5 0.1 pad_maximum_fusion
  29.5 1.9 %collective-permute-start.2 = (bf16[2,128,1024]{2,1,0:T(8,128)(2,1)S(1)}, bf16[2,128,1024]{2,1,0:T(8,128)(2,1)S(1)}, u32[]{:S(2)}, u32[]{:S(2)}) collective-permute-start(bf16[2,128,1024]{2,1,0:T(8,128)(2,1)S(1)} %pad_maximum_fusion), channel_id=1, source_target_pairs={{0,1},{1,0},{2,3},{3,2},{4,5},{5,4},{6,7},{7,6},{8,9},{9,8},{10,11... | collective-permute-start | bytes 1572872 | tf_op jit(solution)/shard_map/ppermute | solution.py:402
  31.4 0.0 collective-permute-done.1.came_ref
  31.4 2.7 %all-to-all-done.1.rows_ref = bf16[4,128,256]{2,1,0:T(8,128)(2,1)S(1)} async-done(((bf16[4,128,256]{2,1,0:T(8,128)(2,1)}), bf16[4,128,256]{2,1,0:T(8,128)(2,1)S(1)}, u32[]{:S(2)}, u32[]{:S(2)}) %all-to-all-start.1) | async-done | bytes 262176 | tf_op jit(solution)/shard_map/all_to_all | solution.py:404
  34.1 1.7 %gated_norm.1 = bf16[8,128,128]{2,1,0:T(8,128)(2,1)} custom-call(bf16[4,128,256]{2,1,0:T(8,128)(2,1)S(1)} %all-to-all-done.1.rows_ref, f32[128,256]{1,0:T(8,128)S(1)} %get-tuple-element.27.ahead_ref, bf16[128,256]{1,0:T(8,128)(2,1)S(1)} %get-tuple-element.28.first_ref, f32[3,256,128]{2,1,0:T(8,128)S(1)} %get-tuple-element.29.keep_ref, ...), custom_call_target="tpu_custom_call" | custom-call | flops 10000000000 | bytes 1000 | tf_op jit(solution)/shard_map/gated_norm/pallas_call | solution.py:327
  35.8 3.4 %all-to-all-start.2 = ((bf16[8,128,128]{2,1,0:T(8,128)(2,1)}), bf16[8,128,128]{2,1,0:T(8,128)(2,1)S(1)}, u32[]{:S(2)}, u32[]{:S(2)}) async-start(bf16[8,128,128]{2,1,0:T(8,128)(2,1)} %gated_norm.1), calls=%async_computation.2 | async-start | bytes 524288 | tf_op jit(solution)/shard_map/all_to_all | solution.py:423
  39.2 7.5 %collective-permute-done.2.rows_ref = bf16[2,128,1024]{2,1,0:T(8,128)(2,1)S(1)} collective-permute-done((bf16[2,128,1024]{2,1,0:T(8,128)(2,1)S(1)}, bf16[2,128,1024]{2,1,0:T(8,128)(2,1)S(1)}, u32[]{:S(2)}, u32[]{:S(2)}) %collective-permute-start.2) | collective-permute-done | bytes 524320 | tf_op jit(solution)/shard_map/ppermute | solution.py:402
  46.7 3.8 %all-to-all-done.2.normed_ref = bf16[8,128,128]{2,1,0:T(8,128)(2,1)S(1)} async-done(((bf16[8,128,128]{2,1,0:T(8,128)(2,1)}), bf16[8,128,128]{2,1,0:T(8,128)(2,1)S(1)}, u32[]{:S(2)}, u32[]{:S(2)}) %all-to-all-start.2) | async-done | bytes 262176 | tf_op jit(solution)/shard_map/all_to_all | solution.py:423
  50.5 0.7 project.1
  51.2 1.9 %collective-permute-start.3 = (bf16[2,64,1024]{2,1,0:T(8,128)(2,1)S(1)}, bf16[2,64,1024]{2,1,0:T(8,128)(2,1)S(1)}, u32[]{:S(2)}, u32[]{:S(2)}) collective-permute-start(bf16[2,64,1024]{2,1,0:T(8,128)(2,1)S(1)} %get-tuple-element.32), channel_id=1, source_target_pairs={{0,16},{16,0},{32,48},{48,32},{64,80},{80,64},{96,112},{112,96},{1... | collective-permute-start | bytes 786440 | tf_op jit(solution)/shard_map/ppermute | solution.py:440
  53.1 1.5 %collective-permute-done.3.came_ref = bf16[2,64,1024]{2,1,0:T(8,128)(2,1)S(1)} collective-permute-done((bf16[2,64,1024]{2,1,0:T(8,128)(2,1)S(1)}, bf16[2,64,1024]{2,1,0:T(8,128)(2,1)S(1)}, u32[]{:S(2)}, u32[]{:S(2)}) %collective-permute-start.3) | collective-permute-done | bytes 262176 | tf_op jit(solution)/shard_map/ppermute | solution.py:440
  54.7 27.1 %all_to_all.20.parts_ref = bf16[8,16,1024]{2,1,0:T(8,128)(2,1)S(1)} all-to-all(bf16[8,16,1024]{2,1,0:T(8,128)(2,1)S(1)} %join.1), channel_id=1, replica_groups={{0,4,11,15,32,36,43,47},{1,5,10,14,33,37,42,46},{2,6,9,13,34,38,41,45},..., dimensions={0} | all-to-all | bytes 524288 | tf_op jit(solution)/shard_map/all_to_all | solution.py:442
  81.8 0.7 sum_shares.1
  (2 shorter events, 0.1 us)
Async XLA Ops:
  5.2 4.5 %copy-start = (bf16[128,1024]{1,0:T(8,128)(2,1)S(1)}, bf16[128,1024]{1,0:T(8,128)(2,1)}, u32[]{:S(2)}) copy-start(bf16[128,1024]{1,0:T(8,128)(2,1)} %get-tuple-element.25.w0_ref) | copy-start | bytes 786436
  5.2 9.7 %copy-start.1 = (bf16[256,256]{1,0:T(8,128)(2,1)S(1)}, bf16[256,256]{1,0:T(8,128)(2,1)}, u32[]{:S(2)}) copy-start(bf16[256,256]{1,0:T(8,128)(2,1)} %gate_ref.1) | copy-start | bytes 393220
  5.2 9.7 %copy-start.2 = (bf16[256,128]{1,0:T(8,128)(2,1)S(1)}, bf16[256,128]{1,0:T(8,128)(2,1)}, u32[]{:S(2)}) copy-start(bf16[256,128]{1,0:T(8,128)(2,1)} %k_ref.1) | copy-start | bytes 196612
  5.2 9.7 %copy-start.3 = (bf16[256,128]{1,0:T(8,128)(2,1)S(1)}, bf16[256,128]{1,0:T(8,128)(2,1)}, u32[]{:S(2)}) copy-start(bf16[256,128]{1,0:T(8,128)(2,1)} %q_ref.1) | copy-start | bytes 196612
  5.2 9.7 %copy-start.6 = (f32[2,256,256]{2,1,0:T(8,128)S(1)}, f32[2,256,256]{2,1,0:T(8,128)}, u32[]{:S(2)}) copy-start(f32[2,256,256]{2,1,0:T(8,128)} %get-tuple-element.20.solved_ref) | copy-start | bytes 1572868
  5.2 14.8 %all-to-all-start = ((bf16[8,128,256]{2,1,0:T(8,128)(2,1)}), bf16[8,128,256]{2,1,0:T(8,128)(2,1)S(1)}, u32[]{:S(2)}, u32[]{:S(2)}) async-start(bf16[8,128,256]{2,1,0:T(8,128)(2,1)} %get-tuple-element.19), calls=%async_computation | async-start | bytes 1048576 | tf_op jit(solution)/shard_map/all_to_all | solution.py:376
  9.7 5.2 %copy-start.4 = (f32[256,2]{0,1:T(2,128)S(1)}, f32[256,2]{0,1:T(2,128)}, u32[]{:S(2)}) copy-start(f32[256,2]{0,1:T(2,128)} %param.13) | copy-start | bytes 6148
  9.7 19.8 %collective-permute-start = (bf16[128,1024]{1,0:T(8,128)(2,1)S(1)}, bf16[128,1024]{1,0:T(8,128)(2,1)S(1)}, u32[]{:S(2)}, u32[]{:S(2)}) collective-permute-start(bf16[128,1024]{1,0:T(8,128)(2,1)S(1)} %copy-done), channel_id=1, source_target_pairs={{0,2},{1,3},{2,0},{3,1},{4,6},{5,7},{6,4},{7,5},{8,10},{9,11},{10,... | collective-permute-start | bytes 786440 | tf_op jit(solution)/shard_map/ppermute | solution.py:392
  14.9 0.7 copy-start.5
  16.2 15.2 %collective-permute-start.1 = (bf16[3,256,128]{2,1,0:T(8,128)(2,1)S(1)}, bf16[3,256,128]{2,1,0:T(8,128)(2,1)S(1)}, u32[]{:S(2)}, u32[]{:S(2)}) collective-permute-start(bf16[3,256,128]{2,1,0:T(8,128)(2,1)S(1)} %get-tuple-element.22), channel_id=1, source_target_pairs={{0,16},{16,0},{32,48},{48,32},{64,80},{80,64},{96,112},{112,96},{1... | collective-permute-start | bytes 589832 | tf_op jit(solution)/shard_map/ppermute | solution.py:390
  21.4 12.8 %all-to-all-start.1 = ((bf16[4,128,256]{2,1,0:T(8,128)(2,1)}), bf16[4,128,256]{2,1,0:T(8,128)(2,1)S(1)}, u32[]{:S(2)}, u32[]{:S(2)}) async-start(bf16[4,128,256]{2,1,0:T(8,128)(2,1)} %get-tuple-element.24), calls=%async_computation.1 | async-start | bytes 524288 | tf_op jit(solution)/shard_map/all_to_all | solution.py:404
  29.5 17.2 %collective-permute-start.2 = (bf16[2,128,1024]{2,1,0:T(8,128)(2,1)S(1)}, bf16[2,128,1024]{2,1,0:T(8,128)(2,1)S(1)}, u32[]{:S(2)}, u32[]{:S(2)}) collective-permute-start(bf16[2,128,1024]{2,1,0:T(8,128)(2,1)S(1)} %pad_maximum_fusion), channel_id=1, source_target_pairs={{0,1},{1,0},{2,3},{3,2},{4,5},{5,4},{6,7},{7,6},{8,9},{9,8},{10,11... | collective-permute-start | bytes 1572872 | tf_op jit(solution)/shard_map/ppermute | solution.py:402
  35.8 14.7 %all-to-all-start.2 = ((bf16[8,128,128]{2,1,0:T(8,128)(2,1)}), bf16[8,128,128]{2,1,0:T(8,128)(2,1)S(1)}, u32[]{:S(2)}, u32[]{:S(2)}) async-start(bf16[8,128,128]{2,1,0:T(8,128)(2,1)} %gated_norm.1), calls=%async_computation.2 | async-start | bytes 524288 | tf_op jit(solution)/shard_map/all_to_all | solution.py:423
  51.2 3.4 %collective-permute-start.3 = (bf16[2,64,1024]{2,1,0:T(8,128)(2,1)S(1)}, bf16[2,64,1024]{2,1,0:T(8,128)(2,1)S(1)}, u32[]{:S(2)}, u32[]{:S(2)}) collective-permute-start(bf16[2,64,1024]{2,1,0:T(8,128)(2,1)S(1)} %get-tuple-element.32), channel_id=1, source_target_pairs={{0,16},{16,0},{32,48},{48,32},{64,80},{80,64},{96,112},{112,96},{1... | collective-permute-start | bytes 786440 | tf_op jit(solution)/shard_map/ppermute | solution.py:440

commit v13 on v12

--- a/solution.py
+++ b/solution.py
@@ -299,15 +299,6 @@
             out_ref[4 * side + group] = total[16 * group : 16 * (group + 1)]
 
 
-def sum_kernel(parts_ref, out_ref):
-    columns = parts_ref.shape[2]
-    for side in range(2):
-        total = parts_ref[4 * side].astype(F32)
-        for group in range(1, 4):
-            total = total + parts_ref[4 * side + group].astype(F32)
-        out_ref[:, side * columns : (side + 1) * columns] = total.astype(BF)
-
-
 def places():
     at = lax.axis_index("ctx")
     return at // 8, (at // 2) % 4, at % 2
@@ -440,7 +431,10 @@
     other_part = lax.ppermute(other_part, "ctx", across)
     partial = call(join_kernel, shape((8, 16, half_width), BF), part, other_part, name="join")
     shares = lax.all_to_all(partial, both, 0, 0, axis_index_groups=far)
-    return call(sum_kernel, shape((16, width), BF), shares, name="sum_shares")
+    sides = [
+        sum(shares[4 * side + g].astype(F32) for g in range(4)).astype(BF) for side in range(2)
+    ]
+    return jnp.concatenate(sides, axis=1)
 
 
 def solution(mesh):

time: 83.8 us -> 83.9 us (level)
    pallas_call x8 -> x7, Pallas kernels: 10.3 us -> 9.66 us  [call(): pl.pallas_call(kernel, out_shape=outs, in_specs=ins, out_specs=jax.tree.m...]
where the time goes in v13:
time: 83.9 us; the launch traced here: 82.5 us
  starting transfers between devices  27.2 us (32%)
  blocking collectives  27.1 us (32%)
  waiting for transfers between devices  16.9 us (20%)
  Pallas kernels  9.66 us (12%)
    all_to_all x1, blocking collectives, local(): shares = lax.all_to_all(partial, both, 0, 0, axis_index_groups=far)  27.1 us
    pallas_call x7, Pallas kernels, call(): pl.pallas_call(kernel, out_shape=outs, in_specs=ins, out_specs=jax.tree.m...  9.66 us
    all_to_all x1, starting transfers between devices, local(): rows = lax.all_to_all(total, 'ctx', 0, 0, axis_index_groups=columns)  8.08 us
    ppermute x1, waiting for transfers between devices, local(): lax.ppermute(jnp.stack([w0, w2]), 'tp', [(j, j ^ 1) for j in range(16)])  7.47 us
    ppermute x1, starting transfers between devices, local(): w2 = lax.ppermute(w0, 'tp', [(j, j ^ 2) for j in range(16)])  5.17 us
    all_to_all x1, starting transfers between devices, local(): parts = lax.all_to_all(maps, 'ctx', 0, 0, axis_index_groups=lines)  4.45 us
    all_to_all x1, waiting for transfers between devices, local(): gathered = lax.all_to_all(normed, both, 0, 0, axis_index_groups=close)  3.76 us
    all_to_all x1, starting transfers between devices, local(): gathered = lax.all_to_all(normed, both, 0, 0, axis_index_groups=close)  3.41 us
  transfers between devices with their start and end apart: 7, of which 5 were waited for; matrix products, arithmetic and copies ran while one was open for 0% of the time, Pallas kernels for 5%

profile of v13, /device:TPU:24, one launch (start us, length us, event | category | flops | bytes accessed | tf_op | source)
XLA Modules:
  0.0 82.5 jit_solution(13005397364059189299)
XLA Ops:
  0.0 5.2 %shard_maps.1 = (bf16[8,128,256]{2,1,0:T(8,128)(2,1)}, f32[2,256,256]{2,1,0:T(8,128)}, bf16[128,1024]{1,0:T(8,128)(2,1)}) custom-call(bf16[256,128]{1,0:T(8,128)(2,1)} %k_ref.1, bf16[256,256]{1,0:T(8,128)(2,1)} %v_far.1, f32[2,256]{1,0:T(2,128)} %bitcast.14, f32[2,256]{1,0:T(2,128)} %bitcast.11, bf16[256,2048]{1,0:T(8,128)(2,1)} %weight_far.1), custom_call_target="tpu_custom_call" | custom-call | flops 1000000000 | bytes 1000 | tf_op jit(solution)/shard_map/shard_maps/pallas_call | solution.py:318
  5.2 0.0 copy-start
  5.2 0.0 copy-start.1
  5.2 0.0 copy-start.2
  5.2 0.0 copy-start.3
  5.2 0.0 copy-start.6
  5.2 4.5 %all-to-all-start = ((bf16[8,128,256]{2,1,0:T(8,128)(2,1)}), bf16[8,128,256]{2,1,0:T(8,128)(2,1)S(1)}, u32[]{:S(2)}, u32[]{:S(2)}) async-start(bf16[8,128,256]{2,1,0:T(8,128)(2,1)} %get-tuple-element.19), calls=%async_computation | async-start | bytes 1048576 | tf_op jit(solution)/shard_map/all_to_all | solution.py:367
  9.7 0.0 copy-done
  9.7 0.0 copy-start.4
  9.7 5.2 %collective-permute-start = (bf16[128,1024]{1,0:T(8,128)(2,1)S(1)}, bf16[128,1024]{1,0:T(8,128)(2,1)S(1)}, u32[]{:S(2)}, u32[]{:S(2)}) collective-permute-start(bf16[128,1024]{1,0:T(8,128)(2,1)S(1)} %copy-done), channel_id=1, source_target_pairs={{0,2},{1,3},{2,0},{3,1},{4,6},{5,7},{6,4},{7,5},{8,10},{9,11},{10,... | collective-permute-start | bytes 786440 | tf_op jit(solution)/shard_map/ppermute | solution.py:383
  14.9 0.0 copy-start.5
  14.9 0.0 copy-done.1
  14.9 0.0 copy-done.2
  14.9 0.0 copy-done.3
  14.9 0.0 copy-done.6
  14.9 0.0 copy-done.4
  14.9 0.6 copy-done.5
  15.5 0.7 read_parts.1
  16.3 2.2 %collective-permute-start.1 = (bf16[3,256,128]{2,1,0:T(8,128)(2,1)S(1)}, bf16[3,256,128]{2,1,0:T(8,128)(2,1)S(1)}, u32[]{:S(2)}, u32[]{:S(2)}) collective-permute-start(bf16[3,256,128]{2,1,0:T(8,128)(2,1)S(1)} %get-tuple-element.22), channel_id=1, source_target_pairs={{0,16},{16,0},{32,48},{48,32},{64,80},{80,64},{96,112},{112,96},{1... | collective-permute-start | bytes 589832 | tf_op jit(solution)/shard_map/ppermute | solution.py:381
  18.5 1.5 %all-to-all-done.parts_ref = bf16[8,128,256]{2,1,0:T(8,128)(2,1)S(1)} async-done(((bf16[8,128,256]{2,1,0:T(8,128)(2,1)}), bf16[8,128,256]{2,1,0:T(8,128)(2,1)S(1)}, u32[]{:S(2)}, u32[]{:S(2)}) %all-to-all-start) | async-done | bytes 524320 | tf_op jit(solution)/shard_map/all_to_all | solution.py:367
  20.0 1.3 %row_maps.1 = (bf16[4,128,256]{2,1,0:T(8,128)(2,1)}, f32[128,256]{1,0:T(8,128)S(1)}, bf16[128,256]{1,0:T(8,128)(2,1)S(1)}) custom-call(bf16[8,128,256]{2,1,0:T(8,128)(2,1)S(1)} %all-to-all-done.parts_ref), custom_call_target="tpu_custom_call" | custom-call | flops 1000 | bytes 1000 | tf_op jit(solution)/shard_map/row_maps/pallas_call | solution.py:318
  21.4 8.1 %all-to-all-start.1 = ((bf16[4,128,256]{2,1,0:T(8,128)(2,1)}), bf16[4,128,256]{2,1,0:T(8,128)(2,1)S(1)}, u32[]{:S(2)}, u32[]{:S(2)}) async-start(bf16[4,128,256]{2,1,0:T(8,128)(2,1)} %get-tuple-element.24), calls=%async_computation.1 | async-start | bytes 524288 | tf_op jit(solution)/shard_map/all_to_all | solution.py:395
  29.5 0.0 collective-permute-done.w2_ref
  29.5 0.1 pad_maximum_fusion
  29.5 1.9 %collective-permute-start.2 = (bf16[2,128,1024]{2,1,0:T(8,128)(2,1)S(1)}, bf16[2,128,1024]{2,1,0:T(8,128)(2,1)S(1)}, u32[]{:S(2)}, u32[]{:S(2)}) collective-permute-start(bf16[2,128,1024]{2,1,0:T(8,128)(2,1)S(1)} %pad_maximum_fusion), channel_id=1, source_target_pairs={{0,1},{1,0},{2,3},{3,2},{4,5},{5,4},{6,7},{7,6},{8,9},{9,8},{10,11... | collective-permute-start | bytes 1572872 | tf_op jit(solution)/shard_map/ppermute | solution.py:393
  31.4 0.0 collective-permute-done.1.came_ref
  31.5 2.7 %all-to-all-done.1.rows_ref = bf16[4,128,256]{2,1,0:T(8,128)(2,1)S(1)} async-done(((bf16[4,128,256]{2,1,0:T(8,128)(2,1)}), bf16[4,128,256]{2,1,0:T(8,128)(2,1)S(1)}, u32[]{:S(2)}, u32[]{:S(2)}) %all-to-all-start.1) | async-done | bytes 262176 | tf_op jit(solution)/shard_map/all_to_all | solution.py:395
  34.1 1.7 %gated_norm.1 = bf16[8,128,128]{2,1,0:T(8,128)(2,1)} custom-call(bf16[4,128,256]{2,1,0:T(8,128)(2,1)S(1)} %all-to-all-done.1.rows_ref, f32[128,256]{1,0:T(8,128)S(1)} %get-tuple-element.27.ahead_ref, bf16[128,256]{1,0:T(8,128)(2,1)S(1)} %get-tuple-element.28.first_ref, f32[3,256,128]{2,1,0:T(8,128)S(1)} %get-tuple-element.29.keep_ref, ...), custom_call_target="tpu_custom_call" | custom-call | flops 10000000000 | bytes 1000 | tf_op jit(solution)/shard_map/gated_norm/pallas_call | solution.py:318
  35.8 3.4 %all-to-all-start.2 = ((bf16[8,128,128]{2,1,0:T(8,128)(2,1)}), bf16[8,128,128]{2,1,0:T(8,128)(2,1)S(1)}, u32[]{:S(2)}, u32[]{:S(2)}) async-start(bf16[8,128,128]{2,1,0:T(8,128)(2,1)} %gated_norm.1), calls=%async_computation.2 | async-start | bytes 524288 | tf_op jit(solution)/shard_map/all_to_all | solution.py:414
  39.2 7.5 %collective-permute-done.2.rows_ref = bf16[2,128,1024]{2,1,0:T(8,128)(2,1)S(1)} collective-permute-done((bf16[2,128,1024]{2,1,0:T(8,128)(2,1)S(1)}, bf16[2,128,1024]{2,1,0:T(8,128)(2,1)S(1)}, u32[]{:S(2)}, u32[]{:S(2)}) %collective-permute-start.2) | collective-permute-done | bytes 524320 | tf_op jit(solution)/shard_map/ppermute | solution.py:393
  46.7 3.8 %all-to-all-done.2.normed_ref = bf16[8,128,128]{2,1,0:T(8,128)(2,1)S(1)} async-done(((bf16[8,128,128]{2,1,0:T(8,128)(2,1)}), bf16[8,128,128]{2,1,0:T(8,128)(2,1)S(1)}, u32[]{:S(2)}, u32[]{:S(2)}) %all-to-all-start.2) | async-done | bytes 262176 | tf_op jit(solution)/shard_map/all_to_all | solution.py:414
  50.5 0.7 project.1
  51.2 1.9 %collective-permute-start.3 = (bf16[2,64,1024]{2,1,0:T(8,128)(2,1)S(1)}, bf16[2,64,1024]{2,1,0:T(8,128)(2,1)S(1)}, u32[]{:S(2)}, u32[]{:S(2)}) collective-permute-start(bf16[2,64,1024]{2,1,0:T(8,128)(2,1)S(1)} %get-tuple-element.32), channel_id=1, source_target_pairs={{0,16},{16,0},{32,48},{48,32},{64,80},{80,64},{96,112},{112,96},{1... | collective-permute-start | bytes 786440 | tf_op jit(solution)/shard_map/ppermute | solution.py:431
  53.1 1.5 %collective-permute-done.3.came_ref = bf16[2,64,1024]{2,1,0:T(8,128)(2,1)S(1)} collective-permute-done((bf16[2,64,1024]{2,1,0:T(8,128)(2,1)S(1)}, bf16[2,64,1024]{2,1,0:T(8,128)(2,1)S(1)}, u32[]{:S(2)}, u32[]{:S(2)}) %collective-permute-start.3) | collective-permute-done | bytes 262176 | tf_op jit(solution)/shard_map/ppermute | solution.py:431
  54.7 27.1 %all_to_all.20 = bf16[8,16,1024]{2,1,0:T(8,128)(2,1)S(1)} all-to-all(bf16[8,16,1024]{2,1,0:T(8,128)(2,1)S(1)} %join.1), channel_id=1, replica_groups={{0,4,11,15,32,36,43,47},{1,5,10,14,33,37,42,46},{2,6,9,13,34,38,41,45},..., dimensions={0} | all-to-all | bytes 524288 | tf_op jit(solution)/shard_map/all_to_all | solution.py:433
  81.8 0.6 pad_maximum_fusion.1
  (3 shorter events, 0.1 us)
Async XLA Ops:
  5.2 4.5 %copy-start = (bf16[128,1024]{1,0:T(8,128)(2,1)S(1)}, bf16[128,1024]{1,0:T(8,128)(2,1)}, u32[]{:S(2)}) copy-start(bf16[128,1024]{1,0:T(8,128)(2,1)} %get-tuple-element.25.w0_ref) | copy-start | bytes 786436
  5.2 9.7 %copy-start.1 = (bf16[256,256]{1,0:T(8,128)(2,1)S(1)}, bf16[256,256]{1,0:T(8,128)(2,1)}, u32[]{:S(2)}) copy-start(bf16[256,256]{1,0:T(8,128)(2,1)} %gate_ref.1) | copy-start | bytes 393220
  5.2 9.7 %copy-start.2 = (bf16[256,128]{1,0:T(8,128)(2,1)S(1)}, bf16[256,128]{1,0:T(8,128)(2,1)}, u32[]{:S(2)}) copy-start(bf16[256,128]{1,0:T(8,128)(2,1)} %k_ref.1) | copy-start | bytes 196612
  5.2 9.7 %copy-start.3 = (bf16[256,128]{1,0:T(8,128)(2,1)S(1)}, bf16[256,128]{1,0:T(8,128)(2,1)}, u32[]{:S(2)}) copy-start(bf16[256,128]{1,0:T(8,128)(2,1)} %q_ref.1) | copy-start | bytes 196612
  5.2 9.7 %copy-start.6 = (f32[2,256,256]{2,1,0:T(8,128)S(1)}, f32[2,256,256]{2,1,0:T(8,128)}, u32[]{:S(2)}) copy-start(f32[2,256,256]{2,1,0:T(8,128)} %get-tuple-element.20.solved_ref) | copy-start | bytes 1572868
  5.2 14.8 %all-to-all-start = ((bf16[8,128,256]{2,1,0:T(8,128)(2,1)}), bf16[8,128,256]{2,1,0:T(8,128)(2,1)S(1)}, u32[]{:S(2)}, u32[]{:S(2)}) async-start(bf16[8,128,256]{2,1,0:T(8,128)(2,1)} %get-tuple-element.19), calls=%async_computation | async-start | bytes 1048576 | tf_op jit(solution)/shard_map/all_to_all | solution.py:367
  9.7 5.2 %copy-start.4 = (f32[256,2]{0,1:T(2,128)S(1)}, f32[256,2]{0,1:T(2,128)}, u32[]{:S(2)}) copy-start(f32[256,2]{0,1:T(2,128)} %param.13) | copy-start | bytes 6148
  9.7 19.8 %collective-permute-start = (bf16[128,1024]{1,0:T(8,128)(2,1)S(1)}, bf16[128,1024]{1,0:T(8,128)(2,1)S(1)}, u32[]{:S(2)}, u32[]{:S(2)}) collective-permute-start(bf16[128,1024]{1,0:T(8,128)(2,1)S(1)} %copy-done), channel_id=1, source_target_pairs={{0,2},{1,3},{2,0},{3,1},{4,6},{5,7},{6,4},{7,5},{8,10},{9,11},{10,... | collective-permute-start | bytes 786440 | tf_op jit(solution)/shard_map/ppermute | solution.py:383
  14.9 0.7 copy-start.5
  16.3 15.2 %collective-permute-start.1 = (bf16[3,256,128]{2,1,0:T(8,128)(2,1)S(1)}, bf16[3,256,128]{2,1,0:T(8,128)(2,1)S(1)}, u32[]{:S(2)}, u32[]{:S(2)}) collective-permute-start(bf16[3,256,128]{2,1,0:T(8,128)(2,1)S(1)} %get-tuple-element.22), channel_id=1, source_target_pairs={{0,16},{16,0},{32,48},{48,32},{64,80},{80,64},{96,112},{112,96},{1... | collective-permute-start | bytes 589832 | tf_op jit(solution)/shard_map/ppermute | solution.py:381
  21.4 12.8 %all-to-all-start.1 = ((bf16[4,128,256]{2,1,0:T(8,128)(2,1)}), bf16[4,128,256]{2,1,0:T(8,128)(2,1)S(1)}, u32[]{:S(2)}, u32[]{:S(2)}) async-start(bf16[4,128,256]{2,1,0:T(8,128)(2,1)} %get-tuple-element.24), calls=%async_computation.1 | async-start | bytes 524288 | tf_op jit(solution)/shard_map/all_to_all | solution.py:395
  29.5 17.2 %collective-permute-start.2 = (bf16[2,128,1024]{2,1,0:T(8,128)(2,1)S(1)}, bf16[2,128,1024]{2,1,0:T(8,128)(2,1)S(1)}, u32[]{:S(2)}, u32[]{:S(2)}) collective-permute-start(bf16[2,128,1024]{2,1,0:T(8,128)(2,1)S(1)} %pad_maximum_fusion), channel_id=1, source_target_pairs={{0,1},{1,0},{2,3},{3,2},{4,5},{5,4},{6,7},{7,6},{8,9},{9,8},{10,11... | collective-permute-start | bytes 1572872 | tf_op jit(solution)/shard_map/ppermute | solution.py:393
  35.8 14.7 %all-to-all-start.2 = ((bf16[8,128,128]{2,1,0:T(8,128)(2,1)}), bf16[8,128,128]{2,1,0:T(8,128)(2,1)S(1)}, u32[]{:S(2)}, u32[]{:S(2)}) async-start(bf16[8,128,128]{2,1,0:T(8,128)(2,1)} %gated_norm.1), calls=%async_computation.2 | async-start | bytes 524288 | tf_op jit(solution)/shard_map/all_to_all | solution.py:414
  51.2 3.4 %collective-permute-start.3 = (bf16[2,64,1024]{2,1,0:T(8,128)(2,1)S(1)}, bf16[2,64,1024]{2,1,0:T(8,128)(2,1)S(1)}, u32[]{:S(2)}, u32[]{:S(2)}) collective-permute-start(bf16[2,64,1024]{2,1,0:T(8,128)(2,1)S(1)} %get-tuple-element.32), channel_id=1, source_target_pairs={{0,16},{16,0},{32,48},{48,32},{64,80},{80,64},{96,112},{112,96},{1... | collective-permute-start | bytes 786440 | tf_op jit(solution)/shard_map/ppermute | solution.py:431

commit v14 on v12

--- a/solution.py
+++ b/solution.py
@@ -384,6 +384,7 @@
         norm_gain.reshape(1, DV),
         solved,
         flops=10**9,
+        room=60,
         name="read_parts",
     )
     across = [(i, i ^ 1) for i in range(32)]

time: 83.8 us -> 83.8 us (level)
  Pallas kernels: 10.3 us -> 12.4 us
  waiting for transfers between devices: 16.9 us -> 15.5 us
    pallas_call x8, Pallas kernels: 10.3 us -> 12.4 us  [call(): pl.pallas_call(kernel, out_shape=outs, in_specs=ins, out_specs=jax.tree.m...]
    all_to_all x1, waiting for transfers between devices: 1.52 us -> 0.25 us  [local(): parts = lax.all_to_all(maps, 'ctx', 0, 0, axis_index_groups=lines)]
  transfers between devices with their start and end apart: 7 -> 7, of which waited for: 5 -> 5; matrix products, arithmetic and copies ran while one was open for 0% -> 0% of each run, Pallas kernels for 5% -> 7%
where the time goes in v14:
time: 83.8 us; the launch traced here: 82.3 us
  starting transfers between devices  27.2 us (32%)
  blocking collectives  27 us (32%)
  waiting for transfers between devices  15.5 us (18%)
  Pallas kernels  12.4 us (15%)
    all_to_all x1, blocking collectives, local(): shares = lax.all_to_all(partial, both, 0, 0, axis_index_groups=far)  27 us
    pallas_call x8, Pallas kernels, call(): pl.pallas_call(kernel, out_shape=outs, in_specs=ins, out_specs=jax.tree.m...  12.4 us
    all_to_all x1, starting transfers between devices, local(): rows = lax.all_to_all(total, 'ctx', 0, 0, axis_index_groups=columns)  8.08 us
    ppermute x1, waiting for transfers between devices, local(): lax.ppermute(jnp.stack([w0, w2]), 'tp', [(j, j ^ 1) for j in range(16)])  7.59 us
    ppermute x1, starting transfers between devices, local(): w2 = lax.ppermute(w0, 'tp', [(j, j ^ 2) for j in range(16)])  5.17 us
    all_to_all x1, starting transfers between devices, local(): parts = lax.all_to_all(maps, 'ctx', 0, 0, axis_index_groups=lines)  4.45 us
    all_to_all x1, waiting for transfers between devices, local(): gathered = lax.all_to_all(normed, both, 0, 0, axis_index_groups=close)  3.62 us
    all_to_all x1, starting transfers between devices, local(): gathered = lax.all_to_all(normed, both, 0, 0, axis_index_groups=close)  3.41 us
  transfers between devices with their start and end apart: 7, of which 5 were waited for; matrix products, arithmetic and copies ran while one was open for 0% of the time, Pallas kernels for 7%

profile of v14, /device:TPU:24, one launch (start us, length us, event | category | flops | bytes accessed | tf_op | source)
XLA Modules:
  0.0 82.3 jit_solution(1636053375329293598)
XLA Ops:
  0.0 5.1 %shard_maps.1 = (bf16[8,128,256]{2,1,0:T(8,128)(2,1)}, f32[2,256,256]{2,1,0:T(8,128)}, bf16[128,1024]{1,0:T(8,128)(2,1)}) custom-call(bf16[256,128]{1,0:T(8,128)(2,1)} %k_ref.1, bf16[256,256]{1,0:T(8,128)(2,1)} %v_far.1, f32[2,256]{1,0:T(2,128)} %bitcast.7, f32[2,256]{1,0:T(2,128)} %bitcast.8, bf16[256,2048]{1,0:T(8,128)(2,1)} %weight_far.1), custom_call_target="tpu_custom_call" | custom-call | flops 1000000000 | bytes 1000 | tf_op jit(solution)/shard_map/shard_maps/pallas_call | solution.py:327
  5.2 0.0 copy-start
  5.2 4.5 %all-to-all-start = ((bf16[8,128,256]{2,1,0:T(8,128)(2,1)}), bf16[8,128,256]{2,1,0:T(8,128)(2,1)S(1)}, u32[]{:S(2)}, u32[]{:S(2)}) async-start(bf16[8,128,256]{2,1,0:T(8,128)(2,1)} %get-tuple-element.19), calls=%async_computation | async-start | bytes 1048576 | tf_op jit(solution)/shard_map/all_to_all | solution.py:376
  9.6 0.0 copy-done
  9.6 5.2 %collective-permute-start = (bf16[128,1024]{1,0:T(8,128)(2,1)S(1)}, bf16[128,1024]{1,0:T(8,128)(2,1)S(1)}, u32[]{:S(2)}, u32[]{:S(2)}) collective-permute-start(bf16[128,1024]{1,0:T(8,128)(2,1)S(1)} %copy-done), channel_id=1, source_target_pairs={{0,2},{1,3},{2,0},{3,1},{4,6},{5,7},{6,4},{7,5},{8,10},{9,11},{10,... | collective-permute-start | bytes 786440 | tf_op jit(solution)/shard_map/ppermute | solution.py:393
  14.8 2.8 %read_parts.1 = (f32[3,256,128]{2,1,0:T(8,128)}, bf16[3,256,128]{2,1,0:T(8,128)(2,1)}) custom-call(bf16[256,128]{1,0:T(8,128)(2,1)} %q_ref.1, bf16[256,128]{1,0:T(8,128)(2,1)} %k_ref.1, f32[2,256]{1,0:T(2,128)} %bitcast.9, bf16[256,256]{1,0:T(8,128)(2,1)} %gate_ref.1, f32[1,128]{1,0:T(1,128)} %bitcast.10, f32[2,256,256]{2,1,0:T(8,128)} %get-tuple-element.20.solved_ref), custom_call_target="tpu_custom_call" | custom-call | flops 1000000000 | bytes 1000 | tf_op jit(solution)/shard_map/read_parts/pallas_call | solution.py:327
  17.6 2.1 %collective-permute-start.1 = (bf16[3,256,128]{2,1,0:T(8,128)(2,1)}, bf16[3,256,128]{2,1,0:T(8,128)(2,1)S(1)}, u32[]{:S(2)}, u32[]{:S(2)}) collective-permute-start(bf16[3,256,128]{2,1,0:T(8,128)(2,1)} %get-tuple-element.22), channel_id=1, source_target_pairs={{0,16},{16,0},{32,48},{48,32},{64,80},{80,64},{96,112},{112,96},{1... | collective-permute-start | bytes 589832 | tf_op jit(solution)/shard_map/ppermute | solution.py:391
  19.7 0.2 all-to-all-done.parts_ref
  20.0 1.3 %row_maps.1 = (bf16[4,128,256]{2,1,0:T(8,128)(2,1)}, f32[128,256]{1,0:T(8,128)S(1)}, bf16[128,256]{1,0:T(8,128)(2,1)S(1)}) custom-call(bf16[8,128,256]{2,1,0:T(8,128)(2,1)S(1)} %all-to-all-done.parts_ref), custom_call_target="tpu_custom_call" | custom-call | flops 1000 | bytes 1000 | tf_op jit(solution)/shard_map/row_maps/pallas_call | solution.py:327
  21.3 8.1 %all-to-all-start.1 = ((bf16[4,128,256]{2,1,0:T(8,128)(2,1)}), bf16[4,128,256]{2,1,0:T(8,128)(2,1)S(1)}, u32[]{:S(2)}, u32[]{:S(2)}) async-start(bf16[4,128,256]{2,1,0:T(8,128)(2,1)} %get-tuple-element.24), calls=%async_computation.1 | async-start | bytes 524288 | tf_op jit(solution)/shard_map/all_to_all | solution.py:405
  29.4 0.0 collective-permute-done.w2_ref
  29.4 0.0 copy-start.1
  29.4 0.1 pad_maximum_fusion
  29.5 2.1 %collective-permute-start.2 = (bf16[2,128,1024]{2,1,0:T(8,128)(2,1)S(1)}, bf16[2,128,1024]{2,1,0:T(8,128)(2,1)S(1)}, u32[]{:S(2)}, u32[]{:S(2)}) collective-permute-start(bf16[2,128,1024]{2,1,0:T(8,128)(2,1)S(1)} %pad_maximum_fusion), channel_id=1, source_target_pairs={{0,1},{1,0},{2,3},{3,2},{4,5},{5,4},{6,7},{7,6},{8,9},{9,8},{10,11... | collective-permute-start | bytes 1572872 | tf_op jit(solution)/shard_map/ppermute | solution.py:403
  31.5 0.0 collective-permute-done.1.came_ref
  31.5 2.6 %all-to-all-done.1.rows_ref = bf16[4,128,256]{2,1,0:T(8,128)(2,1)S(1)} async-done(((bf16[4,128,256]{2,1,0:T(8,128)(2,1)}), bf16[4,128,256]{2,1,0:T(8,128)(2,1)S(1)}, u32[]{:S(2)}, u32[]{:S(2)}) %all-to-all-start.1) | async-done | bytes 262176 | tf_op jit(solution)/shard_map/all_to_all | solution.py:405
  34.1 0.0 copy-done.1
  34.1 1.7 %gated_norm.1 = bf16[8,128,128]{2,1,0:T(8,128)(2,1)} custom-call(bf16[4,128,256]{2,1,0:T(8,128)(2,1)S(1)} %all-to-all-done.1.rows_ref, f32[128,256]{1,0:T(8,128)S(1)} %get-tuple-element.27.ahead_ref, bf16[128,256]{1,0:T(8,128)(2,1)S(1)} %get-tuple-element.28.first_ref, f32[3,256,128]{2,1,0:T(8,128)S(1)} %copy-done.1, ...), custom_call_target="tpu_custom_call" | custom-call | flops 10000000000 | bytes 1000 | tf_op jit(solution)/shard_map/gated_norm/pallas_call | solution.py:327
  35.8 3.4 %all-to-all-start.2 = ((bf16[8,128,128]{2,1,0:T(8,128)(2,1)}), bf16[8,128,128]{2,1,0:T(8,128)(2,1)S(1)}, u32[]{:S(2)}, u32[]{:S(2)}) async-start(bf16[8,128,128]{2,1,0:T(8,128)(2,1)} %gated_norm.1), calls=%async_computation.2 | async-start | bytes 524288 | tf_op jit(solution)/shard_map/all_to_all | solution.py:424
  39.2 7.6 %collective-permute-done.2.rows_ref = bf16[2,128,1024]{2,1,0:T(8,128)(2,1)S(1)} collective-permute-done((bf16[2,128,1024]{2,1,0:T(8,128)(2,1)S(1)}, bf16[2,128,1024]{2,1,0:T(8,128)(2,1)S(1)}, u32[]{:S(2)}, u32[]{:S(2)}) %collective-permute-start.2) | collective-permute-done | bytes 524320 | tf_op jit(solution)/shard_map/ppermute | solution.py:403
  46.8 3.6 %all-to-all-done.2.normed_ref = bf16[8,128,128]{2,1,0:T(8,128)(2,1)S(1)} async-done(((bf16[8,128,128]{2,1,0:T(8,128)(2,1)}), bf16[8,128,128]{2,1,0:T(8,128)(2,1)S(1)}, u32[]{:S(2)}, u32[]{:S(2)}) %all-to-all-start.2) | async-done | bytes 262176 | tf_op jit(solution)/shard_map/all_to_all | solution.py:424
  50.4 0.7 project.1
  51.1 1.9 %collective-permute-start.3 = (bf16[2,64,1024]{2,1,0:T(8,128)(2,1)S(1)}, bf16[2,64,1024]{2,1,0:T(8,128)(2,1)S(1)}, u32[]{:S(2)}, u32[]{:S(2)}) collective-permute-start(bf16[2,64,1024]{2,1,0:T(8,128)(2,1)S(1)} %get-tuple-element.32), channel_id=1, source_target_pairs={{0,16},{16,0},{32,48},{48,32},{64,80},{80,64},{96,112},{112,96},{1... | collective-permute-start | bytes 786440 | tf_op jit(solution)/shard_map/ppermute | solution.py:441
  53.1 1.5 %collective-permute-done.3.came_ref = bf16[2,64,1024]{2,1,0:T(8,128)(2,1)S(1)} collective-permute-done((bf16[2,64,1024]{2,1,0:T(8,128)(2,1)S(1)}, bf16[2,64,1024]{2,1,0:T(8,128)(2,1)S(1)}, u32[]{:S(2)}, u32[]{:S(2)}) %collective-permute-start.3) | collective-permute-done | bytes 262176 | tf_op jit(solution)/shard_map/ppermute | solution.py:441
  54.6 27.0 %all_to_all.20.parts_ref = bf16[8,16,1024]{2,1,0:T(8,128)(2,1)S(1)} all-to-all(bf16[8,16,1024]{2,1,0:T(8,128)(2,1)S(1)} %join.1), channel_id=1, replica_groups={{0,4,11,15,32,36,43,47},{1,5,10,14,33,37,42,46},{2,6,9,13,34,38,41,45},..., dimensions={0} | all-to-all | bytes 524288 | tf_op jit(solution)/shard_map/all_to_all | solution.py:443
  81.6 0.7 sum_shares.1
  (2 shorter events, 0.1 us)
Async XLA Ops:
  5.2 4.5 %copy-start = (bf16[128,1024]{1,0:T(8,128)(2,1)S(1)}, bf16[128,1024]{1,0:T(8,128)(2,1)}, u32[]{:S(2)}) copy-start(bf16[128,1024]{1,0:T(8,128)(2,1)} %get-tuple-element.25.w0_ref) | copy-start | bytes 786436
  5.2 14.8 %all-to-all-start = ((bf16[8,128,256]{2,1,0:T(8,128)(2,1)}), bf16[8,128,256]{2,1,0:T(8,128)(2,1)S(1)}, u32[]{:S(2)}, u32[]{:S(2)}) async-start(bf16[8,128,256]{2,1,0:T(8,128)(2,1)} %get-tuple-element.19), calls=%async_computation | async-start | bytes 1048576 | tf_op jit(solution)/shard_map/all_to_all | solution.py:376
  9.6 19.8 %collective-permute-start = (bf16[128,1024]{1,0:T(8,128)(2,1)S(1)}, bf16[128,1024]{1,0:T(8,128)(2,1)S(1)}, u32[]{:S(2)}, u32[]{:S(2)}) collective-permute-start(bf16[128,1024]{1,0:T(8,128)(2,1)S(1)} %copy-done), channel_id=1, source_target_pairs={{0,2},{1,3},{2,0},{3,1},{4,6},{5,7},{6,4},{7,5},{8,10},{9,11},{10,... | collective-permute-start | bytes 786440 | tf_op jit(solution)/shard_map/ppermute | solution.py:393
  17.6 13.9 %collective-permute-start.1 = (bf16[3,256,128]{2,1,0:T(8,128)(2,1)}, bf16[3,256,128]{2,1,0:T(8,128)(2,1)S(1)}, u32[]{:S(2)}, u32[]{:S(2)}) collective-permute-start(bf16[3,256,128]{2,1,0:T(8,128)(2,1)} %get-tuple-element.22), channel_id=1, source_target_pairs={{0,16},{16,0},{32,48},{48,32},{64,80},{80,64},{96,112},{112,96},{1... | collective-permute-start | bytes 589832 | tf_op jit(solution)/shard_map/ppermute | solution.py:391
  21.3 12.8 %all-to-all-start.1 = ((bf16[4,128,256]{2,1,0:T(8,128)(2,1)}), bf16[4,128,256]{2,1,0:T(8,128)(2,1)S(1)}, u32[]{:S(2)}, u32[]{:S(2)}) async-start(bf16[4,128,256]{2,1,0:T(8,128)(2,1)} %get-tuple-element.24), calls=%async_computation.1 | async-start | bytes 524288 | tf_op jit(solution)/shard_map/all_to_all | solution.py:405
  29.4 4.7 %copy-start.1 = (f32[3,256,128]{2,1,0:T(8,128)S(1)}, f32[3,256,128]{2,1,0:T(8,128)}, u32[]{:S(2)}) copy-start(f32[3,256,128]{2,1,0:T(8,128)} %get-tuple-element.29.keep_ref) | copy-start | bytes 1179652
  29.5 17.3 %collective-permute-start.2 = (bf16[2,128,1024]{2,1,0:T(8,128)(2,1)S(1)}, bf16[2,128,1024]{2,1,0:T(8,128)(2,1)S(1)}, u32[]{:S(2)}, u32[]{:S(2)}) collective-permute-start(bf16[2,128,1024]{2,1,0:T(8,128)(2,1)S(1)} %pad_maximum_fusion), channel_id=1, source_target_pairs={{0,1},{1,0},{2,3},{3,2},{4,5},{5,4},{6,7},{7,6},{8,9},{9,8},{10,11... | collective-permute-start | bytes 1572872 | tf_op jit(solution)/shard_map/ppermute | solution.py:403
  35.8 14.7 %all-to-all-start.2 = ((bf16[8,128,128]{2,1,0:T(8,128)(2,1)}), bf16[8,128,128]{2,1,0:T(8,128)(2,1)S(1)}, u32[]{:S(2)}, u32[]{:S(2)}) async-start(bf16[8,128,128]{2,1,0:T(8,128)(2,1)} %gated_norm.1), calls=%async_computation.2 | async-start | bytes 524288 | tf_op jit(solution)/shard_map/all_to_all | solution.py:424
  51.1 3.4 %collective-permute-start.3 = (bf16[2,64,1024]{2,1,0:T(8,128)(2,1)S(1)}, bf16[2,64,1024]{2,1,0:T(8,128)(2,1)S(1)}, u32[]{:S(2)}, u32[]{:S(2)}) collective-permute-start(bf16[2,64,1024]{2,1,0:T(8,128)(2,1)S(1)} %get-tuple-element.32), channel_id=1, source_target_pairs={{0,16},{16,0},{32,48},{48,32},{64,80},{80,64},{96,112},{112,96},{1... | collective-permute-start | bytes 786440 | tf_op jit(solution)/shard_map/ppermute | solution.py:441
